TPU v7x, 512 devices: a whole 4x8x8 slice. The times are simulated.
512 devices in a mesh: dp: 64 (over z, y), group: 8 (over x, core).
Axes of the slice: x: 4, y: 8, z: 8, core: 2. Of those that a mesh axis runs over, the one named last changes fastest.
Arguments:
- caption_tower_final_vectors: bfloat16 [2, 32768, 2048], P(None, ('dp', 'group')), may hold values from -6 to 6
- precomputed_picture_vectors: bfloat16 [16384, 1408], P('dp'), may hold values from -6 to 6
- pair_holder_rank: int32 [2, 32768, 1], P(None, ('dp', 'group')), may hold values from 0 to 63; in each aligned block of 64 rows (0 to 63, 64 to 127, ..., all dimensions but the last counted through in order) at most 2 rows name the same one
- pair_entry_position: int32 [2, 32768], P(None, ('dp', 'group')), may hold values from 0 to 255
- pair_targets: int32 [2, 32768], P(None, ('dp', 'group')), may hold values from 0 to 255
- picture_embedding_weights: bfloat16 [1408, 1024], P('dp'), may hold values from -0.15625 to 0.15625
- caption_embedding_weights: bfloat16 [2048, 1024], P('dp'), may hold values from -0.125 to 0.125
- score_stretch_learned: float32 [1], replicated, may hold values from 4 to 12
- sigmoid_offset_term: float32 [1], replicated, may hold values from -6 to -2
Outputs:
- text_grad: bfloat16 [2, 32768, 2048], P(None, ('dp', 'group'))
Inputs may be any that keep to these rules, and one draw needn't show every extreme that they name: `pair_holder_rank`: among the 64 pairs of one device in one microbatch, at most 2 name the same owner, a bound that some block reaches.
All inputs are finite; a program needn't handle non-finite values.
Results may differ from a plain program's by a relative error of at most 0.007.
Values may be sent and summed in bfloat16 or wider, within the bound.
No kernel may reach another device: no remote copies, remote signals or barrier semaphores. Data moves between devices by JAX's collectives and lax.ppermute only.
A program may use at most 64 MiB of HBM per device.

v0:
```python
import jax
import jax.numpy as jnp
from jax import lax
from jax.sharding import PartitionSpec as P

epsilon = 1e-06
loss_scale = 256.0


def unit_rows(values):
    inverse = lax.rsqrt(jnp.sum(values * values, axis=-1, keepdims=True) + epsilon)
    return (values * inverse, inverse)


def local(
    caption_tower_final_vectors,
    precomputed_picture_vectors,
    pair_holder_rank,
    pair_entry_position,
    pair_targets,
    picture_embedding_weights,
    caption_embedding_weights,
    score_stretch_learned,
    sigmoid_offset_term,
):
    image_full, text_full = (
        lax.all_gather(picture_embedding_weights, "dp", axis=0, tiled=True),
        lax.all_gather(caption_embedding_weights, "dp", axis=0, tiled=True),
    )
    owners_count = lax.axis_size("dp")
    pair_count = caption_tower_final_vectors.shape[1]
    capacity = max(2, 2 * pair_count // owners_count)
    reciprocal_warmth_gain = score_stretch_learned[0]
    additive_displacement = sigmoid_offset_term[0]
    results = []
    for step_index in range(caption_tower_final_vectors.shape[0]):
        owners_now = pair_holder_rank[step_index, :, 0]
        one_hot = (
            owners_now[:, None] == jnp.arange(owners_count, dtype=jnp.int32)[None, :]
        ).astype(jnp.int32)
        earlier = jnp.cumsum(one_hot, axis=0) - one_hot
        position = jnp.sum(earlier * one_hot, axis=1)
        slot_index = owners_now * capacity + position
        requests = (
            jnp.zeros((owners_count * capacity,), jnp.int32)
            .at[slot_index]
            .set(pair_entry_position[step_index])
        )
        requests = requests.reshape(owners_count, capacity)
        served = precomputed_picture_vectors[
            lax.all_to_all(requests, "dp", split_axis=0, concat_axis=0, tiled=True)
        ]
        fetched = lax.all_to_all(served, "dp", split_axis=0, concat_axis=0, tiled=True)
        picked = fetched.reshape(owners_count * capacity, fetched.shape[2])[slot_index]
        image_emb = unit_rows(jnp.dot(picked, image_full, preferred_element_type=jnp.float32))[
            0
        ].astype(jnp.bfloat16)
        text_raw = jnp.dot(
            caption_tower_final_vectors[step_index], text_full, preferred_element_type=jnp.float32
        )
        text_unit, inverse = unit_rows(text_raw)
        sentence_encodings_halfwidth = text_unit.astype(jnp.bfloat16)
        own_labels = pair_targets[step_index]
        visual_frozen_encodings = lax.all_gather(image_emb, "group", axis=0, tiled=True)
        piece_labels = lax.all_gather(own_labels, "group", axis=0, tiled=True)
        pairwise_agreement_scores = (
            reciprocal_warmth_gain
            * lax.dot_general(
                sentence_encodings_halfwidth,
                visual_frozen_encodings,
                (((1,), (1,)), ((), ())),
                preferred_element_type=jnp.float32,
            )
            + additive_displacement
        )
        matched = (own_labels[:, None] == piece_labels[None, :]).astype(jnp.float32)
        language_learned_parameters = (
            loss_scale * (jax.nn.sigmoid(pairwise_agreement_scores) - matched)
        ).astype(jnp.bfloat16)
        descent_direction_vectors = reciprocal_warmth_gain * jnp.dot(
            language_learned_parameters, visual_frozen_encodings, preferred_element_type=jnp.float32
        )
        grad_raw = (
            inverse
            * (
                descent_direction_vectors
                - text_unit * jnp.sum(text_unit * descent_direction_vectors, axis=-1, keepdims=True)
            )
        ).astype(jnp.bfloat16)
        text_grad = lax.dot_general(
            grad_raw, text_full, (((1,), (1,)), ((), ())), preferred_element_type=jnp.float32
        )
        results.append(text_grad.astype(jnp.bfloat16))
    return jnp.stack(results)


def solution(mesh):
    return jax.shard_map(
        local,
        mesh=mesh,
        in_specs=(
            P(None, ("dp", "group"), None),
            P("dp", None),
            P(None, ("dp", "group"), None),
            P(None, ("dp", "group")),
            P(None, ("dp", "group")),
            P("dp", None),
            P("dp", None),
            P(),
            P(),
        ),
        out_specs=P(None, ("dp", "group"), None),
        check_vma=False,
    )
```

profile of v0, /device:TPU:1, one launch (start us, length us, event | category | flops | bytes accessed | tf_op | source)
XLA Modules:
  0.0 267.5 jit_solution(7256324407501851118)
XLA Ops:
  6.5 0.0 copy-start
  6.5 0.0 all-gather.14.cloned.1.call-start
  6.5 0.7 all-gather.14.cloned.1.call-update
  7.3 0.0 all-gather.8.cloned.1.call-start
  7.3 0.7 all-gather.8.cloned.1.call-update
  8.0 0.7 slice_bitcast_fusion.5
  8.7 0.1 fusion.49
  8.8 0.1 reduce_window_sum.17
  8.9 0.1 fusion.48
  8.9 0.1 reduce_window_sum.18
  9.0 0.2 select_reduce_fusion
  9.2 0.8 slice_bitcast_fusion.3
  10.0 0.7 fusion.50
  10.7 0.8 scatter_custom_fusion
  11.4 0.1 all_to_all.22
  11.6 27.8 %all_to_all.34 = s32[64,1,2]{2,1,0:T(1,128)S(1)} all-to-all(s32[64,1,2]{2,1,0:T(1,128)S(1)} %bitcast.76), channel_id=1, replica_groups=mesh['dp'=64,'group'=8] {'dp'}, dimensions={0} | all-to-all | bytes 1024 | tf_op jit(solution)/shard_map/all_to_all | solution.py:51
  39.4 0.1 copy.19
  39.4 0.1 copy.20
  39.5 0.1 reshape.162
  39.7 0.0 copy-done
  39.7 0.9 gather_fusion
  40.6 0.9 reshape.161
  41.5 4.6 %all-to-all-start.1 = ((bf16[64,2,1408]{2,1,0:T(2,128)(2,1)}), bf16[64,2,1408]{2,1,0:T(2,128)(2,1)S(1)}, u32[]{:S(2)}, u32[]{:S(2)}) async-start(bf16[64,2,1408]{2,1,0:T(2,128)(2,1)} %reshape.161), calls=%async_computation.1 | async-start | bytes 720896 | tf_op jit(solution)/shard_map/all_to_all | solution.py:53
  46.1 0.0 all-gather.10.cloned.1.call-start
  46.2 13.4 %all-to-all-done.1 = bf16[64,2,1408]{2,1,0:T(2,128)(2,1)S(1)} async-done(((bf16[64,2,1408]{2,1,0:T(2,128)(2,1)}), bf16[64,2,1408]{2,1,0:T(2,128)(2,1)S(1)}, u32[]{:S(2)}, u32[]{:S(2)}) %all-to-all-start.1) | async-done | bytes 360480 | tf_op jit(solution)/shard_map/all_to_all | solution.py:53
  59.6 0.1 reshape.158
  59.7 0.7 gather_fusion.1
  60.4 40.8 %all-gather.14.cloned.1.call-done = bf16[64,22,1024]{2,1,0:T(8,128)(2,1)} async-done(((bf16[1,22,1024]{2,1,0:T(8,128)(2,1)}), bf16[64,22,1024]{2,1,0:T(8,128)(2,1)}) %all-gather.14.cloned.1.call-update) | async-done | bytes 2883600 | tf_op jit(solution)/shard_map/all_gather | solution.py:27
  101.3 5.4 %reshape.219 = bf16[1408,1024]{1,0:T(8,128)(2,1)} reshape(bf16[64,22,1024]{2,1,0:T(8,128)(2,1)} %all-gather.14.cloned.1.call-done) | data formatting | bytes 5767168
  106.7 2.6 multiply_reduce_fusion.4
  109.3 0.7 multiply_convert_fusion.3
  110.0 0.0 all-gather.10.cloned.1.call-update
  110.0 0.8 scatter_custom_fusion.1
  110.8 0.1 all_to_all.26
  111.0 18.9 %all_to_all.35 = s32[64,1,2]{2,1,0:T(1,128)S(1)} all-to-all(s32[64,1,2]{2,1,0:T(1,128)S(1)} %bitcast.77), channel_id=1, replica_groups=mesh['dp'=64,'group'=8] {'dp'}, dimensions={0} | all-to-all | bytes 1024 | tf_op jit(solution)/shard_map/all_to_all | solution.py:51
  129.8 0.1 copy.22
  129.9 0.1 copy.23
  130.0 0.1 reshape.178
  130.2 0.9 gather_fusion.2
  131.1 0.9 reshape.177
  132.0 4.6 %all-to-all-start.3 = ((bf16[64,2,1408]{2,1,0:T(2,128)(2,1)}), bf16[64,2,1408]{2,1,0:T(2,128)(2,1)S(1)}, u32[]{:S(2)}, u32[]{:S(2)}) async-start(bf16[64,2,1408]{2,1,0:T(2,128)(2,1)} %reshape.177), calls=%async_computation.3 | async-start | bytes 720896 | tf_op jit(solution)/shard_map/all_to_all | solution.py:53
  136.6 0.0 all-gather.12.cloned.1.call-start
  136.6 1.2 dynamic-slice
  138.5 0.0 copy-done.3
  138.5 0.1 fusion.60
  138.6 11.1 %all-to-all-done.3 = bf16[64,2,1408]{2,1,0:T(2,128)(2,1)S(1)} async-done(((bf16[64,2,1408]{2,1,0:T(2,128)(2,1)}), bf16[64,2,1408]{2,1,0:T(2,128)(2,1)S(1)}, u32[]{:S(2)}, u32[]{:S(2)}) %all-to-all-start.3) | async-done | bytes 360480 | tf_op jit(solution)/shard_map/all_to_all | solution.py:53
  149.7 0.1 reshape.159
  149.8 0.7 gather_fusion.3
  150.5 2.5 multiply_reduce_fusion.1
  153.1 0.8 multiply_convert_fusion.1
  153.9 0.0 all-gather.12.cloned.1.call-update
  153.9 0.1 fusion.61
  155.3 14.8 %all-reduce.2 = (s32[512]{0:T(512)S(1)}, s32[512]{0:T(512)S(1)}) all-reduce(s32[512]{0:T(512)S(1)} %fusion.61, s32[512]{0:T(512)S(1)} %fusion.60), channel_id=3, replica_groups=mesh['dp'=64,'group'=8] {'group'}, use_global_device_ids=true, to_apply=%add.1 | all-reduce | flops 1024 | bytes 8192
  170.1 21.4 %all-gather.8.cloned.1.call-done = bf16[2048,1024]{1,0:T(8,128)(2,1)} async-done(((bf16[32,1024]{1,0:T(8,128)(2,1)}), bf16[2048,1024]{1,0:T(8,128)(2,1)}) %all-gather.8.cloned.1.call-update) | async-done | bytes 4194320 | tf_op jit(solution)/shard_map/all_gather | solution.py:28
  191.4 3.3 %multiply_reduce_fusion.5 = (f32[64]{0:T(128)S(1)}, f32[64,1024]{1,0:T(8,128)S(1)}) fusion(bf16[2048,1024]{1,0:T(8,128)(2,1)} %all-gather.8.cloned.1.call-done, bf16[2,64,2048]{2,1,0:T(8,128)(2,1)S(1)} %copy-done.2), kind=kOutput, calls=%fused_computation.45 | convolution fusion | flops 268566464 | bytes 4718848 | tf_op jit(solution)/shard_map/dot_general | solution.py:58
  194.7 0.1 copy-done.1
  194.9 1.0 multiply_reduce_fusion.2
  195.9 27.6 %all-gather.10.cloned.1.call-done = bf16[512,1024]{1,0:T(8,128)(2,1)} async-done(((bf16[64,1024]{1,0:T(8,128)(2,1)}), bf16[512,1024]{1,0:T(8,128)(2,1)}) %all-gather.10.cloned.1.call-update) | async-done | bytes 1048592 | tf_op jit(solution)/shard_map/all_gather | solution.py:64
  223.5 2.4 multiply_reduce_fusion.3
  225.9 3.6 %fusion = bf16[1,64,2048]{2,1,0:T(8,128)(2,1)S(1)} fusion(bf16[2048,1024]{1,0:T(8,128)(2,1)} %all-gather.8.cloned.1.call-done, f32[64,1024]{1,0:T(8,128)S(1)} %get-tuple-element.26, f32[64,1024]{1,0:T(8,128)S(1)} %get-tuple-element.24, f32[64]{0:T(128)S(1)} %get-tuple-element.25, f32[64]{0:T(128)S(1)} %add_rsqrt_fusion.3), kind=kOutput, calls=%fused_computation.8 | convolution fusion | flops 268894208 | bytes 4981248 | tf_op jit(solution)/shard_map/dot_general | solution.py:90
  229.5 24.7 %all-gather.12.cloned.1.call-done = bf16[512,1024]{1,0:T(8,128)(2,1)} async-done(((bf16[64,1024]{1,0:T(8,128)(2,1)}), bf16[512,1024]{1,0:T(8,128)(2,1)}) %all-gather.12.cloned.1.call-update) | async-done | bytes 1048592 | tf_op jit(solution)/shard_map/all_gather | solution.py:64
  254.1 2.4 multiply_reduce_fusion
  256.6 3.6 %fusion.1 = bf16[1,64,2048]{2,1,0:T(8,128)(2,1)S(1)} fusion(bf16[2048,1024]{1,0:T(8,128)(2,1)} %all-gather.8.cloned.1.call-done, f32[64,1024]{1,0:T(8,128)S(1)} %get-tuple-element.20, f32[64,1024]{1,0:T(8,128)S(1)} %get-tuple-element.18, f32[64]{0:T(128)S(1)} %get-tuple-element.19, f32[64]{0:T(128)S(1)} %add_rsqrt_fusion.1), kind=kOutput, calls=%fused_computation.9 | convolution fusion | flops 268894208 | bytes 4981248 | tf_op jit(solution)/shard_map/dot_general | solution.py:90
  260.2 0.8 pad_maximum_fusion
  (17 shorter events, 0.1 us)
Async XLA Ops:
  6.5 33.2 %copy-start = (bf16[256,1408]{1,0:T(8,128)(2,1)S(1)}, bf16[256,1408]{1,0:T(8,128)(2,1)}, u32[]{:S(2)}) copy-start(bf16[256,1408]{1,0:T(8,128)(2,1)} %param.10) | copy-start | bytes 2162692
  6.5 94.7 %all-gather.14.cloned.1.call-start = ((), (), s32[]{:S(2)}) async-start(), calls=%async_computation.7 | async-start | bytes 3194880 | tf_op jit(solution)/shard_map/all_gather | solution.py:27
  7.3 184.2 %all-gather.8.cloned.1.call-start = ((), (), s32[]{:S(2)}) async-start(), calls=%async_computation.4 | async-start | bytes 4259840 | tf_op jit(solution)/shard_map/all_gather | solution.py:28
  41.5 18.1 %all-to-all-start.1 = ((bf16[64,2,1408]{2,1,0:T(2,128)(2,1)}), bf16[64,2,1408]{2,1,0:T(2,128)(2,1)S(1)}, u32[]{:S(2)}, u32[]{:S(2)}) async-start(bf16[64,2,1408]{2,1,0:T(2,128)(2,1)} %reshape.161), calls=%async_computation.1 | async-start | bytes 720896 | tf_op jit(solution)/shard_map/all_to_all | solution.py:53
  46.1 177.4 %all-gather.10.cloned.1.call-start = ((), (), s32[]{:S(2)}) async-start(), calls=%async_computation.5 | async-start | bytes 1179648 | tf_op jit(solution)/shard_map/all_gather | solution.py:64
  106.7 31.8 %copy-start.3 = (s32[2,64]{1,0:T(2,128)S(1)}, s32[2,64]{1,0:T(2,128)}, u32[]{:S(2)}) copy-start(s32[2,64]{1,0:T(2,128)} %param.13) | copy-start | bytes 1540
  131.1 60.4 %copy-start.2 = (bf16[2,64,2048]{2,1,0:T(8,128)(2,1)S(1)}, bf16[2,64,2048]{2,1,0:T(8,128)(2,1)}, u32[]{:S(2)}) copy-start(bf16[2,64,2048]{2,1,0:T(8,128)(2,1)} %param.9) | copy-start | bytes 1572868
  132.0 17.7 %all-to-all-start.3 = ((bf16[64,2,1408]{2,1,0:T(2,128)(2,1)}), bf16[64,2,1408]{2,1,0:T(2,128)(2,1)S(1)}, u32[]{:S(2)}, u32[]{:S(2)}) async-start(bf16[64,2,1408]{2,1,0:T(2,128)(2,1)} %reshape.177), calls=%async_computation.3 | async-start | bytes 720896 | tf_op jit(solution)/shard_map/all_to_all | solution.py:53
  136.6 117.5 %all-gather.12.cloned.1.call-start = ((), (), s32[]{:S(2)}) async-start(), calls=%async_computation.6 | async-start | bytes 1179648 | tf_op jit(solution)/shard_map/all_gather | solution.py:64
  191.4 3.4 %copy-start.1 = (bf16[2048,1024]{1,0:T(8,128)(2,1)S(1)}, bf16[2048,1024]{1,0:T(8,128)(2,1)}, u32[]{:S(2)}) copy-start(bf16[2048,1024]{1,0:T(8,128)(2,1)} %all-gather.8.cloned.1.call-done) | copy-start | bytes 12582916
Sparse Core Ops, SparseCore 0:
  10.4 90.8 all-gather.13
  104.3 87.0 all-gather.7
  193.6 29.8 all-gather.9
  225.5 28.5 all-gather.11
where the time goes:
time: 268 us
  waiting for transfers between devices  140 us (52%)
  blocking collectives  61.4 us (23%)
  matrix products  21.3 us (8%)
  local copies, waits for them, and re-layouts  16.2 us (6%)
  between operations  15.2 us (6%)
  starting transfers between devices  9.38 us (4%)
  other arithmetic  3.6 us (1%)
    all_gather x2, waiting for transfers between devices, local(): lax.all_gather(image_emb, 'group', axis=0, tiled=True)  52.3 us
    all_to_all x2, blocking collectives, local(): lax.all_to_all(requests, 'dp', split_axis=0, concat_axis=0, tiled=True)  46.7 us
    all_gather x1, waiting for transfers between devices, local(): lax.all_gather(picture_embedding_weights, 'dp', axis=0, tiled=True)  40.8 us
    all_to_all x2, waiting for transfers between devices, local(): lax.all_to_all(served, 'dp', split_axis=0, concat_axis=0, tiled=True)  24.5 us
    all_gather x1, waiting for transfers between devices, local(): lax.all_gather(caption_embedding_weights, 'dp', axis=0, tiled=True)  21.4 us
    unnamed x1, blocking collectives  14.8 us
    all_to_all x2, starting transfers between devices, local(): lax.all_to_all(served, 'dp', split_axis=0, concat_axis=0, tiled=True)  9.26 us
    dot_general x2, matrix products, local(): lax.dot_general(grad_raw, text_full, (((1,), (1,)), ((), ())), preferred_...  7.2 us
  transfers between devices with their start and end apart: 6, of which 6 were waited for; matrix products, arithmetic and copies ran while one was open for 13% of the time, Pallas kernels for 0%

commit v1 on v0

v1 whole, which is shorter than its diff:
```python
import functools

import jax
import jax.numpy as jnp
from jax import lax
from jax.experimental import pallas as pl
from jax.experimental.pallas import tpu as pltpu
from jax.sharding import Mesh, PartitionSpec as P

EPS = 1e-06
LOSS_SCALE = 256.0
CAP = 2
LANES = 128
BF = jnp.bfloat16
F32 = jnp.float32
I32 = jnp.int32
VMEM = pl.BlockSpec(memory_space=pltpu.VMEM)
SMEM = pl.BlockSpec(memory_space=pltpu.SMEM)
ANY = pl.BlockSpec(memory_space=pl.ANY)
PARAMS = pltpu.CompilerParams(vmem_limit_bytes=40 * 1024 * 1024)


def dot(a, b, left, right):
    return lax.dot_general(a, b, (((left,), (right,)), ((), ())), preferred_element_type=F32)


def iota(shape, dim):
    return lax.broadcasted_iota(I32, shape, dim)


def as_column(row):
    return jnp.broadcast_to(row, (row.shape[1], row.shape[1])).T


def ask_kernel(micro, rows, owners, info, ask, slot):
    members = info.shape[0]
    pairs, slots = micro * rows, members * micro * CAP
    r, c = iota((pairs, pairs), 0), iota((pairs, pairs), 1)
    before = ((r < c) & ((r >= rows) == (c >= rows))).astype(F32).astype(BF)
    owner_id, slot_id = iota((owners, pairs), 0), iota((LANES, pairs), 0)
    half = (iota((1, pairs), 1) >= rows).astype(I32) * CAP
    total = jnp.zeros((owners, LANES), F32)
    for g in range(members):
        own, pos = info[g, 0:1, :], info[g, 1:2, :]
        hit = own == owner_id
        hits = hit.astype(F32)
        earlier = dot(hits.astype(BF), before, 1, 0)
        nth = jnp.sum(hits * earlier, axis=0, keepdims=True).astype(I32)
        place = g * micro * CAP + half + nth
        slot[g:g + 1, :] = own * slots + place
        put = jnp.where(place == slot_id, pos, 0).astype(F32).astype(BF)
        total = total + dot(hits.astype(BF), put, 1, 1)
    ask[...] = total.astype(BF)


def unsort_kernel(slot, fetched, mine):
    members, pairs = slot.shape
    count = fetched.shape[0]
    lane = iota((pairs, count), 1)
    for g in range(members):
        column = as_column(slot[g:g + 1, :])
        where = (lane == jnp.concatenate([column] * (count // pairs), axis=1)).astype(F32).astype(BF)
        mine[g * pairs:(g + 1) * pairs, :] = dot(where, fetched[...], 1, 0).astype(BF)


def load_columns(order, pieces, whole, sems):
    width = whole.shape[1] // len(pieces)
    copies = [
        pltpu.make_async_copy(
            piece, whole.at[:, pl.ds(pl.multiple_of(order[k] * width, LANES), width)], sems.at[k]
        )
        for k, piece in enumerate(pieces)
    ]
    for copy in copies:
        copy.start()
    return copies


def text_kernel(members, order, text, *refs):
    pieces, (unit, inverse, wt, sems) = refs[:members], refs[members:]
    for copy in load_columns(order, pieces, wt, sems):
        copy.wait()
    raw = dot(text[...], wt[...], 1, 0)
    inv = lax.rsqrt(jnp.sum(raw * raw, axis=1, keepdims=True) + EPS)
    unit[...] = raw * inv
    inverse[...] = jnp.broadcast_to(inv, inverse.shape)


def grad_kernel(members, rows, order, scalars, info, labels, unit, inverse, *refs):
    images, weights = refs[:members], refs[members:2 * members]
    out, img, wt, slopes, img_sems, wt_sems = refs[2 * members:]
    img_copies = load_columns(order, images, img, img_sems)
    wt_copies = load_columns(order, weights, wt, wt_sems)
    gain, offset = scalars[0], scalars[1]
    pairs = unit.shape[0]
    text = unit[...].astype(BF)
    same_micro = (iota((pairs, pairs), 0) >= rows) == (iota((pairs, pairs), 1) >= rows)
    for copy in img_copies:
        copy.wait()
    for g in range(members):
        span = slice(g * pairs, (g + 1) * pairs)
        block = img[span, :]
        wide = block.astype(F32)
        inv = lax.rsqrt(jnp.sum(wide * wide, axis=1, keepdims=True) + EPS)
        logit = gain * inv * dot(block, text, 1, 1) + offset
        match = (as_column(info[g, 2:3, :]) == labels[...]).astype(F32)
        slope = LOSS_SCALE * inv * (jax.nn.sigmoid(logit) - match)
        slopes[span, :] = jnp.where(same_micro, slope, 0.0).astype(BF)
    grad = gain * dot(slopes[...], img[...], 0, 0)
    grad = grad - unit[...] * jnp.sum(unit[...] * grad, axis=1, keepdims=True)
    grad = (inverse[:, 0:1] * grad).astype(BF)
    for copy in wt_copies:
        copy.wait()
    out[...] = dot(grad, wt[...], 1, 1).astype(BF)


def make_local(nz, ny, nx, nc):
    members, owners = nx * nc, nz * ny

    def swap(v):
        return lax.ppermute(v, "core", [(i, nc - 1 - i) for i in range(nc)])

    def shift(v, by):
        return lax.ppermute(v, "x", [(i, (i + by) % nx) for i in range(nx)])

    def turn(v):
        moves = [(i * nc + c, (i + (1 if c == 0 else -1)) % nx * nc + c) for i in range(nx) for c in range(nc)]
        return lax.ppermute(v, ("x", "core"), moves)

    def whole_group(v, core):
        up, down = shift(v, 1), shift(v, -1)
        far = turn(jnp.where(core == 0, up, down))
        near = [v, up, far, down]
        return near + [swap(p) for p in near]

    def local(text, cache, owner, entry, labels, wi, wt, stretch, offset):
        micro, rows, d_txt = text.shape
        d_img, emb = cache.shape[1], wi.shape[1]
        wi_rows, wt_rows = wi.shape[0], wt.shape[0]
        width = emb // members
        pairs = micro * rows
        slots = members * micro * CAP
        x, core = lax.axis_index("x"), lax.axis_index("core")
        me = x * nc + core
        order = jnp.stack([(x - k) % nx * nc + (core ^ d) for d in range(nc) for k in range(nx)])

        info = jnp.stack([owner.reshape(pairs), entry.reshape(pairs), labels.reshape(pairs)])
        info = jnp.broadcast_to(info[None], (members,) + info.shape)
        info = lax.all_to_all(info, ("x", "core"), split_axis=0, concat_axis=0, tiled=True)
        ask, slot = pl.pallas_call(
            functools.partial(ask_kernel, micro, rows, owners),
            out_shape=(
                jax.ShapeDtypeStruct((owners, LANES), BF),
                jax.ShapeDtypeStruct((members, pairs), I32),
            ),
            in_specs=[VMEM],
            out_specs=(VMEM, VMEM),
            compiler_params=PARAMS,
        )(info)

        wi_pad = -(-(wi_rows + 1) // 8) * 8
        wt_part = lax.dynamic_slice(wt, (0, me * width), (wt_rows, width))
        wi_part = lax.dynamic_slice(wi, (0, me * width), (wi_rows, width))
        fixed = jnp.concatenate([wt_part, wi_part], axis=0)
        sent = jnp.concatenate(
            [
                jnp.broadcast_to(fixed[None], (owners,) + fixed.shape),
                ask[:, None, :],
                jnp.zeros((owners, wi_pad - wi_rows - 1, width), BF),
            ],
            axis=1,
        )
        got = lax.all_to_all(sent, ("z", "y"), split_axis=0, concat_axis=0, tiled=True)

        old, new = iota((d_img, owners * wi_pad), 0), iota((d_img, owners * wi_pad), 1)
        spread = (old // wi_rows * wi_pad + old % wi_rows == new).astype(BF)
        cache_pad = dot(cache, spread, 1, 0).astype(BF)
        wi_all = got[:, wt_rows:].reshape(owners * wi_pad, width)
        table = dot(cache_pad, wi_all, 1, 0).astype(BF)
        asked = got[:, wt_rows + wi_rows, :slots].astype(I32).reshape(-1)
        pick = (asked[:, None] == jnp.arange(cache.shape[0], dtype=I32)).astype(BF)
        served = dot(pick, table, 1, 0).astype(BF).reshape(owners, slots, width)
        fetched = lax.all_to_all(served, ("z", "y"), split_axis=0, concat_axis=0, tiled=True)
        mine = pl.pallas_call(
            unsort_kernel,
            out_shape=jax.ShapeDtypeStruct((members * pairs, width), BF),
            in_specs=[VMEM, VMEM],
            out_specs=VMEM,
            compiler_params=PARAMS,
        )(slot, fetched.reshape(owners * slots, width))

        wt_pieces = whole_group(got[:, :wt_rows].reshape(owners * wt_rows, width), core)
        unit, inverse = pl.pallas_call(
            functools.partial(text_kernel, members),
            out_shape=(
                jax.ShapeDtypeStruct((pairs, emb), F32),
                jax.ShapeDtypeStruct((pairs, LANES), F32),
            ),
            in_specs=[SMEM, VMEM] + [ANY] * members,
            out_specs=(VMEM, VMEM),
            scratch_shapes=[
                pltpu.VMEM((d_txt, emb), BF),
                pltpu.SemaphoreType.DMA((members,)),
            ],
            compiler_params=PARAMS,
            cost_estimate=pl.CostEstimate(
                flops=2 * pairs * d_txt * emb, bytes_accessed=2 * d_txt * emb, transcendentals=0
            ),
        )(order, text.reshape(pairs, d_txt), *wt_pieces)

        image_pieces = whole_group(mine, core)
        out = pl.pallas_call(
            functools.partial(grad_kernel, members, rows),
            out_shape=jax.ShapeDtypeStruct((pairs, d_txt), BF),
            in_specs=[SMEM, SMEM, VMEM, VMEM, VMEM, VMEM] + [ANY] * (2 * members),
            out_specs=VMEM,
            scratch_shapes=[
                pltpu.VMEM((members * pairs, emb), BF),
                pltpu.VMEM((d_txt, emb), BF),
                pltpu.VMEM((members * pairs, pairs), BF),
                pltpu.SemaphoreType.DMA((members,)),
                pltpu.SemaphoreType.DMA((members,)),
            ],
            compiler_params=PARAMS,
            cost_estimate=pl.CostEstimate(
                flops=2 * pairs * d_txt * emb, bytes_accessed=2 * d_txt * emb, transcendentals=0
            ),
        )(
            order,
            jnp.concatenate([stretch, offset]),
            info,
            labels.reshape(1, pairs),
            unit,
            inverse,
            *image_pieces,
            *wt_pieces,
        )
        return out.reshape(micro, rows, d_txt)

    return local


def solution(mesh):
    nz, ny, nx, nc = 8, 8, 4, 2
    fine = Mesh(mesh.devices.reshape(nz, ny, nx, nc), ("z", "y", "x", "core"))
    dp, every = ("z", "y"), ("z", "y", "x", "core")
    return jax.shard_map(
        make_local(nz, ny, nx, nc),
        mesh=fine,
        in_specs=(
            P(None, every, None),
            P(dp, None),
            P(None, every, None),
            P(None, every),
            P(None, every),
            P(dp, None),
            P(dp, None),
            P(),
            P(),
        ),
        out_specs=P(None, every, None),
        check_vma=False,
    )
```

time: 268 us -> 142 us (0.53)
  waiting for transfers between devices: 140 us -> 36.2 us
  starting transfers between devices: 9.38 us -> 71.1 us
  blocking collectives: 61.4 us -> 0 us
  matrix products: 21.3 us -> 5.29 us
  between operations: 15.2 us -> 1.88 us
  Pallas kernels: 0 us -> 12.1 us
  local copies, waits for them, and re-layouts: 16.2 us -> 9.4 us
    all_gather x4 -> x0, waiting for transfers between devices: 115 us -> none  [the longest x2 52.3 us: local(): lax.all_gather(image_emb, 'group', axis=0, tiled=True)]
    all_to_all x2 -> x0, blocking collectives: 46.7 us -> none  [local(): lax.all_to_all(requests, 'dp', split_axis=0, concat_axis=0, tiled=True)]
    ppermute x0 -> x14, starting transfers between devices: none -> 41.4 us  [the longest x8 22.1 us: swap(): return lax.ppermute(v, 'core', [(i, nc - 1 - i) for i in range(nc)])]
    all_to_all x2 -> x3, starting transfers between devices: 9.26 us -> 29.7 us  [the longest x1 12 us: local(): lax.all_to_all(sent, ('z', 'y'), split_axis=0, concat_axis=0, tiled=True)]
    dot_general x8 -> x3, matrix products: 21.3 us -> 5.29 us  [dot(): lax.dot_general(a, b, (((left,), (right,)), ((), ())), preferred_element_...]
    unnamed x1 -> x0, blocking collectives: 14.8 us -> none
    pallas_call x0 -> x4, Pallas kernels: none -> 12.1 us  [the longest x1 5.98 us: local(): pl.pallas_call(functools.partial(grad_kernel, members, rows), out_shape=j...]
    all_to_all x2 -> x3, waiting for transfers between devices: 24.5 us -> 35.3 us  [the longest x1 21.2 us: local(): lax.all_to_all(sent, ('z', 'y'), split_axis=0, concat_axis=0, tiled=True)]
  transfers between devices with their start and end apart: 6 -> 17, of which waited for: 6 -> 4; matrix products, arithmetic and copies ran while one was open for 13% -> 6% of each run, Pallas kernels for 0% -> 4%
where the time goes in v1:
time: 142 us; the launch traced here: 141 us
  starting transfers between devices  71.1 us (50%)
  waiting for transfers between devices  36.2 us (25%)
  Pallas kernels  12.1 us (9%)
  local copies, waits for them, and re-layouts  9.4 us (7%)
  matrix products  5.29 us (4%)
  other arithmetic  4.67 us (3%)
  between operations  1.88 us (1%)
    ppermute x8, starting transfers between devices, swap(): return lax.ppermute(v, 'core', [(i, nc - 1 - i) for i in range(nc)])  22.1 us
    all_to_all x1, waiting for transfers between devices, local(): lax.all_to_all(sent, ('z', 'y'), split_axis=0, concat_axis=0, tiled=True)  21.2 us
    all_to_all x1, starting transfers between devices, local(): lax.all_to_all(sent, ('z', 'y'), split_axis=0, concat_axis=0, tiled=True)  12 us
    ppermute x4, starting transfers between devices, shift(): return lax.ppermute(v, 'x', [(i, (i + by) % nx) for i in range(nx)])  11.3 us
    all_to_all x1, waiting for transfers between devices, local(): lax.all_to_all(served, ('z', 'y'), split_axis=0, concat_axis=0, tiled=True)  10.9 us
    all_to_all x1, starting transfers between devices, local(): lax.all_to_all(info, ('x', 'core'), split_axis=0, concat_axis=0, tiled=True)  10.1 us
    ppermute x2, starting transfers between devices, turn(): return lax.ppermute(v, ('x', 'core'), moves)  7.96 us
    all_to_all x1, starting transfers between devices, local(): lax.all_to_all(served, ('z', 'y'), split_axis=0, concat_axis=0, tiled=True)  7.62 us
  transfers between devices with their start and end apart: 17, of which 4 were waited for; matrix products, arithmetic and copies ran while one was open for 6% of the time, Pallas kernels for 4%

profile of v1, /device:TPU:1, one launch (start us, length us, event | category | flops | bytes accessed | tf_op | source)
XLA Modules:
  0.0 140.7 jit_solution(12007968712118223353)
XLA Ops:
  0.0 0.8 stack_reshape.11.labels
  0.8 0.5 broadcast.43
  1.3 1.3 reduce.7
  2.7 0.1 stack_reshape.9
  2.8 0.8 stack_reshape.10
  3.5 0.6 broadcast_in_dim.8
  4.2 10.1 %all-to-all-start = ((s32[8,3,128]{2,1,0:T(4,128)}), s32[8,3,128]{2,1,0:T(4,128)S(1)}, u32[]{:S(2)}, u32[]{:S(2)}) async-start(s32[8,3,128]{2,1,0:T(4,128)} %broadcast_in_dim.8), calls=%async_computation | async-start | bytes 32768 | tf_op jit(solution)/shard_map/all_to_all | solution.py:149
  14.3 0.7 constant_dynamic-slice_fusion
  15.0 0.7 constant_dynamic-slice_fusion.1
  15.7 0.1 pad.2.clone
  15.8 3.2 %all-to-all-done.info = s32[8,3,128]{2,1,0:T(4,128)S(1)} async-done(((s32[8,3,128]{2,1,0:T(4,128)}), s32[8,3,128]{2,1,0:T(4,128)S(1)}, u32[]{:S(2)}, u32[]{:S(2)}) %all-to-all-start) | async-done | bytes 12320 | tf_op jit(solution)/shard_map/all_to_all | solution.py:149
  18.9 0.7 shard_map.91
  19.6 0.1 copy.12
  19.7 0.1 broadcast_in_dim.9
  19.8 1.2 maximum_maximum_fusion
  21.1 12.0 %all-to-all-start.1 = ((bf16[64,56,128]{2,1,0:T(8,128)(2,1)}), bf16[64,56,128]{2,1,0:T(8,128)(2,1)S(1)}, u32[]{:S(2)}, u32[]{:S(2)}) async-start(bf16[64,56,128]{2,1,0:T(8,128)(2,1)} %maximum_maximum_fusion), calls=%async_computation.1 | async-start | bytes 1835008 | tf_op jit(solution)/shard_map/all_to_all | solution.py:173
  33.1 3.6 %fusion.5.clone.6 = bf16[1536,256]{1,0:T(8,128)(2,1)} fusion(bf16[256,1408]{1,0:T(8,128)(2,1)S(1)} %copy-done, s32[1408]{0:T(1024)S(1)} %get-tuple-element.14, s32[1408]{0:T(1024)S(1)} %get-tuple-element.15, s32[1408]{0:T(1024)S(1)} %get-tuple-element.13, s32[1408]{0:T(1024)S(1)} %get-tuple-element.16, ...), kind=kOutput, calls=%fused_computation.5.clone.clone.clone.clone.clone.1 | convolution fusion | flops 1120665600 | bytes 1532672 | tf_op jit(solution)/shard_map/dot_general | solution.py:24
  36.6 21.2 %all-to-all-done.1 = bf16[64,56,128]{2,1,0:T(8,128)(2,1)S(1)} async-done(((bf16[64,56,128]{2,1,0:T(8,128)(2,1)}), bf16[64,56,128]{2,1,0:T(8,128)(2,1)S(1)}, u32[]{:S(2)}, u32[]{:S(2)}) %all-to-all-start.1) | async-done | bytes 917536 | tf_op jit(solution)/shard_map/all_to_all | solution.py:173
  57.9 2.9 %collective-permute-start.1 = (bf16[2048,128]{1,0:T(8,128)(2,1)S(1)}, bf16[2048,128]{1,0:T(8,128)(2,1)S(1)}, u32[]{:S(2)}, u32[]{:S(2)}) collective-permute-start(bf16[2048,128]{1,0:T(8,128)(2,1)S(1)} %bitcast.25), channel_id=1, source_target_pairs={{0,6},{2,0},{4,2},{6,4},{1,7},{3,1},{5,3},{7,5},{8,14},{10,8},{12,... | collective-permute-start | bytes 1572872 | tf_op jit(solution)/shard_map/ppermute | solution.py:124
  60.8 2.5 %collective-permute-start = (bf16[2048,128]{1,0:T(8,128)(2,1)S(1)}, bf16[2048,128]{1,0:T(8,128)(2,1)S(1)}, u32[]{:S(2)}, u32[]{:S(2)}) collective-permute-start(bf16[2048,128]{1,0:T(8,128)(2,1)S(1)} %bitcast.26), channel_id=1, source_target_pairs={{0,2},{2,4},{4,6},{6,0},{1,3},{3,5},{5,7},{7,1},{8,10},{10,12},{12... | collective-permute-start | bytes 1572872 | tf_op jit(solution)/shard_map/ppermute | solution.py:124
  63.4 0.4 fusion.11
  63.8 0.1 fusion.15
  63.9 0.1 reshape.34
  64.0 1.3 convolution_convert_fusion
  65.3 7.6 %all-to-all-start.2 = ((bf16[64,32,128]{2,1,0:T(8,128)(2,1)}), bf16[64,32,128]{2,1,0:T(8,128)(2,1)S(1)}, u32[]{:S(2)}, u32[]{:S(2)}) async-start(bf16[64,32,128]{2,1,0:T(8,128)(2,1)} %bitcast.12), calls=%async_computation.2 | async-start | bytes 1048576 | tf_op jit(solution)/shard_map/all_to_all | solution.py:183
  73.0 0.0 collective-permute-done.1.refs_3_.refs_11_
  73.0 0.9 collective-permute-done.refs_1_.refs_9_
  73.9 0.8 broadcast_select_fusion
  74.7 3.1 %collective-permute-start.2 = (bf16[2048,128]{1,0:T(8,128)(2,1)}, bf16[2048,128]{1,0:T(8,128)(2,1)S(1)}, u32[]{:S(2)}, u32[]{:S(2)}) collective-permute-start(bf16[2048,128]{1,0:T(8,128)(2,1)} %broadcast_select_fusion), channel_id=1, source_target_pairs={{0,2},{1,7},{2,4},{3,1},{4,6},{5,3},{6,0},{7,5},{8,10},{9,15},{10,... | collective-permute-start | bytes 1572872 | tf_op jit(solution)/shard_map/ppermute | solution.py:128
  77.8 10.9 %all-to-all-done.2 = bf16[64,32,128]{2,1,0:T(8,128)(2,1)S(1)} async-done(((bf16[64,32,128]{2,1,0:T(8,128)(2,1)}), bf16[64,32,128]{2,1,0:T(8,128)(2,1)S(1)}, u32[]{:S(2)}, u32[]{:S(2)}) %all-to-all-start.2) | async-done | bytes 524320 | tf_op jit(solution)/shard_map/all_to_all | solution.py:183
  88.7 2.0 %shard_map.93.refs_0_ = bf16[1024,128]{1,0:T(8,128)(2,1)} custom-call(s32[8,128]{1,0:T(8,128)S(1)} %get-tuple-element.12.slot, bf16[2048,128]{1,0:T(8,128)(2,1)S(1)} %bitcast.30), custom_call_target="tpu_custom_call" | custom-call | tf_op jit(solution)/shard_map/pallas_call | solution.py:184
  90.7 4.0 %collective-permute-start.8 = (bf16[1024,128]{1,0:T(8,128)(2,1)}, bf16[1024,128]{1,0:T(8,128)(2,1)}, u32[]{:S(2)}, u32[]{:S(2)}) collective-permute-start(bf16[1024,128]{1,0:T(8,128)(2,1)} %shard_map.93.refs_0_), channel_id=1, source_target_pairs={{0,6},{2,0},{4,2},{6,4},{1,7},{3,1},{5,3},{7,5},{8,14},{10,8},{12,... | collective-permute-start | bytes 786440 | tf_op jit(solution)/shard_map/ppermute | solution.py:124
  94.7 1.9 %collective-permute-start.7 = (bf16[1024,128]{1,0:T(8,128)(2,1)}, bf16[1024,128]{1,0:T(8,128)(2,1)}, u32[]{:S(2)}, u32[]{:S(2)}) collective-permute-start(bf16[1024,128]{1,0:T(8,128)(2,1)} %shard_map.93.refs_0_), channel_id=1, source_target_pairs={{0,2},{2,4},{4,6},{6,0},{1,3},{3,5},{5,7},{7,1},{8,10},{10,12},{12... | collective-permute-start | bytes 786440 | tf_op jit(solution)/shard_map/ppermute | solution.py:124
  96.7 7.1 %collective-permute-start.3 = (bf16[2048,128]{1,0:T(8,128)(2,1)S(1)}, bf16[2048,128]{1,0:T(8,128)(2,1)S(1)}, u32[]{:S(2)}, u32[]{:S(2)}) collective-permute-start(bf16[2048,128]{1,0:T(8,128)(2,1)S(1)} %bitcast.27), channel_id=1, source_target_pairs={{0,1},{1,0},{2,3},{3,2},{4,5},{5,4},{6,7},{7,6},{8,9},{9,8},{10,11... | collective-permute-start | bytes 1572872 | tf_op jit(solution)/shard_map/ppermute | solution.py:121
  103.7 1.9 %collective-permute-start.6 = (bf16[2048,128]{1,0:T(8,128)(2,1)S(1)}, bf16[2048,128]{1,0:T(8,128)(2,1)S(1)}, u32[]{:S(2)}, u32[]{:S(2)}) collective-permute-start(bf16[2048,128]{1,0:T(8,128)(2,1)S(1)} %collective-permute-done.1.refs_3_.refs_11_), channel_id=1, source_target_pairs={{0,1},{1,0},{2,3},{3,2},{4,5},{5,4},{6,7},{7,6},{8,9},{9,8},{10,11... | collective-permute-start | bytes 1572872 | tf_op jit(solution)/shard_map/ppermute | solution.py:121
  105.7 0.0 collective-permute-done.2.refs_2_.refs_10_
  105.7 2.4 %collective-permute-start.4 = (bf16[2048,128]{1,0:T(8,128)(2,1)S(1)}, bf16[2048,128]{1,0:T(8,128)(2,1)S(1)}, u32[]{:S(2)}, u32[]{:S(2)}) collective-permute-start(bf16[2048,128]{1,0:T(8,128)(2,1)S(1)} %collective-permute-done.refs_1_.refs_9_), channel_id=1, source_target_pairs={{0,1},{1,0},{2,3},{3,2},{4,5},{5,4},{6,7},{7,6},{8,9},{9,8},{10,11... | collective-permute-start | bytes 1572872 | tf_op jit(solution)/shard_map/ppermute | solution.py:121
  108.1 0.0 collective-permute-done.8.refs_3_
  108.1 1.9 %collective-permute-start.5 = (bf16[2048,128]{1,0:T(8,128)(2,1)S(1)}, bf16[2048,128]{1,0:T(8,128)(2,1)}, u32[]{:S(2)}, u32[]{:S(2)}) collective-permute-start(bf16[2048,128]{1,0:T(8,128)(2,1)S(1)} %collective-permute-done.2.refs_2_.refs_10_), channel_id=1, source_target_pairs={{0,1},{1,0},{2,3},{3,2},{4,5},{5,4},{6,7},{7,6},{8,9},{9,8},{10,11... | collective-permute-start | bytes 1572872 | tf_op jit(solution)/shard_map/ppermute | solution.py:121
  110.0 0.0 collective-permute-done.7.refs_1_
  110.0 1.0 broadcast_select_fusion.1
  111.0 4.9 %collective-permute-start.9 = (bf16[1024,128]{1,0:T(8,128)(2,1)S(1)}, bf16[1024,128]{1,0:T(8,128)(2,1)}, u32[]{:S(2)}, u32[]{:S(2)}) collective-permute-start(bf16[1024,128]{1,0:T(8,128)(2,1)S(1)} %broadcast_select_fusion.1), channel_id=1, source_target_pairs={{0,2},{1,7},{2,4},{3,1},{4,6},{5,3},{6,0},{7,5},{8,10},{9,15},{10,... | collective-permute-start | bytes 786440 | tf_op jit(solution)/shard_map/ppermute | solution.py:128
  115.9 0.0 collective-permute-done.3.refs_4_.refs_12_
  115.9 1.9 %collective-permute-start.10 = (bf16[1024,128]{1,0:T(8,128)(2,1)}, bf16[1024,128]{1,0:T(8,128)(2,1)}, u32[]{:S(2)}, u32[]{:S(2)}) collective-permute-start(bf16[1024,128]{1,0:T(8,128)(2,1)} %shard_map.93.refs_0_), channel_id=1, source_target_pairs={{0,1},{1,0},{2,3},{3,2},{4,5},{5,4},{6,7},{7,6},{8,9},{9,8},{10,11... | collective-permute-start | bytes 786440 | tf_op jit(solution)/shard_map/ppermute | solution.py:121
  117.8 0.0 collective-permute-done.6.refs_7_.refs_15_
  117.9 0.8 copy-done.1
  118.7 2.4 %collective-permute-start.13 = (bf16[1024,128]{1,0:T(8,128)(2,1)}, bf16[1024,128]{1,0:T(8,128)(2,1)}, u32[]{:S(2)}, u32[]{:S(2)}) collective-permute-start(bf16[1024,128]{1,0:T(8,128)(2,1)} %collective-permute-done.8.refs_3_), channel_id=1, source_target_pairs={{0,1},{1,0},{2,3},{3,2},{4,5},{5,4},{6,7},{7,6},{8,9},{9,8},{10,11... | collective-permute-start | bytes 786440 | tf_op jit(solution)/shard_map/ppermute | solution.py:121
  121.1 0.0 collective-permute-done.4.refs_5_.refs_13_
  121.1 0.0 copy-start.4
  121.1 0.8 copy-done.4
  121.9 1.9 %collective-permute-start.11 = (bf16[1024,128]{1,0:T(8,128)(2,1)}, bf16[1024,128]{1,0:T(8,128)(2,1)}, u32[]{:S(2)}, u32[]{:S(2)}) collective-permute-start(bf16[1024,128]{1,0:T(8,128)(2,1)} %collective-permute-done.7.refs_1_), channel_id=1, source_target_pairs={{0,1},{1,0},{2,3},{3,2},{4,5},{5,4},{6,7},{7,6},{8,9},{9,8},{10,11... | collective-permute-start | bytes 786440 | tf_op jit(solution)/shard_map/ppermute | solution.py:121
  123.8 0.0 collective-permute-done.9.refs_2_
  123.8 2.6 %collective-permute-start.12 = (bf16[1024,128]{1,0:T(8,128)(2,1)}, bf16[1024,128]{1,0:T(8,128)(2,1)}, u32[]{:S(2)}, u32[]{:S(2)}) collective-permute-start(bf16[1024,128]{1,0:T(8,128)(2,1)} %collective-permute-done.9.refs_2_), channel_id=1, source_target_pairs={{0,1},{1,0},{2,3},{3,2},{4,5},{5,4},{6,7},{7,6},{8,9},{9,8},{10,11... | collective-permute-start | bytes 786440 | tf_op jit(solution)/shard_map/ppermute | solution.py:121
  127.8 0.1 stack.38.order
  127.8 0.1 pad_maximum_fusion.1.scalars
  127.9 0.0 collective-permute-done.5.refs_6_.refs_14_
  127.9 1.0 copy-done.2
  129.0 1.0 copy-done.5
  130.0 1.0 copy-done.6
  131.1 3.4 %shard_map.92 = (f32[128,1024]{1,0:T(8,128)S(1)}, f32[128,128]{1,0:T(8,128)S(1)}) custom-call(s32[8]{0:T(128)S(1)} %stack.38.order, bf16[128,2048]{1,0:T(8,128)(2,1)S(1)} %bitcast.31, bf16[2048,128]{1,0:T(8,128)(2,1)S(1)} %bitcast.28, bf16[2048,128]{1,0:T(8,128)(2,1)S(1)} %collective-permute-done.refs_1_.refs_9_, ...), custom_call_target="tpu_custom_call" | custom-call | flops 536870912 | bytes 4194304 | tf_op jit(solution)/shard_map/pallas_call | solution.py:193
  134.5 0.0 collective-permute-done.10.refs_4_
  134.5 0.0 collective-permute-done.13.refs_7_
  134.5 0.0 collective-permute-done.11.refs_5_
  134.5 6.0 %shard_map.94 = bf16[128,2048]{1,0:T(8,128)(2,1)} custom-call(s32[8]{0:T(128)S(1)} %stack.38.order, f32[2]{0:T(128)S(1)} %pad_maximum_fusion.1.scalars, s32[8,3,128]{2,1,0:T(4,128)S(1)} %all-to-all-done.info, s32[1,128]{1,0:T(1,128)S(1)} %stack_reshape.11.labels, f32[128,1024]{1,0:T(8,128)S(1)} %get-tuple-element.10.unit, ...), custom_call_target="tpu_custom_call" | custom-call | flops 536870912 | bytes 4194304 | tf_op jit(solution)/shard_map/pallas_call | solution.py:212
  (18 shorter events, 0.1 us)
Async XLA Ops:
  0.0 33.1 %copy-start = (bf16[256,1408]{1,0:T(8,128)(2,1)S(1)}, bf16[256,1408]{1,0:T(8,128)(2,1)}, u32[]{:S(2)}) copy-start(bf16[256,1408]{1,0:T(8,128)(2,1)} %param.10) | copy-start | bytes 2162692
  4.2 14.8 %all-to-all-start = ((s32[8,3,128]{2,1,0:T(4,128)}), s32[8,3,128]{2,1,0:T(4,128)S(1)}, u32[]{:S(2)}, u32[]{:S(2)}) async-start(s32[8,3,128]{2,1,0:T(4,128)} %broadcast_in_dim.8), calls=%async_computation | async-start | bytes 32768 | tf_op jit(solution)/shard_map/all_to_all | solution.py:149
  21.1 36.8 %all-to-all-start.1 = ((bf16[64,56,128]{2,1,0:T(8,128)(2,1)}), bf16[64,56,128]{2,1,0:T(8,128)(2,1)S(1)}, u32[]{:S(2)}, u32[]{:S(2)}) async-start(bf16[64,56,128]{2,1,0:T(8,128)(2,1)} %maximum_maximum_fusion), calls=%async_computation.1 | async-start | bytes 1835008 | tf_op jit(solution)/shard_map/all_to_all | solution.py:173
  57.8 5.5 %copy-start.7 = (bf16[1536,256]{1,0:T(8,128)(2,1)S(1)}, bf16[1536,256]{1,0:T(8,128)(2,1)}, u32[]{:S(2)}) copy-start(bf16[1536,256]{1,0:T(8,128)(2,1)} %fusion.5.clone.6) | copy-start | bytes 2359300
  57.9 15.1 %collective-permute-start.1 = (bf16[2048,128]{1,0:T(8,128)(2,1)S(1)}, bf16[2048,128]{1,0:T(8,128)(2,1)S(1)}, u32[]{:S(2)}, u32[]{:S(2)}) collective-permute-start(bf16[2048,128]{1,0:T(8,128)(2,1)S(1)} %bitcast.25), channel_id=1, source_target_pairs={{0,6},{2,0},{4,2},{6,4},{1,7},{3,1},{5,3},{7,5},{8,14},{10,8},{12,... | collective-permute-start | bytes 1572872 | tf_op jit(solution)/shard_map/ppermute | solution.py:124
  60.8 13.0 %collective-permute-start = (bf16[2048,128]{1,0:T(8,128)(2,1)S(1)}, bf16[2048,128]{1,0:T(8,128)(2,1)S(1)}, u32[]{:S(2)}, u32[]{:S(2)}) collective-permute-start(bf16[2048,128]{1,0:T(8,128)(2,1)S(1)} %bitcast.26), channel_id=1, source_target_pairs={{0,2},{2,4},{4,6},{6,0},{1,3},{3,5},{5,7},{7,1},{8,10},{10,12},{12... | collective-permute-start | bytes 1572872 | tf_op jit(solution)/shard_map/ppermute | solution.py:124
  65.3 23.4 %all-to-all-start.2 = ((bf16[64,32,128]{2,1,0:T(8,128)(2,1)}), bf16[64,32,128]{2,1,0:T(8,128)(2,1)S(1)}, u32[]{:S(2)}, u32[]{:S(2)}) async-start(bf16[64,32,128]{2,1,0:T(8,128)(2,1)} %bitcast.12), calls=%async_computation.2 | async-start | bytes 1048576 | tf_op jit(solution)/shard_map/all_to_all | solution.py:183
  74.7 31.0 %collective-permute-start.2 = (bf16[2048,128]{1,0:T(8,128)(2,1)}, bf16[2048,128]{1,0:T(8,128)(2,1)S(1)}, u32[]{:S(2)}, u32[]{:S(2)}) collective-permute-start(bf16[2048,128]{1,0:T(8,128)(2,1)} %broadcast_select_fusion), channel_id=1, source_target_pairs={{0,2},{1,7},{2,4},{3,1},{4,6},{5,3},{6,0},{7,5},{8,10},{9,15},{10,... | collective-permute-start | bytes 1572872 | tf_op jit(solution)/shard_map/ppermute | solution.py:128
  90.7 17.4 %collective-permute-start.8 = (bf16[1024,128]{1,0:T(8,128)(2,1)}, bf16[1024,128]{1,0:T(8,128)(2,1)}, u32[]{:S(2)}, u32[]{:S(2)}) collective-permute-start(bf16[1024,128]{1,0:T(8,128)(2,1)} %shard_map.93.refs_0_), channel_id=1, source_target_pairs={{0,6},{2,0},{4,2},{6,4},{1,7},{3,1},{5,3},{7,5},{8,14},{10,8},{12,... | collective-permute-start | bytes 786440 | tf_op jit(solution)/shard_map/ppermute | solution.py:124
  94.7 15.3 %collective-permute-start.7 = (bf16[1024,128]{1,0:T(8,128)(2,1)}, bf16[1024,128]{1,0:T(8,128)(2,1)}, u32[]{:S(2)}, u32[]{:S(2)}) collective-permute-start(bf16[1024,128]{1,0:T(8,128)(2,1)} %shard_map.93.refs_0_), channel_id=1, source_target_pairs={{0,2},{2,4},{4,6},{6,0},{1,3},{3,5},{5,7},{7,1},{8,10},{10,12},{12... | collective-permute-start | bytes 786440 | tf_op jit(solution)/shard_map/ppermute | solution.py:124
  96.7 19.2 %collective-permute-start.3 = (bf16[2048,128]{1,0:T(8,128)(2,1)S(1)}, bf16[2048,128]{1,0:T(8,128)(2,1)S(1)}, u32[]{:S(2)}, u32[]{:S(2)}) collective-permute-start(bf16[2048,128]{1,0:T(8,128)(2,1)S(1)} %bitcast.27), channel_id=1, source_target_pairs={{0,1},{1,0},{2,3},{3,2},{4,5},{5,4},{6,7},{7,6},{8,9},{9,8},{10,11... | collective-permute-start | bytes 1572872 | tf_op jit(solution)/shard_map/ppermute | solution.py:121
  103.7 14.1 %collective-permute-start.6 = (bf16[2048,128]{1,0:T(8,128)(2,1)S(1)}, bf16[2048,128]{1,0:T(8,128)(2,1)S(1)}, u32[]{:S(2)}, u32[]{:S(2)}) collective-permute-start(bf16[2048,128]{1,0:T(8,128)(2,1)S(1)} %collective-permute-done.1.refs_3_.refs_11_), channel_id=1, source_target_pairs={{0,1},{1,0},{2,3},{3,2},{4,5},{5,4},{6,7},{7,6},{8,9},{9,8},{10,11... | collective-permute-start | bytes 1572872 | tf_op jit(solution)/shard_map/ppermute | solution.py:121
  105.7 15.4 %collective-permute-start.4 = (bf16[2048,128]{1,0:T(8,128)(2,1)S(1)}, bf16[2048,128]{1,0:T(8,128)(2,1)S(1)}, u32[]{:S(2)}, u32[]{:S(2)}) collective-permute-start(bf16[2048,128]{1,0:T(8,128)(2,1)S(1)} %collective-permute-done.refs_1_.refs_9_), channel_id=1, source_target_pairs={{0,1},{1,0},{2,3},{3,2},{4,5},{5,4},{6,7},{7,6},{8,9},{9,8},{10,11... | collective-permute-start | bytes 1572872 | tf_op jit(solution)/shard_map/ppermute | solution.py:121
  108.1 19.8 %collective-permute-start.5 = (bf16[2048,128]{1,0:T(8,128)(2,1)S(1)}, bf16[2048,128]{1,0:T(8,128)(2,1)}, u32[]{:S(2)}, u32[]{:S(2)}) collective-permute-start(bf16[2048,128]{1,0:T(8,128)(2,1)S(1)} %collective-permute-done.2.refs_2_.refs_10_), channel_id=1, source_target_pairs={{0,1},{1,0},{2,3},{3,2},{4,5},{5,4},{6,7},{7,6},{8,9},{9,8},{10,11... | collective-permute-start | bytes 1572872 | tf_op jit(solution)/shard_map/ppermute | solution.py:121
  111.0 12.8 %collective-permute-start.9 = (bf16[1024,128]{1,0:T(8,128)(2,1)S(1)}, bf16[1024,128]{1,0:T(8,128)(2,1)}, u32[]{:S(2)}, u32[]{:S(2)}) collective-permute-start(bf16[1024,128]{1,0:T(8,128)(2,1)S(1)} %broadcast_select_fusion.1), channel_id=1, source_target_pairs={{0,2},{1,7},{2,4},{3,1},{4,6},{5,3},{6,0},{7,5},{8,10},{9,15},{10,... | collective-permute-start | bytes 786440 | tf_op jit(solution)/shard_map/ppermute | solution.py:128
  115.9 18.6 %collective-permute-start.10 = (bf16[1024,128]{1,0:T(8,128)(2,1)}, bf16[1024,128]{1,0:T(8,128)(2,1)}, u32[]{:S(2)}, u32[]{:S(2)}) collective-permute-start(bf16[1024,128]{1,0:T(8,128)(2,1)} %shard_map.93.refs_0_), channel_id=1, source_target_pairs={{0,1},{1,0},{2,3},{3,2},{4,5},{5,4},{6,7},{7,6},{8,9},{9,8},{10,11... | collective-permute-start | bytes 786440 | tf_op jit(solution)/shard_map/ppermute | solution.py:121
  117.9 0.8 copy-start.1
  118.7 15.8 %collective-permute-start.13 = (bf16[1024,128]{1,0:T(8,128)(2,1)}, bf16[1024,128]{1,0:T(8,128)(2,1)}, u32[]{:S(2)}, u32[]{:S(2)}) collective-permute-start(bf16[1024,128]{1,0:T(8,128)(2,1)} %collective-permute-done.8.refs_3_), channel_id=1, source_target_pairs={{0,1},{1,0},{2,3},{3,2},{4,5},{5,4},{6,7},{7,6},{8,9},{9,8},{10,11... | collective-permute-start | bytes 786440 | tf_op jit(solution)/shard_map/ppermute | solution.py:121
  121.1 0.8 copy-start.4
  121.9 12.6 %collective-permute-start.11 = (bf16[1024,128]{1,0:T(8,128)(2,1)}, bf16[1024,128]{1,0:T(8,128)(2,1)}, u32[]{:S(2)}, u32[]{:S(2)}) collective-permute-start(bf16[1024,128]{1,0:T(8,128)(2,1)} %collective-permute-done.7.refs_1_), channel_id=1, source_target_pairs={{0,1},{1,0},{2,3},{3,2},{4,5},{5,4},{6,7},{7,6},{8,9},{9,8},{10,11... | collective-permute-start | bytes 786440 | tf_op jit(solution)/shard_map/ppermute | solution.py:121
  123.8 10.7 %collective-permute-start.12 = (bf16[1024,128]{1,0:T(8,128)(2,1)}, bf16[1024,128]{1,0:T(8,128)(2,1)}, u32[]{:S(2)}, u32[]{:S(2)}) collective-permute-start(bf16[1024,128]{1,0:T(8,128)(2,1)} %collective-permute-done.9.refs_2_), channel_id=1, source_target_pairs={{0,1},{1,0},{2,3},{3,2},{4,5},{5,4},{6,7},{7,6},{8,9},{9,8},{10,11... | collective-permute-start | bytes 786440 | tf_op jit(solution)/shard_map/ppermute | solution.py:121
  127.9 1.0 copy-start.2
  129.0 1.0 copy-start.5
  130.0 1.0 copy-start.6
  131.1 3.5 %copy-start.3 = (bf16[2048,128]{1,0:T(8,128)(2,1)S(1)}, bf16[2048,128]{1,0:T(8,128)(2,1)}, u32[]{:S(2)}) copy-start(bf16[2048,128]{1,0:T(8,128)(2,1)} %copy-done.1) | copy-start | bytes 1572868

commit v2 on v1

v2 whole, which is shorter than its diff:
```python
import functools

import jax
import jax.numpy as jnp
from jax import lax
from jax.experimental import pallas as pl
from jax.experimental.pallas import tpu as pltpu
from jax.sharding import Mesh, PartitionSpec as P

EPS = 1e-06
LOSS_SCALE = 256.0
CAP = 2
LANES = 128
BF = jnp.bfloat16
F32 = jnp.float32
I32 = jnp.int32
VMEM = pl.BlockSpec(memory_space=pltpu.VMEM)
SMEM = pl.BlockSpec(memory_space=pltpu.SMEM)
ANY = pl.BlockSpec(memory_space=pl.ANY)
HBM = pl.BlockSpec(memory_space=pltpu.HBM)
PARAMS = pltpu.CompilerParams(vmem_limit_bytes=24 * 1024 * 1024)
SMALL = pltpu.CompilerParams(vmem_limit_bytes=16 * 1024 * 1024)
LARGE = pltpu.CompilerParams(vmem_limit_bytes=58 * 1024 * 1024)


def dot(a, b, left, right):
    return lax.dot_general(a, b, (((left,), (right,)), ((), ())), preferred_element_type=F32)


def iota(shape, dim):
    return lax.broadcasted_iota(I32, shape, dim)


def as_column(row):
    return jnp.broadcast_to(row, (row.shape[1], row.shape[1])).T


def pack_kernel(owner, entry, labels, info):
    micro = owner.shape[0]
    lines = [
        [owner[m] for m in range(micro)],
        [entry[m:m + 1, :] for m in range(micro)],
        [labels[m:m + 1, :] for m in range(micro)],
    ]
    for k, line in enumerate(lines):
        line = jnp.concatenate(line, axis=1)
        info[0, k:k + 1, :] = line


def ask_kernel(micro, rows, owners, info, ask, slot):
    members = info.shape[0]
    pairs, slots = micro * rows, members * micro * CAP
    r, c = iota((pairs, pairs), 0), iota((pairs, pairs), 1)
    before = ((r < c) & ((r >= rows) == (c >= rows))).astype(F32).astype(BF)
    owner_id, slot_id = iota((owners, pairs), 0), iota((LANES, pairs), 0)
    half = (iota((1, pairs), 1) >= rows).astype(I32) * CAP
    total = jnp.zeros((owners, LANES), F32)
    for g in range(members):
        own, pos = info[g, 0:1, :], info[g, 1:2, :]
        hit = own == owner_id
        hits = hit.astype(F32)
        earlier = dot(hits.astype(BF), before, 1, 0)
        nth = jnp.sum(hits * earlier, axis=0, keepdims=True).astype(I32)
        place = g * micro * CAP + half + nth
        slot[g:g + 1, :] = own * slots + place
        put = jnp.where(place == slot_id, pos, 0).astype(F32).astype(BF)
        total = total + dot(hits.astype(BF), put, 1, 1)
    ask[...] = total.astype(BF)


def unsort_kernel(me, slot, fetched, mine):
    members, pairs = slot.shape
    count = fetched.shape[0]
    lane = iota((pairs, count), 1)
    for g in range(members):
        column = as_column(slot[g:g + 1, :])
        where = (lane == jnp.concatenate([column] * (count // pairs), axis=1)).astype(F32).astype(BF)
        start = pl.multiple_of((me[0] ^ g) * pairs, pairs)
        mine[pl.ds(start, pairs), :] = dot(where, fetched[...], 1, 0).astype(BF)


def load_columns(me, cores, pieces, whole, sems):
    chips, width = len(pieces) // cores, whole.shape[1] // len(pieces)
    x, core = me // cores, me % cores
    copies = []
    for k, piece in enumerate(pieces):
        member = (x + chips - k % chips) % chips * cores + (core ^ (k // chips))
        columns = pl.ds(pl.multiple_of(member * width, LANES), width)
        copies.append(pltpu.make_async_copy(piece, whole.at[:, columns], sems.at[k]))
    for copy in copies:
        copy.start()
    return copies


def text_kernel(members, cores, me, text, *refs):
    pieces, (unit, inverse, whole, wt, unit_buf, sems, out_sems) = refs[:members], refs[members:]
    for copy in load_columns(me[0], cores, pieces, wt, sems):
        copy.wait()
    wt_out = pltpu.make_async_copy(wt, whole, out_sems.at[0])
    wt_out.start()
    raw = dot(text[...], wt[...], 1, 0)
    inv = lax.rsqrt(jnp.sum(raw * raw, axis=1, keepdims=True) + EPS)
    unit_buf[...] = raw * inv
    unit_out = pltpu.make_async_copy(unit_buf, unit, out_sems.at[1])
    unit_out.start()
    inverse[...] = jnp.broadcast_to(inv, inverse.shape)
    wt_out.wait()
    unit_out.wait()


def grad_kernel(members, cores, rows, me, stretch, shift, info, inverse, unit_in, weights, *refs):
    images, (out, img, wt, unit, slopes, img_sems, sems) = refs[:members], refs[members:]
    unit_copy = pltpu.make_async_copy(unit_in, unit, sems.at[0])
    unit_copy.start()
    img_copies = load_columns(me[0], cores, images, img, img_sems)
    wt_copy = pltpu.make_async_copy(weights, wt, sems.at[1])
    wt_copy.start()
    gain, offset = stretch[0], shift[0]
    pairs = unit.shape[0]
    unit_copy.wait()
    text = unit[...].astype(BF)
    own_labels = info[0, 2:3, :]
    same_micro = (iota((pairs, pairs), 0) >= rows) == (iota((pairs, pairs), 1) >= rows)
    for copy in img_copies:
        copy.wait()
    for g in range(members):
        span = slice(g * pairs, (g + 1) * pairs)
        block = img[span, :]
        wide = block.astype(F32)
        inv = lax.rsqrt(jnp.sum(wide * wide, axis=1, keepdims=True) + EPS)
        logit = gain * inv * dot(block, text, 1, 1) + offset
        match = (as_column(info[me[0] ^ g, 2:3, :]) == own_labels).astype(F32)
        slope = LOSS_SCALE * inv * (jax.nn.sigmoid(logit) - match)
        slopes[span, :] = jnp.where(same_micro, slope, 0.0).astype(BF)
    grad = gain * dot(slopes[...], img[...], 0, 0)
    grad = grad - unit[...] * jnp.sum(unit[...] * grad, axis=1, keepdims=True)
    grad = (inverse[:, 0:1] * grad).astype(BF)
    wt_copy.wait()
    out[...] = dot(grad, wt[...], 1, 1).astype(BF)


def make_local(nz, ny, nx, nc):
    members, owners = nx * nc, nz * ny

    def swap(v):
        return lax.ppermute(v, "core", [(i, nc - 1 - i) for i in range(nc)])

    def double(v, axis, bit):
        size = lax.axis_size(axis)
        other = lax.ppermute(v, axis, [(i, i ^ (1 << bit)) for i in range(size)])
        return jnp.concatenate([v, other], axis=0)

    def shift(v, by):
        return lax.ppermute(v, "x", [(i, (i + by) % nx) for i in range(nx)])

    def turn(v):
        moves = [(i * nc + c, (i + 1 - 2 * c) % nx * nc + c) for i in range(nx) for c in range(nc)]
        return lax.ppermute(v, ("x", "core"), moves)

    def whole_group(v, core):
        up, down = shift(v, 1), shift(v, -1)
        twin = swap(v)
        far = turn(jnp.where(core == 0, up, down))
        return [v, up, far, down, twin, swap(up), swap(far), swap(down)]

    def local(text, cache, owner, entry, labels, wi, wt, stretch, offset):
        micro, rows, d_txt = text.shape
        d_img, emb = cache.shape[1], wi.shape[1]
        wi_rows, wt_rows = wi.shape[0], wt.shape[0]
        width = emb // members
        pairs = micro * rows
        slots = members * micro * CAP
        x, core = lax.axis_index("x"), lax.axis_index("core")
        me = x * nc + core

        wt_part = lax.dynamic_slice(wt, (0, me * width), (wt_rows, width))
        wt_part = jnp.broadcast_to(wt_part[None], (owners,) + wt_part.shape)
        wt_part = lax.all_to_all(wt_part, ("z", "y"), split_axis=0, concat_axis=0, tiled=True)
        wt_part = wt_part.reshape(owners * wt_rows, width)
        info = pl.pallas_call(
            pack_kernel,
            out_shape=jax.ShapeDtypeStruct((1, 3, pairs), I32),
            in_specs=[VMEM, VMEM, VMEM],
            out_specs=VMEM,
            compiler_params=LARGE,
        )(owner.transpose(0, 2, 1), entry, labels)
        info = double(double(double(info, "core", 0), "x", 0), "x", 1)
        info, wt_part = lax.optimization_barrier((info, wt_part))
        wt_pieces = whole_group(wt_part, core)
        ask, slot = pl.pallas_call(
            functools.partial(ask_kernel, micro, rows, owners),
            out_shape=(
                jax.ShapeDtypeStruct((owners, LANES), BF),
                jax.ShapeDtypeStruct((members, pairs), I32),
            ),
            in_specs=[VMEM],
            out_specs=(VMEM, VMEM),
            compiler_params=SMALL,
        )(info)

        wi_pad = -(-(wi_rows + 1) // 8) * 8
        wi_part = lax.dynamic_slice(wi, (0, me * width), (wi_rows, width))
        sent = jnp.concatenate(
            [
                jnp.broadcast_to(wi_part[None], (owners,) + wi_part.shape),
                ask[:, None, :],
                jnp.zeros((owners, wi_pad - wi_rows - 1, width), BF),
            ],
            axis=1,
        )
        got = lax.all_to_all(sent, ("z", "y"), split_axis=0, concat_axis=0, tiled=True)

        old, new = iota((d_img, owners * wi_pad), 0), iota((d_img, owners * wi_pad), 1)
        spread = (old // wi_rows * wi_pad + old % wi_rows == new).astype(BF)
        cache_pad = dot(cache, spread, 1, 0).astype(BF)
        wi_all = got.reshape(owners * wi_pad, width)
        table = dot(cache_pad, wi_all, 1, 0).astype(BF)
        asked = got[:, wi_rows, :slots].astype(I32).reshape(-1)
        pick = (asked[:, None] == jnp.arange(cache.shape[0], dtype=I32)).astype(BF)
        served = dot(pick, table, 1, 0).astype(BF).reshape(owners, slots, width)
        fetched = lax.all_to_all(served, ("z", "y"), split_axis=0, concat_axis=0, tiled=True)
        unit, inverse, wt_whole = pl.pallas_call(
            functools.partial(text_kernel, members, nc),
            out_shape=(
                jax.ShapeDtypeStruct((pairs, emb), F32),
                jax.ShapeDtypeStruct((pairs, LANES), F32),
                jax.ShapeDtypeStruct((d_txt, emb), BF),
            ),
            in_specs=[SMEM, VMEM] + [ANY] * members,
            out_specs=(HBM, VMEM, HBM),
            scratch_shapes=[
                pltpu.VMEM((d_txt, emb), BF),
                pltpu.VMEM((pairs, emb), F32),
                pltpu.SemaphoreType.DMA((members,)),
                pltpu.SemaphoreType.DMA((2,)),
            ],
            compiler_params=PARAMS,
            cost_estimate=pl.CostEstimate(
                flops=2 * pairs * d_txt * emb, bytes_accessed=4 * d_txt * emb, transcendentals=0
            ),
        )(me.reshape(1), text.reshape(pairs, d_txt), *wt_pieces)
        fetched, unit, inverse, wt_whole = lax.optimization_barrier((fetched, unit, inverse, wt_whole))
        mine = pl.pallas_call(
            unsort_kernel,
            out_shape=jax.ShapeDtypeStruct((members * pairs, width), BF),
            in_specs=[SMEM, VMEM, VMEM],
            out_specs=VMEM,
            compiler_params=SMALL,
        )(me.reshape(1), slot, fetched.reshape(owners * slots, width))

        image_pieces = whole_group(mine, core)
        out = pl.pallas_call(
            functools.partial(grad_kernel, members, nc, rows),
            out_shape=jax.ShapeDtypeStruct((pairs, d_txt), BF),
            in_specs=[SMEM, SMEM, SMEM, VMEM, VMEM, HBM, HBM] + [ANY] * members,
            out_specs=VMEM,
            scratch_shapes=[
                pltpu.VMEM((members * pairs, emb), BF),
                pltpu.VMEM((d_txt, emb), BF),
                pltpu.VMEM((pairs, emb), F32),
                pltpu.VMEM((members * pairs, pairs), BF),
                pltpu.SemaphoreType.DMA((members,)),
                pltpu.SemaphoreType.DMA((2,)),
            ],
            compiler_params=LARGE,
            cost_estimate=pl.CostEstimate(
                flops=2 * pairs * d_txt * emb, bytes_accessed=2 * d_txt * emb, transcendentals=0
            ),
        )(me.reshape(1), stretch, offset, info, inverse, unit, wt_whole, *image_pieces)
        return out.reshape(micro, rows, d_txt)

    return local


def solution(mesh):
    nz, ny, nx, nc = 8, 8, 4, 2
    fine = Mesh(mesh.devices.reshape(nz, ny, nx, nc), ("z", "y", "x", "core"))
    dp, every = ("z", "y"), ("z", "y", "x", "core")
    return jax.shard_map(
        make_local(nz, ny, nx, nc),
        mesh=fine,
        in_specs=(
            P(None, every, None),
            P(dp, None),
            P(None, every, None),
            P(None, every),
            P(None, every),
            P(dp, None),
            P(dp, None),
            P(),
            P(),
        ),
        out_specs=P(None, every, None),
        check_vma=False,
    )
```

time: 142 us -> 136 us (0.958)
  waiting for transfers between devices: 36.2 us -> 16.3 us
  starting transfers between devices: 71.1 us -> 86.9 us
  local copies, waits for them, and re-layouts: 9.4 us -> 7.53 us
    all_to_all x1, waiting for transfers between devices: 21.2 us -> 6.03 us  [local(): lax.all_to_all(sent, ('z', 'y'), split_axis=0, concat_axis=0, tiled=True)]
    all_to_all x1, waiting for transfers between devices: 10.9 us -> 0.01 us  [local(): lax.all_to_all(served, ('z', 'y'), split_axis=0, concat_axis=0, tiled=True)]
    ppermute x0 -> x3, starting transfers between devices: none -> 10.6 us  [double(): other = lax.ppermute(v, axis, [(i, i ^ 1 << bit) for i in range(size)])]
    all_to_all x1, starting transfers between devices: 10.1 us -> 17.1 us  [local(): lax.all_to_all(wt_part, ('z', 'y'), split_axis=0, concat_axis=0, tiled=True)]
    ppermute x4, waiting for transfers between devices: 0.9 us -> 4.93 us  [shift(): return lax.ppermute(v, 'x', [(i, (i + by) % nx) for i in range(nx)])]
    ppermute x0 -> x3, waiting for transfers between devices: none -> 3.24 us  [double(): other = lax.ppermute(v, axis, [(i, i ^ 1 << bit) for i in range(size)])]
    all_to_all x1, waiting for transfers between devices: 3.19 us -> 0.01 us  [local(): lax.all_to_all(wt_part, ('z', 'y'), split_axis=0, concat_axis=0, tiled=True)]
    ppermute x8, waiting for transfers between devices: 0.02 us -> 2.09 us  [swap(): return lax.ppermute(v, 'core', [(i, nc - 1 - i) for i in range(nc)])]
  transfers between devices with their start and end apart: 17 -> 20, of which waited for: 4 -> 7; matrix products, arithmetic and copies ran while one was open for 6% -> 8% of each run, Pallas kernels for 4% -> 3%
where the time goes in v2:
time: 136 us; the launch traced here: 135 us
  starting transfers between devices  86.9 us (64%)
  waiting for transfers between devices  16.3 us (12%)
  Pallas kernels  12.3 us (9%)
  local copies, waits for them, and re-layouts  7.53 us (6%)
  matrix products  6.4 us (5%)
  other arithmetic  3.89 us (3%)
  between operations  1.84 us (1%)
    ppermute x8, starting transfers between devices, swap(): return lax.ppermute(v, 'core', [(i, nc - 1 - i) for i in range(nc)])  20.2 us
    all_to_all x1, starting transfers between devices, local(): lax.all_to_all(wt_part, ('z', 'y'), split_axis=0, concat_axis=0, tiled=True)  17.1 us
    ppermute x4, starting transfers between devices, shift(): return lax.ppermute(v, 'x', [(i, (i + by) % nx) for i in range(nx)])  13 us
    all_to_all x1, starting transfers between devices, local(): lax.all_to_all(sent, ('z', 'y'), split_axis=0, concat_axis=0, tiled=True)  12.1 us
    ppermute x3, starting transfers between devices, double(): other = lax.ppermute(v, axis, [(i, i ^ 1 << bit) for i in range(size)])  10.6 us
    ppermute x2, starting transfers between devices, turn(): return lax.ppermute(v, ('x', 'core'), moves)  7.74 us
    dot_general x3, matrix products, dot(): lax.dot_general(a, b, (((left,), (right,)), ((), ())), preferred_element_...  6.4 us
    pallas_call x1, Pallas kernels, local(): pl.pallas_call(functools.partial(grad_kernel, members, nc, rows), out_sha...  6.35 us
  transfers between devices with their start and end apart: 20, of which 7 were waited for; matrix products, arithmetic and copies ran while one was open for 8% of the time, Pallas kernels for 3%

profile of v2, /device:TPU:1, one launch (start us, length us, event | category | flops | bytes accessed | tf_op | source)
XLA Modules:
  0.0 135.2 jit_solution(9134408561831314906)
XLA Ops:
  0.0 0.8 constant_dynamic-slice_fusion.1
  0.8 0.9 broadcast_in_dim.8
  1.6 17.1 %all-to-all-start = ((bf16[64,32,128]{2,1,0:T(8,128)(2,1)}), bf16[64,32,128]{2,1,0:T(8,128)(2,1)S(1)}, u32[]{:S(2)}, u32[]{:S(2)}) async-start(bf16[64,32,128]{2,1,0:T(8,128)(2,1)} %broadcast_in_dim.8), calls=%async_computation | async-start | bytes 1048576 | tf_op jit(solution)/shard_map/all_to_all | solution.py:178
  18.8 1.3 shard_map.91
  20.1 2.9 %collective-permute-start = (s32[1,3,128]{2,1,0:T(4,128)}, s32[1,3,128]{2,1,0:T(4,128)S(1)}, u32[]{:S(2)}, u32[]{:S(2)}) collective-permute-start(s32[1,3,128]{2,1,0:T(4,128)} %shard_map.91), channel_id=1, source_target_pairs={{0,1},{1,0},{2,3},{3,2},{4,5},{5,4},{6,7},{7,6},{8,9},{9,8},{10,11... | collective-permute-start | bytes 4616 | tf_op jit(solution)/shard_map/ppermute | solution.py:150
  23.0 1.0 collective-permute-done
  24.0 0.6 pad_add_fusion.2
  24.6 3.1 %collective-permute-start.1 = (s32[2,3,128]{2,1,0:T(4,128)S(1)}, s32[2,3,128]{2,1,0:T(4,128)S(1)}, u32[]{:S(2)}, u32[]{:S(2)}) collective-permute-start(s32[2,3,128]{2,1,0:T(4,128)S(1)} %pad_add_fusion.2), channel_id=1, source_target_pairs={{0,2},{2,0},{4,6},{6,4},{1,3},{3,1},{5,7},{7,5},{8,10},{10,8},{12,... | collective-permute-start | bytes 9224 | tf_op jit(solution)/shard_map/ppermute | solution.py:150
  27.7 0.7 constant_dynamic-slice_fusion
  28.4 0.8 collective-permute-done.1
  29.2 0.6 pad_add_fusion.1
  29.9 4.6 %collective-permute-start.2 = (s32[4,3,128]{2,1,0:T(4,128)S(1)}, s32[4,3,128]{2,1,0:T(4,128)S(1)}, u32[]{:S(2)}, u32[]{:S(2)}) collective-permute-start(s32[4,3,128]{2,1,0:T(4,128)S(1)} %pad_add_fusion.1), channel_id=1, source_target_pairs={{0,4},{2,6},{4,0},{6,2},{1,5},{3,7},{5,1},{7,3},{8,12},{10,14},{12... | collective-permute-start | bytes 18440 | tf_op jit(solution)/shard_map/ppermute | solution.py:150
  34.5 0.1 pad.2.clone
  34.6 1.4 %collective-permute-done.2 = s32[4,3,128]{2,1,0:T(4,128)S(1)} collective-permute-done((s32[4,3,128]{2,1,0:T(4,128)S(1)}, s32[4,3,128]{2,1,0:T(4,128)S(1)}, u32[]{:S(2)}, u32[]{:S(2)}) %collective-permute-start.2) | collective-permute-done | bytes 6176 | tf_op jit(solution)/shard_map/ppermute | solution.py:150
  36.1 0.6 pad_add_fusion.info
  36.7 0.0 all-to-all-done
  36.7 3.1 %collective-permute-start.3 = (bf16[2048,128]{1,0:T(8,128)(2,1)S(1)}, bf16[2048,128]{1,0:T(8,128)(2,1)S(1)}, u32[]{:S(2)}, u32[]{:S(2)}) collective-permute-start(bf16[2048,128]{1,0:T(8,128)(2,1)S(1)} %bitcast.20), channel_id=1, source_target_pairs={{0,2},{2,4},{4,6},{6,0},{1,3},{3,5},{5,7},{7,1},{8,10},{10,12},{12... | collective-permute-start | bytes 1572872 | tf_op jit(solution)/shard_map/ppermute | solution.py:154
  39.8 3.4 %collective-permute-start.4 = (bf16[2048,128]{1,0:T(8,128)(2,1)S(1)}, bf16[2048,128]{1,0:T(8,128)(2,1)S(1)}, u32[]{:S(2)}, u32[]{:S(2)}) collective-permute-start(bf16[2048,128]{1,0:T(8,128)(2,1)S(1)} %bitcast.21), channel_id=1, source_target_pairs={{0,6},{2,0},{4,2},{6,4},{1,7},{3,1},{5,3},{7,5},{8,14},{10,8},{12,... | collective-permute-start | bytes 1572872 | tf_op jit(solution)/shard_map/ppermute | solution.py:154
  43.2 0.7 shard_map.92
  43.9 0.1 copy.14
  44.0 0.1 broadcast_in_dim.9
  44.0 1.0 maximum_maximum_fusion
  45.0 12.1 %all-to-all-start.1 = ((bf16[64,24,128]{2,1,0:T(8,128)(2,1)}), bf16[64,24,128]{2,1,0:T(8,128)(2,1)S(1)}, u32[]{:S(2)}, u32[]{:S(2)}) async-start(bf16[64,24,128]{2,1,0:T(8,128)(2,1)} %maximum_maximum_fusion), calls=%async_computation.1 | async-start | bytes 786432 | tf_op jit(solution)/shard_map/all_to_all | solution.py:211
  57.1 3.5 %fusion.5.clone.6 = bf16[1536,256]{1,0:T(8,128)(2,1)} fusion(bf16[256,1408]{1,0:T(8,128)(2,1)S(1)} %copy-done, s32[1408]{0:T(1024)S(1)} %get-tuple-element.28, s32[1408]{0:T(1024)S(1)} %get-tuple-element.29, s32[1408]{0:T(1024)S(1)} %get-tuple-element.27, s32[1408]{0:T(1024)S(1)} %get-tuple-element.30, ...), kind=kOutput, calls=%fused_computation.5.clone.clone.clone.clone.clone.1 | convolution fusion | flops 1120665600 | bytes 1532672 | tf_op jit(solution)/shard_map/dot_general | solution.py:27
  60.6 0.0 collective-permute-done.3.refs_1_
  60.6 0.0 collective-permute-done.4.refs_3_
  60.7 0.9 broadcast_select_fusion
  61.5 3.2 %collective-permute-start.5 = (bf16[2048,128]{1,0:T(8,128)(2,1)}, bf16[2048,128]{1,0:T(8,128)(2,1)}, u32[]{:S(2)}, u32[]{:S(2)}) collective-permute-start(bf16[2048,128]{1,0:T(8,128)(2,1)} %broadcast_select_fusion), channel_id=1, source_target_pairs={{0,2},{1,7},{2,4},{3,1},{4,6},{5,3},{6,0},{7,5},{8,10},{9,15},{10,... | collective-permute-start | bytes 1572872 | tf_op jit(solution)/shard_map/ppermute | solution.py:158
  64.7 6.0 %all-to-all-done.1 = bf16[64,24,128]{2,1,0:T(8,128)(2,1)S(1)} async-done(((bf16[64,24,128]{2,1,0:T(8,128)(2,1)}), bf16[64,24,128]{2,1,0:T(8,128)(2,1)S(1)}, u32[]{:S(2)}, u32[]{:S(2)}) %all-to-all-start.1) | async-done | bytes 393248 | tf_op jit(solution)/shard_map/all_to_all | solution.py:211
  70.7 0.1 fusion.15
  70.8 0.1 reshape.39
  70.9 1.5 %fusion.11 = bf16[256,128]{1,0:T(8,128)(2,1)S(1)} fusion(bf16[1536,128]{1,0:T(8,128)(2,1)S(1)} %bitcast.27, bf16[1536,256]{1,0:T(8,128)(2,1)} %fusion.5.clone.6), kind=kOutput, calls=%fused_computation.9 | convolution fusion | flops 100696064 | bytes 1245184 | tf_op jit(solution)/shard_map/dot_general | solution.py:27
  72.5 1.3 convolution_convert_fusion
  73.8 6.1 %all-to-all-start.2 = ((bf16[64,32,128]{2,1,0:T(8,128)(2,1)}), bf16[64,32,128]{2,1,0:T(8,128)(2,1)S(1)}, u32[]{:S(2)}, u32[]{:S(2)}) async-start(bf16[64,32,128]{2,1,0:T(8,128)(2,1)} %bitcast.28), calls=%async_computation.2 | async-start | bytes 1048576 | tf_op jit(solution)/shard_map/all_to_all | solution.py:221
  79.9 5.1 %collective-permute-start.6 = (bf16[2048,128]{1,0:T(8,128)(2,1)S(1)}, bf16[2048,128]{1,0:T(8,128)(2,1)S(1)}, u32[]{:S(2)}, u32[]{:S(2)}) collective-permute-start(bf16[2048,128]{1,0:T(8,128)(2,1)S(1)} %bitcast.22), channel_id=1, source_target_pairs={{0,1},{1,0},{2,3},{3,2},{4,5},{5,4},{6,7},{7,6},{8,9},{9,8},{10,11... | collective-permute-start | bytes 1572872 | tf_op jit(solution)/shard_map/ppermute | solution.py:146
  85.0 1.9 %collective-permute-start.7 = (bf16[2048,128]{1,0:T(8,128)(2,1)S(1)}, bf16[2048,128]{1,0:T(8,128)(2,1)S(1)}, u32[]{:S(2)}, u32[]{:S(2)}) collective-permute-start(bf16[2048,128]{1,0:T(8,128)(2,1)S(1)} %collective-permute-done.3.refs_1_), channel_id=1, source_target_pairs={{0,1},{1,0},{2,3},{3,2},{4,5},{5,4},{6,7},{7,6},{8,9},{9,8},{10,11... | collective-permute-start | bytes 1572872 | tf_op jit(solution)/shard_map/ppermute | solution.py:146
  87.0 2.4 %collective-permute-start.9 = (bf16[2048,128]{1,0:T(8,128)(2,1)S(1)}, bf16[2048,128]{1,0:T(8,128)(2,1)S(1)}, u32[]{:S(2)}, u32[]{:S(2)}) collective-permute-start(bf16[2048,128]{1,0:T(8,128)(2,1)S(1)} %collective-permute-done.4.refs_3_), channel_id=1, source_target_pairs={{0,1},{1,0},{2,3},{3,2},{4,5},{5,4},{6,7},{7,6},{8,9},{9,8},{10,11... | collective-permute-start | bytes 1572872 | tf_op jit(solution)/shard_map/ppermute | solution.py:146
  89.4 1.9 %collective-permute-start.8 = (bf16[2048,128]{1,0:T(8,128)(2,1)}, bf16[2048,128]{1,0:T(8,128)(2,1)S(1)}, u32[]{:S(2)}, u32[]{:S(2)}) collective-permute-start(bf16[2048,128]{1,0:T(8,128)(2,1)} %collective-permute-done.5.refs_2_), channel_id=1, source_target_pairs={{0,1},{1,0},{2,3},{3,2},{4,5},{5,4},{6,7},{7,6},{8,9},{9,8},{10,11... | collective-permute-start | bytes 1572872 | tf_op jit(solution)/shard_map/ppermute | solution.py:146
  91.3 0.0 collective-permute-done.7.refs_5_
  91.4 2.1 %collective-permute-done.8.refs_6_ = bf16[2048,128]{1,0:T(8,128)(2,1)S(1)} collective-permute-done((bf16[2048,128]{1,0:T(8,128)(2,1)}, bf16[2048,128]{1,0:T(8,128)(2,1)S(1)}, u32[]{:S(2)}, u32[]{:S(2)}) %collective-permute-start.8) | collective-permute-done | bytes 524320 | tf_op jit(solution)/shard_map/ppermute | solution.py:146
  93.4 2.6 %shard_map.93 = (f32[128,1024]{1,0:T(8,128)S(1)}, f32[128,128]{1,0:T(8,128)S(1)}, bf16[2048,1024]{1,0:T(8,128)(2,1)S(1)}) custom-call(s32[1]{0:T(128)} %bitcast.me, bf16[128,2048]{1,0:T(8,128)(2,1)S(1)} %bitcast.25, bf16[2048,128]{1,0:T(8,128)(2,1)S(1)} %bitcast.23, bf16[2048,128]{1,0:T(8,128)(2,1)S(1)} %collective-permute-done.3.refs_1_, ...), custom_call_target="tpu_custom_call" | custom-call | flops 536870912 | bytes 8388608 | tf_op jit(solution)/shard_map/pallas_call | solution.py:222
  96.0 2.0 %copy-done.1 = bf16[2048,1024]{1,0:T(8,128)(2,1)} copy-done((bf16[2048,1024]{1,0:T(8,128)(2,1)}, bf16[2048,1024]{1,0:T(8,128)(2,1)S(1)}, u32[]{:S(2)}) %copy-start.1) | copy-done | bytes 4194328
  98.0 0.8 copy-done.4
  98.8 0.6 copy-done.6
  99.4 0.0 all-to-all-done.2
  99.4 1.3 shard_map.94.refs_0_
  100.8 2.7 %collective-permute-start.10 = (bf16[1024,128]{1,0:T(8,128)(2,1)S(1)}, bf16[1024,128]{1,0:T(8,128)(2,1)S(1)}, u32[]{:S(2)}, u32[]{:S(2)}) collective-permute-start(bf16[1024,128]{1,0:T(8,128)(2,1)S(1)} %shard_map.94.refs_0_), channel_id=1, source_target_pairs={{0,2},{2,4},{4,6},{6,0},{1,3},{3,5},{5,7},{7,1},{8,10},{10,12},{12... | collective-permute-start | bytes 786440 | tf_op jit(solution)/shard_map/ppermute | solution.py:154
  103.4 3.8 %collective-permute-start.11 = (bf16[1024,128]{1,0:T(8,128)(2,1)S(1)}, bf16[1024,128]{1,0:T(8,128)(2,1)S(1)}, u32[]{:S(2)}, u32[]{:S(2)}) collective-permute-start(bf16[1024,128]{1,0:T(8,128)(2,1)S(1)} %shard_map.94.refs_0_), channel_id=1, source_target_pairs={{0,6},{2,0},{4,2},{6,4},{1,7},{3,1},{5,3},{7,5},{8,14},{10,8},{12,... | collective-permute-start | bytes 786440 | tf_op jit(solution)/shard_map/ppermute | solution.py:154
  107.3 3.3 %collective-permute-done.10.refs_1_ = bf16[1024,128]{1,0:T(8,128)(2,1)S(1)} collective-permute-done((bf16[1024,128]{1,0:T(8,128)(2,1)S(1)}, bf16[1024,128]{1,0:T(8,128)(2,1)S(1)}, u32[]{:S(2)}, u32[]{:S(2)}) %collective-permute-start.10) | collective-permute-done | bytes 262176 | tf_op jit(solution)/shard_map/ppermute | solution.py:154
  110.6 1.6 %collective-permute-done.11.refs_3_ = bf16[1024,128]{1,0:T(8,128)(2,1)S(1)} collective-permute-done((bf16[1024,128]{1,0:T(8,128)(2,1)S(1)}, bf16[1024,128]{1,0:T(8,128)(2,1)S(1)}, u32[]{:S(2)}, u32[]{:S(2)}) %collective-permute-start.11) | collective-permute-done | bytes 262176 | tf_op jit(solution)/shard_map/ppermute | solution.py:154
  112.3 4.6 %collective-permute-start.12 = (bf16[1024,128]{1,0:T(8,128)(2,1)S(1)}, bf16[1024,128]{1,0:T(8,128)(2,1)S(1)}, u32[]{:S(2)}, u32[]{:S(2)}) collective-permute-start(bf16[1024,128]{1,0:T(8,128)(2,1)S(1)} %broadcast_select_fusion.1), channel_id=1, source_target_pairs={{0,2},{1,7},{2,4},{3,1},{4,6},{5,3},{6,0},{7,5},{8,10},{9,15},{10,... | collective-permute-start | bytes 786440 | tf_op jit(solution)/shard_map/ppermute | solution.py:158
  116.8 2.3 %collective-permute-start.13 = (bf16[1024,128]{1,0:T(8,128)(2,1)S(1)}, bf16[1024,128]{1,0:T(8,128)(2,1)S(1)}, u32[]{:S(2)}, u32[]{:S(2)}) collective-permute-start(bf16[1024,128]{1,0:T(8,128)(2,1)S(1)} %shard_map.94.refs_0_), channel_id=1, source_target_pairs={{0,1},{1,0},{2,3},{3,2},{4,5},{5,4},{6,7},{7,6},{8,9},{9,8},{10,11... | collective-permute-start | bytes 786440 | tf_op jit(solution)/shard_map/ppermute | solution.py:146
  119.1 2.1 %collective-permute-start.14 = (bf16[1024,128]{1,0:T(8,128)(2,1)S(1)}, bf16[1024,128]{1,0:T(8,128)(2,1)S(1)}, u32[]{:S(2)}, u32[]{:S(2)}) collective-permute-start(bf16[1024,128]{1,0:T(8,128)(2,1)S(1)} %collective-permute-done.10.refs_1_), channel_id=1, source_target_pairs={{0,1},{1,0},{2,3},{3,2},{4,5},{5,4},{6,7},{7,6},{8,9},{9,8},{10,11... | collective-permute-start | bytes 786440 | tf_op jit(solution)/shard_map/ppermute | solution.py:146
  121.2 2.5 %collective-permute-start.16 = (bf16[1024,128]{1,0:T(8,128)(2,1)S(1)}, bf16[1024,128]{1,0:T(8,128)(2,1)S(1)}, u32[]{:S(2)}, u32[]{:S(2)}) collective-permute-start(bf16[1024,128]{1,0:T(8,128)(2,1)S(1)} %collective-permute-done.11.refs_3_), channel_id=1, source_target_pairs={{0,1},{1,0},{2,3},{3,2},{4,5},{5,4},{6,7},{7,6},{8,9},{9,8},{10,11... | collective-permute-start | bytes 786440 | tf_op jit(solution)/shard_map/ppermute | solution.py:146
  123.6 0.0 collective-permute-done.12.refs_2_
  123.7 2.1 %collective-permute-start.15 = (bf16[1024,128]{1,0:T(8,128)(2,1)S(1)}, bf16[1024,128]{1,0:T(8,128)(2,1)S(1)}, u32[]{:S(2)}, u32[]{:S(2)}) collective-permute-start(bf16[1024,128]{1,0:T(8,128)(2,1)S(1)} %collective-permute-done.12.refs_2_), channel_id=1, source_target_pairs={{0,1},{1,0},{2,3},{3,2},{4,5},{5,4},{6,7},{7,6},{8,9},{9,8},{10,11... | collective-permute-start | bytes 786440 | tf_op jit(solution)/shard_map/ppermute | solution.py:146
  127.0 0.0 collective-permute-done.13.refs_4_
  127.0 0.0 collective-permute-done.14.refs_5_
  127.1 0.0 collective-permute-done.15.refs_6_
  127.1 0.6 copy-done.10
  127.7 0.1 copy-done.11
  127.8 0.1 copy-done.12
  128.0 0.7 copy-done.13
  128.7 6.4 %shard_map.95 = bf16[128,2048]{1,0:T(8,128)(2,1)} custom-call(s32[1]{0:T(128)} %bitcast.me, f32[1]{0:T(128)S(6)} %copy.15.stretch, f32[1]{0:T(128)S(6)} %copy.16.shift, s32[8,3,128]{2,1,0:T(4,128)} %copy-done.5, f32[128,128]{1,0:T(8,128)} %copy-done.6, f32[128,1024]{1,0:T(8,128)} %copy-done.4, bf16[2048,1024]{1,0:T(8,128)(2,1)} %copy-done.1, ...), custom_call_target="tpu_custom_call" | custom-call | flops 536870912 | bytes 4194304 | tf_op jit(solution)/shard_map/pallas_call | solution.py:252
  (29 shorter events, 0.1 us)
Async XLA Ops:
  0.0 57.1 %copy-start = (bf16[256,1408]{1,0:T(8,128)(2,1)S(1)}, bf16[256,1408]{1,0:T(8,128)(2,1)}, u32[]{:S(2)}) copy-start(bf16[256,1408]{1,0:T(8,128)(2,1)} %param.10) | copy-start | bytes 2162692
  1.6 35.1 %all-to-all-start = ((bf16[64,32,128]{2,1,0:T(8,128)(2,1)}), bf16[64,32,128]{2,1,0:T(8,128)(2,1)S(1)}, u32[]{:S(2)}, u32[]{:S(2)}) async-start(bf16[64,32,128]{2,1,0:T(8,128)(2,1)} %broadcast_in_dim.8), calls=%async_computation | async-start | bytes 1048576 | tf_op jit(solution)/shard_map/all_to_all | solution.py:178
  20.1 3.9 %collective-permute-start = (s32[1,3,128]{2,1,0:T(4,128)}, s32[1,3,128]{2,1,0:T(4,128)S(1)}, u32[]{:S(2)}, u32[]{:S(2)}) collective-permute-start(s32[1,3,128]{2,1,0:T(4,128)} %shard_map.91), channel_id=1, source_target_pairs={{0,1},{1,0},{2,3},{3,2},{4,5},{5,4},{6,7},{7,6},{8,9},{9,8},{10,11... | collective-permute-start | bytes 4616 | tf_op jit(solution)/shard_map/ppermute | solution.py:150
  24.6 4.6 %collective-permute-start.1 = (s32[2,3,128]{2,1,0:T(4,128)S(1)}, s32[2,3,128]{2,1,0:T(4,128)S(1)}, u32[]{:S(2)}, u32[]{:S(2)}) collective-permute-start(s32[2,3,128]{2,1,0:T(4,128)S(1)} %pad_add_fusion.2), channel_id=1, source_target_pairs={{0,2},{2,0},{4,6},{6,4},{1,3},{3,1},{5,7},{7,5},{8,10},{10,8},{12,... | collective-permute-start | bytes 9224 | tf_op jit(solution)/shard_map/ppermute | solution.py:150
  29.9 6.2 %collective-permute-start.2 = (s32[4,3,128]{2,1,0:T(4,128)S(1)}, s32[4,3,128]{2,1,0:T(4,128)S(1)}, u32[]{:S(2)}, u32[]{:S(2)}) collective-permute-start(s32[4,3,128]{2,1,0:T(4,128)S(1)} %pad_add_fusion.1), channel_id=1, source_target_pairs={{0,4},{2,6},{4,0},{6,2},{1,5},{3,7},{5,1},{7,3},{8,12},{10,14},{12... | collective-permute-start | bytes 18440 | tf_op jit(solution)/shard_map/ppermute | solution.py:150
  36.7 23.9 %copy-start.5 = (s32[8,3,128]{2,1,0:T(4,128)}, s32[8,3,128]{2,1,0:T(4,128)S(1)}, u32[]{:S(2)}) copy-start(s32[8,3,128]{2,1,0:T(4,128)S(1)} %pad_add_fusion.info) | copy-start | bytes 36868
  36.7 23.9 %collective-permute-start.3 = (bf16[2048,128]{1,0:T(8,128)(2,1)S(1)}, bf16[2048,128]{1,0:T(8,128)(2,1)S(1)}, u32[]{:S(2)}, u32[]{:S(2)}) collective-permute-start(bf16[2048,128]{1,0:T(8,128)(2,1)S(1)} %bitcast.20), channel_id=1, source_target_pairs={{0,2},{2,4},{4,6},{6,0},{1,3},{3,5},{5,7},{7,1},{8,10},{10,12},{12... | collective-permute-start | bytes 1572872 | tf_op jit(solution)/shard_map/ppermute | solution.py:154
  39.8 20.8 %collective-permute-start.4 = (bf16[2048,128]{1,0:T(8,128)(2,1)S(1)}, bf16[2048,128]{1,0:T(8,128)(2,1)S(1)}, u32[]{:S(2)}, u32[]{:S(2)}) collective-permute-start(bf16[2048,128]{1,0:T(8,128)(2,1)S(1)} %bitcast.21), channel_id=1, source_target_pairs={{0,6},{2,0},{4,2},{6,4},{1,7},{3,1},{5,3},{7,5},{8,14},{10,8},{12,... | collective-permute-start | bytes 1572872 | tf_op jit(solution)/shard_map/ppermute | solution.py:154
  45.0 25.7 %all-to-all-start.1 = ((bf16[64,24,128]{2,1,0:T(8,128)(2,1)}), bf16[64,24,128]{2,1,0:T(8,128)(2,1)S(1)}, u32[]{:S(2)}, u32[]{:S(2)}) async-start(bf16[64,24,128]{2,1,0:T(8,128)(2,1)} %maximum_maximum_fusion), calls=%async_computation.1 | async-start | bytes 786432 | tf_op jit(solution)/shard_map/all_to_all | solution.py:211
  60.6 32.8 %copy-start.3 = (bf16[2,64,2048]{2,1,0:T(8,128)(2,1)S(1)}, bf16[2,64,2048]{2,1,0:T(8,128)(2,1)}, u32[]{:S(2)}) copy-start(bf16[2,64,2048]{2,1,0:T(8,128)(2,1)} %param.9) | copy-start | bytes 1572868
  61.5 27.9 %collective-permute-start.5 = (bf16[2048,128]{1,0:T(8,128)(2,1)}, bf16[2048,128]{1,0:T(8,128)(2,1)}, u32[]{:S(2)}, u32[]{:S(2)}) collective-permute-start(bf16[2048,128]{1,0:T(8,128)(2,1)} %broadcast_select_fusion), channel_id=1, source_target_pairs={{0,2},{1,7},{2,4},{3,1},{4,6},{5,3},{6,0},{7,5},{8,10},{9,15},{10,... | collective-permute-start | bytes 1572872 | tf_op jit(solution)/shard_map/ppermute | solution.py:158
  73.8 25.7 %all-to-all-start.2 = ((bf16[64,32,128]{2,1,0:T(8,128)(2,1)}), bf16[64,32,128]{2,1,0:T(8,128)(2,1)S(1)}, u32[]{:S(2)}, u32[]{:S(2)}) async-start(bf16[64,32,128]{2,1,0:T(8,128)(2,1)} %bitcast.28), calls=%async_computation.2 | async-start | bytes 1048576 | tf_op jit(solution)/shard_map/all_to_all | solution.py:221
  79.9 11.4 %collective-permute-start.6 = (bf16[2048,128]{1,0:T(8,128)(2,1)S(1)}, bf16[2048,128]{1,0:T(8,128)(2,1)S(1)}, u32[]{:S(2)}, u32[]{:S(2)}) collective-permute-start(bf16[2048,128]{1,0:T(8,128)(2,1)S(1)} %bitcast.22), channel_id=1, source_target_pairs={{0,1},{1,0},{2,3},{3,2},{4,5},{5,4},{6,7},{7,6},{8,9},{9,8},{10,11... | collective-permute-start | bytes 1572872 | tf_op jit(solution)/shard_map/ppermute | solution.py:146
  85.0 6.3 %collective-permute-start.7 = (bf16[2048,128]{1,0:T(8,128)(2,1)S(1)}, bf16[2048,128]{1,0:T(8,128)(2,1)S(1)}, u32[]{:S(2)}, u32[]{:S(2)}) collective-permute-start(bf16[2048,128]{1,0:T(8,128)(2,1)S(1)} %collective-permute-done.3.refs_1_), channel_id=1, source_target_pairs={{0,1},{1,0},{2,3},{3,2},{4,5},{5,4},{6,7},{7,6},{8,9},{9,8},{10,11... | collective-permute-start | bytes 1572872 | tf_op jit(solution)/shard_map/ppermute | solution.py:146
  87.0 4.4 %collective-permute-start.9 = (bf16[2048,128]{1,0:T(8,128)(2,1)S(1)}, bf16[2048,128]{1,0:T(8,128)(2,1)S(1)}, u32[]{:S(2)}, u32[]{:S(2)}) collective-permute-start(bf16[2048,128]{1,0:T(8,128)(2,1)S(1)} %collective-permute-done.4.refs_3_), channel_id=1, source_target_pairs={{0,1},{1,0},{2,3},{3,2},{4,5},{5,4},{6,7},{7,6},{8,9},{9,8},{10,11... | collective-permute-start | bytes 1572872 | tf_op jit(solution)/shard_map/ppermute | solution.py:146
  89.4 4.0 %collective-permute-start.8 = (bf16[2048,128]{1,0:T(8,128)(2,1)}, bf16[2048,128]{1,0:T(8,128)(2,1)S(1)}, u32[]{:S(2)}, u32[]{:S(2)}) collective-permute-start(bf16[2048,128]{1,0:T(8,128)(2,1)} %collective-permute-done.5.refs_2_), channel_id=1, source_target_pairs={{0,1},{1,0},{2,3},{3,2},{4,5},{5,4},{6,7},{7,6},{8,9},{9,8},{10,11... | collective-permute-start | bytes 1572872 | tf_op jit(solution)/shard_map/ppermute | solution.py:146
  96.0 2.0 %copy-start.1 = (bf16[2048,1024]{1,0:T(8,128)(2,1)}, bf16[2048,1024]{1,0:T(8,128)(2,1)S(1)}, u32[]{:S(2)}) copy-start(bf16[2048,1024]{1,0:T(8,128)(2,1)S(1)} %get-tuple-element.24.weights) | copy-start | bytes 12582916
  98.0 0.8 copy-start.4
  98.8 0.6 copy-start.6
  100.8 26.3 %copy-start.2 = (bf16[1024,128]{1,0:T(8,128)(2,1)}, bf16[1024,128]{1,0:T(8,128)(2,1)S(1)}, u32[]{:S(2)}) copy-start(bf16[1024,128]{1,0:T(8,128)(2,1)S(1)} %shard_map.94.refs_0_) | copy-start | bytes 786436
  100.8 9.8 %collective-permute-start.10 = (bf16[1024,128]{1,0:T(8,128)(2,1)S(1)}, bf16[1024,128]{1,0:T(8,128)(2,1)S(1)}, u32[]{:S(2)}, u32[]{:S(2)}) collective-permute-start(bf16[1024,128]{1,0:T(8,128)(2,1)S(1)} %shard_map.94.refs_0_), channel_id=1, source_target_pairs={{0,2},{2,4},{4,6},{6,0},{1,3},{3,5},{5,7},{7,1},{8,10},{10,12},{12... | collective-permute-start | bytes 786440 | tf_op jit(solution)/shard_map/ppermute | solution.py:154
  103.4 8.8 %collective-permute-start.11 = (bf16[1024,128]{1,0:T(8,128)(2,1)S(1)}, bf16[1024,128]{1,0:T(8,128)(2,1)S(1)}, u32[]{:S(2)}, u32[]{:S(2)}) collective-permute-start(bf16[1024,128]{1,0:T(8,128)(2,1)S(1)} %shard_map.94.refs_0_), channel_id=1, source_target_pairs={{0,6},{2,0},{4,2},{6,4},{1,7},{3,1},{5,3},{7,5},{8,14},{10,8},{12,... | collective-permute-start | bytes 786440 | tf_op jit(solution)/shard_map/ppermute | solution.py:154
  110.6 16.5 %copy-start.7 = (bf16[1024,128]{1,0:T(8,128)(2,1)}, bf16[1024,128]{1,0:T(8,128)(2,1)S(1)}, u32[]{:S(2)}) copy-start(bf16[1024,128]{1,0:T(8,128)(2,1)S(1)} %collective-permute-done.10.refs_1_) | copy-start | bytes 786436
  112.2 14.9 %copy-start.8 = (bf16[1024,128]{1,0:T(8,128)(2,1)}, bf16[1024,128]{1,0:T(8,128)(2,1)S(1)}, u32[]{:S(2)}) copy-start(bf16[1024,128]{1,0:T(8,128)(2,1)S(1)} %collective-permute-done.11.refs_3_) | copy-start | bytes 786436
  112.3 11.4 %collective-permute-start.12 = (bf16[1024,128]{1,0:T(8,128)(2,1)S(1)}, bf16[1024,128]{1,0:T(8,128)(2,1)S(1)}, u32[]{:S(2)}, u32[]{:S(2)}) collective-permute-start(bf16[1024,128]{1,0:T(8,128)(2,1)S(1)} %broadcast_select_fusion.1), channel_id=1, source_target_pairs={{0,2},{1,7},{2,4},{3,1},{4,6},{5,3},{6,0},{7,5},{8,10},{9,15},{10,... | collective-permute-start | bytes 786440 | tf_op jit(solution)/shard_map/ppermute | solution.py:158
  116.8 10.2 %collective-permute-start.13 = (bf16[1024,128]{1,0:T(8,128)(2,1)S(1)}, bf16[1024,128]{1,0:T(8,128)(2,1)S(1)}, u32[]{:S(2)}, u32[]{:S(2)}) collective-permute-start(bf16[1024,128]{1,0:T(8,128)(2,1)S(1)} %shard_map.94.refs_0_), channel_id=1, source_target_pairs={{0,1},{1,0},{2,3},{3,2},{4,5},{5,4},{6,7},{7,6},{8,9},{9,8},{10,11... | collective-permute-start | bytes 786440 | tf_op jit(solution)/shard_map/ppermute | solution.py:146
  119.1 7.9 %collective-permute-start.14 = (bf16[1024,128]{1,0:T(8,128)(2,1)S(1)}, bf16[1024,128]{1,0:T(8,128)(2,1)S(1)}, u32[]{:S(2)}, u32[]{:S(2)}) collective-permute-start(bf16[1024,128]{1,0:T(8,128)(2,1)S(1)} %collective-permute-done.10.refs_1_), channel_id=1, source_target_pairs={{0,1},{1,0},{2,3},{3,2},{4,5},{5,4},{6,7},{7,6},{8,9},{9,8},{10,11... | collective-permute-start | bytes 786440 | tf_op jit(solution)/shard_map/ppermute | solution.py:146
  121.2 5.9 %collective-permute-start.16 = (bf16[1024,128]{1,0:T(8,128)(2,1)S(1)}, bf16[1024,128]{1,0:T(8,128)(2,1)S(1)}, u32[]{:S(2)}, u32[]{:S(2)}) collective-permute-start(bf16[1024,128]{1,0:T(8,128)(2,1)S(1)} %collective-permute-done.11.refs_3_), channel_id=1, source_target_pairs={{0,1},{1,0},{2,3},{3,2},{4,5},{5,4},{6,7},{7,6},{8,9},{9,8},{10,11... | collective-permute-start | bytes 786440 | tf_op jit(solution)/shard_map/ppermute | solution.py:146
  123.7 3.5 %copy-start.9 = (bf16[1024,128]{1,0:T(8,128)(2,1)}, bf16[1024,128]{1,0:T(8,128)(2,1)S(1)}, u32[]{:S(2)}) copy-start(bf16[1024,128]{1,0:T(8,128)(2,1)S(1)} %collective-permute-done.12.refs_2_) | copy-start | bytes 786436
  123.7 3.4 %collective-permute-start.15 = (bf16[1024,128]{1,0:T(8,128)(2,1)S(1)}, bf16[1024,128]{1,0:T(8,128)(2,1)S(1)}, u32[]{:S(2)}, u32[]{:S(2)}) collective-permute-start(bf16[1024,128]{1,0:T(8,128)(2,1)S(1)} %collective-permute-done.12.refs_2_), channel_id=1, source_target_pairs={{0,1},{1,0},{2,3},{3,2},{4,5},{5,4},{6,7},{7,6},{8,9},{9,8},{10,11... | collective-permute-start | bytes 786440 | tf_op jit(solution)/shard_map/ppermute | solution.py:146
  127.0 0.7 copy-start.10
  127.1 0.8 copy-start.11
  127.1 0.9 copy-start.12
  128.0 0.7 copy-start.13

commit v3 on v2

v3 whole, which is shorter than its diff:
```python
import functools

import jax
import jax.numpy as jnp
from jax import lax
from jax.experimental import pallas as pl
from jax.experimental.pallas import tpu as pltpu
from jax.sharding import Mesh, PartitionSpec as P

EPS = 1e-06
LOSS_SCALE = 256.0
CAP = 2
LANES = 128
BF = jnp.bfloat16
F32 = jnp.float32
I32 = jnp.int32
VMEM = pl.BlockSpec(memory_space=pltpu.VMEM)
SMEM = pl.BlockSpec(memory_space=pltpu.SMEM)
ANY = pl.BlockSpec(memory_space=pl.ANY)
SMALL = pltpu.CompilerParams(vmem_limit_bytes=16 * 1024 * 1024)
LARGE = pltpu.CompilerParams(vmem_limit_bytes=58 * 1024 * 1024)


def dot(a, b, left, right):
    return lax.dot_general(a, b, (((left,), (right,)), ((), ())), preferred_element_type=F32)


def iota(shape, dim):
    return lax.broadcasted_iota(I32, shape, dim)


def as_column(row):
    return jnp.broadcast_to(row, (row.shape[1], row.shape[1])).T


def pack_kernel(owner, entry, labels, info):
    micro = owner.shape[0]
    lines = [
        [owner[m] for m in range(micro)],
        [entry[m:m + 1, :] for m in range(micro)],
        [labels[m:m + 1, :] for m in range(micro)],
    ]
    for k, line in enumerate(lines):
        line = jnp.concatenate(line, axis=1)
        for g in range(info.shape[0]):
            info[g, k:k + 1, :] = line


def ask_kernel(micro, rows, owners, info, ask, slot):
    members = info.shape[0]
    pairs, slots = micro * rows, members * micro * CAP
    r, c = iota((pairs, pairs), 0), iota((pairs, pairs), 1)
    before = ((r < c) & ((r >= rows) == (c >= rows))).astype(F32).astype(BF)
    owner_id, slot_id = iota((owners, pairs), 0), iota((LANES, pairs), 0)
    half = (iota((1, pairs), 1) >= rows).astype(I32) * CAP
    total = jnp.zeros((owners, LANES), F32)
    for g in range(members):
        own, pos = info[g, 0:1, :], info[g, 1:2, :]
        hit = own == owner_id
        hits = hit.astype(F32)
        earlier = dot(hits.astype(BF), before, 1, 0)
        nth = jnp.sum(hits * earlier, axis=0, keepdims=True).astype(I32)
        place = g * micro * CAP + half + nth
        slot[g:g + 1, :] = own * slots + place
        put = jnp.where(place == slot_id, pos, 0).astype(F32).astype(BF)
        total = total + dot(hits.astype(BF), put, 1, 1)
    ask[...] = total.astype(BF)


def unsort_kernel(slot, fetched, mine):
    members, pairs = slot.shape
    count = fetched.shape[0]
    lane = iota((pairs, count), 1)
    for g in range(members):
        column = as_column(slot[g:g + 1, :])
        where = (lane == jnp.concatenate([column] * (count // pairs), axis=1)).astype(F32).astype(BF)
        mine[g * pairs:(g + 1) * pairs, :] = dot(where, fetched[...], 1, 0).astype(BF)


def load_columns(me, cores, pieces, whole, sems):
    chips, width = len(pieces) // cores, whole.shape[1] // len(pieces)
    x, core = me // cores, me % cores
    copies = []
    for k, piece in enumerate(pieces):
        member = (x + chips - k % chips) % chips * cores + (core ^ (k // chips))
        columns = pl.ds(pl.multiple_of(member * width, LANES), width)
        copies.append(pltpu.make_async_copy(piece, whole.at[:, columns], sems.at[k]))
    for copy in copies:
        copy.start()
    return copies


def grad_kernel(members, cores, rows, me, stretch, shift, info, text, weights, *refs):
    images, (out, img, wt, slopes, img_sems, wt_sems) = refs[:members], refs[members:]
    chunk = wt.shape[0] // wt_sems.shape[0]
    wt_copies = []
    for k in range(wt_sems.shape[0]):
        span = slice(k * chunk, (k + 1) * chunk)
        wt_copies.append(pltpu.make_async_copy(weights.at[span], wt.at[span], wt_sems.at[k]))
        wt_copies[k].start()
    img_copies = load_columns(me[0], cores, images, img, img_sems)
    gain, offset = stretch[0], shift[0]
    pairs = text.shape[0]
    own_labels = info[me[0], 2:3, :]
    same_micro = (iota((pairs, pairs), 0) >= rows) == (iota((pairs, pairs), 1) >= rows)
    raw = jnp.zeros((pairs, wt.shape[1]), F32)
    for k, copy in enumerate(wt_copies):
        copy.wait()
        span = slice(k * chunk, (k + 1) * chunk)
        raw = raw + dot(text[:, span], wt[span, :], 1, 0)
    inverse = lax.rsqrt(jnp.sum(raw * raw, axis=1, keepdims=True) + EPS)
    unit = raw * inverse
    unit_bf = unit.astype(BF)
    for copy in img_copies:
        copy.wait()
    for g in range(members):
        span = slice(g * pairs, (g + 1) * pairs)
        block = img[span, :]
        wide = block.astype(F32)
        inv = lax.rsqrt(jnp.sum(wide * wide, axis=1, keepdims=True) + EPS)
        logit = gain * inv * dot(block, unit_bf, 1, 1) + offset
        match = (as_column(info[g, 2:3, :]) == own_labels).astype(F32)
        slope = LOSS_SCALE * inv * (jax.nn.sigmoid(logit) - match)
        slopes[span, :] = jnp.where(same_micro, slope, 0.0).astype(BF)
    grad = gain * dot(slopes[...], img[...], 0, 0)
    grad = grad - unit * jnp.sum(unit * grad, axis=1, keepdims=True)
    grad = (inverse * grad).astype(BF)
    out[...] = dot(grad, wt[...], 1, 1).astype(BF)


def make_local(nz, ny, nx, nc):
    members, owners = nx * nc, nz * ny

    def swap(v):
        return lax.ppermute(v, "core", [(i, nc - 1 - i) for i in range(nc)])

    def shift(v, by):
        return lax.ppermute(v, "x", [(i, (i + by) % nx) for i in range(nx)])

    def turn(v):
        moves = [(i * nc + c, (i + 1 - 2 * c) % nx * nc + c) for i in range(nx) for c in range(nc)]
        return lax.ppermute(v, ("x", "core"), moves)

    def whole_group(v, core):
        up, down = shift(v, 1), shift(v, -1)
        twin = swap(v)
        up, down, twin = lax.optimization_barrier((up, down, twin))
        far = turn(jnp.where(core == 0, up, down))
        return [v, up, far, down, twin, swap(up), swap(far), swap(down)]

    def local(text, cache, owner, entry, labels, wi, wt, stretch, offset):
        micro, rows, d_txt = text.shape
        d_img, emb = cache.shape[1], wi.shape[1]
        wi_rows, wt_rows = wi.shape[0], wt.shape[0]
        width = emb // members
        pairs = micro * rows
        slots = members * micro * CAP
        x, core = lax.axis_index("x"), lax.axis_index("core")
        me = x * nc + core

        wt_all = lax.all_gather(wt, ("z", "y"), axis=0, tiled=True)

        info = pl.pallas_call(
            pack_kernel,
            out_shape=jax.ShapeDtypeStruct((members, 3, pairs), I32),
            in_specs=[VMEM, VMEM, VMEM],
            out_specs=VMEM,
            compiler_params=LARGE,
        )(owner.transpose(0, 2, 1), entry, labels)
        info = lax.all_to_all(info, ("x", "core"), split_axis=0, concat_axis=0, tiled=True)
        ask, slot = pl.pallas_call(
            functools.partial(ask_kernel, micro, rows, owners),
            out_shape=(
                jax.ShapeDtypeStruct((owners, LANES), BF),
                jax.ShapeDtypeStruct((members, pairs), I32),
            ),
            in_specs=[VMEM],
            out_specs=(VMEM, VMEM),
            compiler_params=SMALL,
        )(info)

        wi_pad = -(-(wi_rows + 1) // 8) * 8
        wi_part = lax.dynamic_slice(wi, (0, me * width), (wi_rows, width))
        sent = jnp.concatenate(
            [
                jnp.broadcast_to(wi_part[None], (owners,) + wi_part.shape),
                ask[:, None, :],
                jnp.zeros((owners, wi_pad - wi_rows - 1, width), BF),
            ],
            axis=1,
        )
        got = lax.all_to_all(sent, ("z", "y"), split_axis=0, concat_axis=0, tiled=True)

        old, new = iota((d_img, owners * wi_pad), 0), iota((d_img, owners * wi_pad), 1)
        spread = (old // wi_rows * wi_pad + old % wi_rows == new).astype(BF)
        cache_pad = dot(cache, spread, 1, 0).astype(BF)
        wi_all = got.reshape(owners * wi_pad, width)
        table = dot(cache_pad, wi_all, 1, 0).astype(BF)
        asked = got[:, wi_rows, :slots].astype(I32).reshape(-1)
        pick = (asked[:, None] == jnp.arange(cache.shape[0], dtype=I32)).astype(BF)
        served = dot(pick, table, 1, 0).astype(BF).reshape(owners, slots, width)
        fetched = lax.all_to_all(served, ("z", "y"), split_axis=0, concat_axis=0, tiled=True)
        mine = pl.pallas_call(
            unsort_kernel,
            out_shape=jax.ShapeDtypeStruct((members * pairs, width), BF),
            in_specs=[VMEM, VMEM],
            out_specs=VMEM,
            compiler_params=SMALL,
        )(slot, fetched.reshape(owners * slots, width))

        image_pieces = whole_group(mine, core)
        out = pl.pallas_call(
            functools.partial(grad_kernel, members, nc, rows),
            out_shape=jax.ShapeDtypeStruct((pairs, d_txt), BF),
            in_specs=[SMEM, SMEM, SMEM, VMEM, VMEM] + [ANY] * (members + 1),
            out_specs=VMEM,
            scratch_shapes=[
                pltpu.VMEM((members * pairs, emb), BF),
                pltpu.VMEM((d_txt, emb), BF),
                pltpu.VMEM((members * pairs, pairs), BF),
                pltpu.SemaphoreType.DMA((members,)),
                pltpu.SemaphoreType.DMA((4,)),
            ],
            compiler_params=LARGE,
            cost_estimate=pl.CostEstimate(
                flops=4 * pairs * d_txt * emb, bytes_accessed=2 * d_txt * emb, transcendentals=0
            ),
        )(me.reshape(1), stretch, offset, info, text.reshape(pairs, d_txt), wt_all, *image_pieces)
        return out.reshape(micro, rows, d_txt)

    return local


def solution(mesh):
    nz, ny, nx, nc = 8, 8, 4, 2
    fine = Mesh(mesh.devices.reshape(nz, ny, nx, nc), ("z", "y", "x", "core"))
    dp, every = ("z", "y"), ("z", "y", "x", "core")
    return jax.shard_map(
        make_local(nz, ny, nx, nc),
        mesh=fine,
        in_specs=(
            P(None, every, None),
            P(dp, None),
            P(None, every, None),
            P(None, every),
            P(None, every),
            P(dp, None),
            P(dp, None),
            P(),
            P(),
        ),
        out_specs=P(None, every, None),
        check_vma=False,
    )
```

time: 136 us -> 128 us (0.941)
  starting transfers between devices: 86.9 us -> 45.3 us
  blocking collectives: 0 us -> 23 us
  between operations: 1.84 us -> 15 us
  waiting for transfers between devices: 16.3 us -> 26.4 us
  local copies, waits for them, and re-layouts: 7.53 us -> 1.75 us
  matrix products: 6.4 us -> 3.55 us
  other arithmetic: 3.89 us -> 1.11 us
    all_to_all x0 -> x1, blocking collectives: none -> 23 us  [local(): lax.all_to_all(served, ('z', 'y'), split_axis=0, concat_axis=0, tiled=True)]
    all_to_all x2 -> x1, starting transfers between devices: 23.3 us -> 10.1 us  [local(): lax.all_to_all(info, ('x', 'core'), split_axis=0, concat_axis=0, tiled=True)]
    ppermute x3 -> x0, starting transfers between devices: 10.6 us -> none  [double(): other = lax.ppermute(v, axis, [(i, i ^ 1 << bit) for i in range(size)])]
    ppermute x4 -> x2, starting transfers between devices: 13 us -> 5.28 us  [shift(): return lax.ppermute(v, 'x', [(i, (i + by) % nx) for i in range(nx)])]
    all_to_all x1, waiting for transfers between devices: 6.03 us -> 12.3 us  [local(): lax.all_to_all(sent, ('z', 'y'), split_axis=0, concat_axis=0, tiled=True)]
    ppermute x2 -> x1, starting transfers between devices: 7.74 us -> 1.92 us  [turn(): return lax.ppermute(v, ('x', 'core'), moves)]
    ppermute x8 -> x4, starting transfers between devices: 20.2 us -> 16 us  [swap(): return lax.ppermute(v, 'core', [(i, nc - 1 - i) for i in range(nc)])]
    unnamed x28 -> x20, local copies, waits for them, and re-layouts: 4.95 us -> 0.79 us
  transfers between devices with their start and end apart: 20 -> 10, of which waited for: 7 -> 5; matrix products, arithmetic and copies ran while one was open for 8% -> 4% of each run, Pallas kernels for 3% -> 3%
where the time goes in v3:
time: 128 us; the launch traced here: 127 us
  starting transfers between devices  45.3 us (35%)
  waiting for transfers between devices  26.4 us (21%)
  blocking collectives  23 us (18%)
  between operations  15 us (12%)
  Pallas kernels  11.3 us (9%)
  matrix products  3.55 us (3%)
  local copies, waits for them, and re-layouts  1.75 us (1%)
    all_to_all x1, blocking collectives, local(): lax.all_to_all(served, ('z', 'y'), split_axis=0, concat_axis=0, tiled=True)  23 us
    ppermute x4, starting transfers between devices, swap(): return lax.ppermute(v, 'core', [(i, nc - 1 - i) for i in range(nc)])  16 us
    all_to_all x1, waiting for transfers between devices, local(): lax.all_to_all(sent, ('z', 'y'), split_axis=0, concat_axis=0, tiled=True)  12.3 us
    all_to_all x1, starting transfers between devices, local(): lax.all_to_all(sent, ('z', 'y'), split_axis=0, concat_axis=0, tiled=True)  12 us
    all_to_all x1, starting transfers between devices, local(): lax.all_to_all(info, ('x', 'core'), split_axis=0, concat_axis=0, tiled=True)  10.1 us
    ppermute x2, waiting for transfers between devices, shift(): return lax.ppermute(v, 'x', [(i, (i + by) % nx) for i in range(nx)])  8.68 us
    pallas_call x1, Pallas kernels, local(): pl.pallas_call(functools.partial(grad_kernel, members, nc, rows), out_sha...  7.93 us
    ppermute x2, starting transfers between devices, shift(): return lax.ppermute(v, 'x', [(i, (i + by) % nx) for i in range(nx)])  5.28 us
  transfers between devices with their start and end apart: 10, of which 5 were waited for; matrix products, arithmetic and copies ran while one was open for 4% of the time, Pallas kernels for 3%

profile of v3, /device:TPU:1, one launch (start us, length us, event | category | flops | bytes accessed | tf_op | source)
XLA Modules:
  0.0 127.4 jit_solution(8433449224471026179)
XLA Ops:
  6.5 0.0 copy-start
  6.5 0.0 all-gather.2.cloned.1.call-start
  6.5 0.7 all-gather.2.cloned.1.call-update
  7.3 1.4 %shard_map.91 = s32[8,3,128]{2,1,0:T(4,128)} custom-call(s32[2,1,64]{2,1,0:T(1,128)} %bitcast.24, s32[2,64]{1,0:T(2,128)} %entry.1, s32[2,64]{1,0:T(2,128)} %labels.1), custom_call_target="tpu_custom_call" | custom-call | tf_op jit(solution)/shard_map/pallas_call | solution.py:163
  8.7 10.1 %all-to-all-start = ((s32[8,3,128]{2,1,0:T(4,128)}), s32[8,3,128]{2,1,0:T(4,128)S(1)}, u32[]{:S(2)}, u32[]{:S(2)}) async-start(s32[8,3,128]{2,1,0:T(4,128)} %shard_map.91), calls=%async_computation | async-start | bytes 32768 | tf_op jit(solution)/shard_map/all_to_all | solution.py:170
  18.8 0.7 constant_dynamic-slice_fusion
  19.5 0.1 pad.2.clone
  19.6 3.9 %all-to-all-done.info = s32[8,3,128]{2,1,0:T(4,128)S(1)} async-done(((s32[8,3,128]{2,1,0:T(4,128)}), s32[8,3,128]{2,1,0:T(4,128)S(1)}, u32[]{:S(2)}, u32[]{:S(2)}) %all-to-all-start) | async-done | bytes 12320 | tf_op jit(solution)/shard_map/all_to_all | solution.py:170
  23.4 0.0 copy-start.2
  23.4 0.7 shard_map.92
  24.1 0.1 copy.14
  24.2 0.1 broadcast_in_dim.6
  24.2 0.9 maximum_maximum_fusion
  25.2 12.0 %all-to-all-start.1 = ((bf16[64,24,128]{2,1,0:T(8,128)(2,1)}), bf16[64,24,128]{2,1,0:T(8,128)(2,1)S(1)}, u32[]{:S(2)}, u32[]{:S(2)}) async-start(bf16[64,24,128]{2,1,0:T(8,128)(2,1)} %maximum_maximum_fusion), calls=%async_computation.1 | async-start | bytes 786432 | tf_op jit(solution)/shard_map/all_to_all | solution.py:192
  37.2 0.0 copy-done
  37.2 2.6 %fusion.5.clone.6 = bf16[1536,256]{1,0:T(8,128)(2,1)S(1)} fusion(bf16[256,1408]{1,0:T(8,128)(2,1)S(1)} %copy-done, s32[1408]{0:T(1024)S(1)} %get-tuple-element.16, s32[1408]{0:T(1024)S(1)} %get-tuple-element.17, s32[1408]{0:T(1024)S(1)} %get-tuple-element.15, s32[1408]{0:T(1024)S(1)} %get-tuple-element.18, ...), kind=kOutput, calls=%fused_computation.5.clone.clone.clone.clone.clone.1 | convolution fusion | flops 1120665600 | bytes 1532672 | tf_op jit(solution)/shard_map/dot_general | solution.py:25
  39.8 0.0 copy-done.2
  39.8 12.3 %all-to-all-done.1 = bf16[64,24,128]{2,1,0:T(8,128)(2,1)S(1)} async-done(((bf16[64,24,128]{2,1,0:T(8,128)(2,1)}), bf16[64,24,128]{2,1,0:T(8,128)(2,1)S(1)}, u32[]{:S(2)}, u32[]{:S(2)}) %all-to-all-start.1) | async-done | bytes 393248 | tf_op jit(solution)/shard_map/all_to_all | solution.py:192
  52.2 0.1 fusion.15
  52.3 0.1 reshape.32
  52.4 0.4 fusion.11
  52.8 0.5 convolution_convert_fusion
  53.3 23.0 %all_to_all.15 = bf16[64,32,128]{2,1,0:T(8,128)(2,1)S(1)} all-to-all(bf16[64,32,128]{2,1,0:T(8,128)(2,1)S(1)} %bitcast.22), channel_id=1, replica_groups=mesh['z'=8,'y'=8,'x'=4,'core'=2] {'z','y'}, dimensions={0} | all-to-all | bytes 1048576 | tf_op jit(solution)/shard_map/all_to_all | solution.py:202
  76.3 1.3 %shard_map.93.refs_0_ = bf16[1024,128]{1,0:T(8,128)(2,1)S(1)} custom-call(s32[8,128]{1,0:T(8,128)S(1)} %get-tuple-element.10.slot, bf16[2048,128]{1,0:T(8,128)(2,1)S(1)} %bitcast.19), custom_call_target="tpu_custom_call" | custom-call | tf_op jit(solution)/shard_map/pallas_call | solution.py:203
  77.7 0.0 copy-start.1
  77.7 6.3 %collective-permute-start.2 = (bf16[1024,128]{1,0:T(8,128)(2,1)S(1)}, bf16[1024,128]{1,0:T(8,128)(2,1)S(1)}, u32[]{:S(2)}, u32[]{:S(2)}) collective-permute-start(bf16[1024,128]{1,0:T(8,128)(2,1)S(1)} %shard_map.93.refs_0_), channel_id=1, source_target_pairs={{0,1},{1,0},{2,3},{3,2},{4,5},{5,4},{6,7},{7,6},{8,9},{9,8},{10,11... | collective-permute-start | bytes 786440 | tf_op jit(solution)/shard_map/ppermute | solution.py:135
  84.0 3.2 %collective-permute-start.1 = (bf16[1024,128]{1,0:T(8,128)(2,1)S(1)}, bf16[1024,128]{1,0:T(8,128)(2,1)S(1)}, u32[]{:S(2)}, u32[]{:S(2)}) collective-permute-start(bf16[1024,128]{1,0:T(8,128)(2,1)S(1)} %shard_map.93.refs_0_), channel_id=1, source_target_pairs={{0,6},{2,0},{4,2},{6,4},{1,7},{3,1},{5,3},{7,5},{8,14},{10,8},{12,... | collective-permute-start | bytes 786440 | tf_op jit(solution)/shard_map/ppermute | solution.py:138
  87.1 2.1 %collective-permute-start = (bf16[1024,128]{1,0:T(8,128)(2,1)S(1)}, bf16[1024,128]{1,0:T(8,128)(2,1)S(1)}, u32[]{:S(2)}, u32[]{:S(2)}) collective-permute-start(bf16[1024,128]{1,0:T(8,128)(2,1)S(1)} %shard_map.93.refs_0_), channel_id=1, source_target_pairs={{0,2},{2,4},{4,6},{6,0},{1,3},{3,5},{5,7},{7,1},{8,10},{10,12},{12... | collective-permute-start | bytes 786440 | tf_op jit(solution)/shard_map/ppermute | solution.py:138
  89.3 0.0 collective-permute-done.2.refs_4_
  89.3 0.0 copy-start.5
  89.3 4.6 %collective-permute-done.1.refs_3_ = bf16[1024,128]{1,0:T(8,128)(2,1)S(1)} collective-permute-done((bf16[1024,128]{1,0:T(8,128)(2,1)S(1)}, bf16[1024,128]{1,0:T(8,128)(2,1)S(1)}, u32[]{:S(2)}, u32[]{:S(2)}) %collective-permute-start.1) | collective-permute-done | bytes 262176 | tf_op jit(solution)/shard_map/ppermute | solution.py:138
  93.9 0.0 copy-start.3
  93.9 4.1 %collective-permute-done.refs_1_ = bf16[1024,128]{1,0:T(8,128)(2,1)S(1)} collective-permute-done((bf16[1024,128]{1,0:T(8,128)(2,1)S(1)}, bf16[1024,128]{1,0:T(8,128)(2,1)S(1)}, u32[]{:S(2)}, u32[]{:S(2)}) %collective-permute-start) | collective-permute-done | bytes 262176 | tf_op jit(solution)/shard_map/ppermute | solution.py:138
  98.0 0.0 copy-start.4
  98.0 1.9 %collective-permute-start.3 = (bf16[1024,128]{1,0:T(8,128)(2,1)S(1)}, bf16[1024,128]{1,0:T(8,128)(2,1)S(1)}, u32[]{:S(2)}, u32[]{:S(2)}) collective-permute-start(bf16[1024,128]{1,0:T(8,128)(2,1)S(1)} %broadcast_select_fusion), channel_id=1, source_target_pairs={{0,2},{1,7},{2,4},{3,1},{4,6},{5,3},{6,0},{7,5},{8,10},{9,15},{10,... | collective-permute-start | bytes 786440 | tf_op jit(solution)/shard_map/ppermute | solution.py:142
  99.9 2.9 %collective-permute-start.4 = (bf16[1024,128]{1,0:T(8,128)(2,1)S(1)}, bf16[1024,128]{1,0:T(8,128)(2,1)S(1)}, u32[]{:S(2)}, u32[]{:S(2)}) collective-permute-start(bf16[1024,128]{1,0:T(8,128)(2,1)S(1)} %collective-permute-done.refs_1_), channel_id=1, source_target_pairs={{0,1},{1,0},{2,3},{3,2},{4,5},{5,4},{6,7},{7,6},{8,9},{9,8},{10,11... | collective-permute-start | bytes 786440 | tf_op jit(solution)/shard_map/ppermute | solution.py:135
  102.9 1.9 %collective-permute-start.6 = (bf16[1024,128]{1,0:T(8,128)(2,1)S(1)}, bf16[1024,128]{1,0:T(8,128)(2,1)S(1)}, u32[]{:S(2)}, u32[]{:S(2)}) collective-permute-start(bf16[1024,128]{1,0:T(8,128)(2,1)S(1)} %collective-permute-done.1.refs_3_), channel_id=1, source_target_pairs={{0,1},{1,0},{2,3},{3,2},{4,5},{5,4},{6,7},{7,6},{8,9},{9,8},{10,11... | collective-permute-start | bytes 786440 | tf_op jit(solution)/shard_map/ppermute | solution.py:135
  104.8 0.7 collective-permute-done.3.refs_2_
  105.5 0.0 copy-start.6
  105.5 4.9 %collective-permute-start.5 = (bf16[1024,128]{1,0:T(8,128)(2,1)S(1)}, bf16[1024,128]{1,0:T(8,128)(2,1)S(1)}, u32[]{:S(2)}, u32[]{:S(2)}) collective-permute-start(bf16[1024,128]{1,0:T(8,128)(2,1)S(1)} %collective-permute-done.3.refs_2_), channel_id=1, source_target_pairs={{0,1},{1,0},{2,3},{3,2},{4,5},{5,4},{6,7},{7,6},{8,9},{9,8},{10,11... | collective-permute-start | bytes 786440 | tf_op jit(solution)/shard_map/ppermute | solution.py:135
  111.7 0.0 collective-permute-done.4.refs_5_
  111.7 0.0 copy-start.7
  111.7 0.0 collective-permute-done.6.refs_7_
  111.7 0.0 copy-start.8
  111.7 0.0 collective-permute-done.5.refs_6_
  111.7 0.0 copy-start.9
  111.7 0.0 all-gather.2.cloned.1.call-done.weights
  111.8 0.0 copy-done.1
  111.8 0.0 copy-done.5
  111.8 0.0 copy-done.3
  111.8 0.0 copy-done.4
  111.8 0.0 copy-done.6
  111.8 0.6 copy-done.7
  112.4 0.1 copy-done.8
  112.5 0.1 copy-done.9
  112.6 7.9 %shard_map.94 = bf16[128,2048]{1,0:T(8,128)(2,1)} custom-call(s32[1]{0:T(128)} %bitcast.me, f32[1]{0:T(128)S(6)} %copy.15.stretch, f32[1]{0:T(128)S(6)} %copy.16.shift, s32[8,3,128]{2,1,0:T(4,128)} %copy-done.2, bf16[128,2048]{1,0:T(8,128)(2,1)} %bitcast.23, bf16[2048,1024]{1,0:T(8,128)(2,1)} %all-gather.2.cloned.1.call-done.weights, ...), custom_call_target="tpu_custom_call" | custom-call | flops 1073741824 | bytes 4194304 | tf_op jit(solution)/shard_map/pallas_call | solution.py:212
  (4 shorter events, 0.1 us)
Async XLA Ops:
  6.5 30.7 %copy-start = (bf16[256,1408]{1,0:T(8,128)(2,1)S(1)}, bf16[256,1408]{1,0:T(8,128)(2,1)}, u32[]{:S(2)}) copy-start(bf16[256,1408]{1,0:T(8,128)(2,1)} %param.10) | copy-start | bytes 2162692
  6.5 105.2 %all-gather.2.cloned.1.call-start = ((), (), s32[]{:S(2)}) async-start(), calls=%async_computation.3 | async-start | bytes 4259840 | tf_op jit(solution)/shard_map/all_gather | solution.py:161
  8.7 14.8 %all-to-all-start = ((s32[8,3,128]{2,1,0:T(4,128)}), s32[8,3,128]{2,1,0:T(4,128)S(1)}, u32[]{:S(2)}, u32[]{:S(2)}) async-start(s32[8,3,128]{2,1,0:T(4,128)} %shard_map.91), calls=%async_computation | async-start | bytes 32768 | tf_op jit(solution)/shard_map/all_to_all | solution.py:170
  23.4 16.4 %copy-start.2 = (s32[8,3,128]{2,1,0:T(4,128)}, s32[8,3,128]{2,1,0:T(4,128)S(1)}, u32[]{:S(2)}) copy-start(s32[8,3,128]{2,1,0:T(4,128)S(1)} %all-to-all-done.info) | copy-start | bytes 36868
  25.2 27.0 %all-to-all-start.1 = ((bf16[64,24,128]{2,1,0:T(8,128)(2,1)}), bf16[64,24,128]{2,1,0:T(8,128)(2,1)S(1)}, u32[]{:S(2)}, u32[]{:S(2)}) async-start(bf16[64,24,128]{2,1,0:T(8,128)(2,1)} %maximum_maximum_fusion), calls=%async_computation.1 | async-start | bytes 786432 | tf_op jit(solution)/shard_map/all_to_all | solution.py:192
  77.7 34.1 %copy-start.1 = (bf16[1024,128]{1,0:T(8,128)(2,1)}, bf16[1024,128]{1,0:T(8,128)(2,1)S(1)}, u32[]{:S(2)}) copy-start(bf16[1024,128]{1,0:T(8,128)(2,1)S(1)} %shard_map.93.refs_0_) | copy-start | bytes 786436
  77.7 11.6 %collective-permute-start.2 = (bf16[1024,128]{1,0:T(8,128)(2,1)S(1)}, bf16[1024,128]{1,0:T(8,128)(2,1)S(1)}, u32[]{:S(2)}, u32[]{:S(2)}) collective-permute-start(bf16[1024,128]{1,0:T(8,128)(2,1)S(1)} %shard_map.93.refs_0_), channel_id=1, source_target_pairs={{0,1},{1,0},{2,3},{3,2},{4,5},{5,4},{6,7},{7,6},{8,9},{9,8},{10,11... | collective-permute-start | bytes 786440 | tf_op jit(solution)/shard_map/ppermute | solution.py:135
  84.0 9.9 %collective-permute-start.1 = (bf16[1024,128]{1,0:T(8,128)(2,1)S(1)}, bf16[1024,128]{1,0:T(8,128)(2,1)S(1)}, u32[]{:S(2)}, u32[]{:S(2)}) collective-permute-start(bf16[1024,128]{1,0:T(8,128)(2,1)S(1)} %shard_map.93.refs_0_), channel_id=1, source_target_pairs={{0,6},{2,0},{4,2},{6,4},{1,7},{3,1},{5,3},{7,5},{8,14},{10,8},{12,... | collective-permute-start | bytes 786440 | tf_op jit(solution)/shard_map/ppermute | solution.py:138
  87.1 10.8 %collective-permute-start = (bf16[1024,128]{1,0:T(8,128)(2,1)S(1)}, bf16[1024,128]{1,0:T(8,128)(2,1)S(1)}, u32[]{:S(2)}, u32[]{:S(2)}) collective-permute-start(bf16[1024,128]{1,0:T(8,128)(2,1)S(1)} %shard_map.93.refs_0_), channel_id=1, source_target_pairs={{0,2},{2,4},{4,6},{6,0},{1,3},{3,5},{5,7},{7,1},{8,10},{10,12},{12... | collective-permute-start | bytes 786440 | tf_op jit(solution)/shard_map/ppermute | solution.py:138
  89.3 22.5 %copy-start.5 = (bf16[1024,128]{1,0:T(8,128)(2,1)}, bf16[1024,128]{1,0:T(8,128)(2,1)S(1)}, u32[]{:S(2)}) copy-start(bf16[1024,128]{1,0:T(8,128)(2,1)S(1)} %collective-permute-done.2.refs_4_) | copy-start | bytes 786436
  93.9 17.9 %copy-start.3 = (bf16[1024,128]{1,0:T(8,128)(2,1)}, bf16[1024,128]{1,0:T(8,128)(2,1)S(1)}, u32[]{:S(2)}) copy-start(bf16[1024,128]{1,0:T(8,128)(2,1)S(1)} %collective-permute-done.1.refs_3_) | copy-start | bytes 786436
  98.0 13.8 %copy-start.4 = (bf16[1024,128]{1,0:T(8,128)(2,1)}, bf16[1024,128]{1,0:T(8,128)(2,1)S(1)}, u32[]{:S(2)}) copy-start(bf16[1024,128]{1,0:T(8,128)(2,1)S(1)} %collective-permute-done.refs_1_) | copy-start | bytes 786436
  98.0 7.5 %collective-permute-start.3 = (bf16[1024,128]{1,0:T(8,128)(2,1)S(1)}, bf16[1024,128]{1,0:T(8,128)(2,1)S(1)}, u32[]{:S(2)}, u32[]{:S(2)}) collective-permute-start(bf16[1024,128]{1,0:T(8,128)(2,1)S(1)} %broadcast_select_fusion), channel_id=1, source_target_pairs={{0,2},{1,7},{2,4},{3,1},{4,6},{5,3},{6,0},{7,5},{8,10},{9,15},{10,... | collective-permute-start | bytes 786440 | tf_op jit(solution)/shard_map/ppermute | solution.py:142
  99.9 11.8 %collective-permute-start.4 = (bf16[1024,128]{1,0:T(8,128)(2,1)S(1)}, bf16[1024,128]{1,0:T(8,128)(2,1)S(1)}, u32[]{:S(2)}, u32[]{:S(2)}) collective-permute-start(bf16[1024,128]{1,0:T(8,128)(2,1)S(1)} %collective-permute-done.refs_1_), channel_id=1, source_target_pairs={{0,1},{1,0},{2,3},{3,2},{4,5},{5,4},{6,7},{7,6},{8,9},{9,8},{10,11... | collective-permute-start | bytes 786440 | tf_op jit(solution)/shard_map/ppermute | solution.py:135
  102.9 8.9 %collective-permute-start.6 = (bf16[1024,128]{1,0:T(8,128)(2,1)S(1)}, bf16[1024,128]{1,0:T(8,128)(2,1)S(1)}, u32[]{:S(2)}, u32[]{:S(2)}) collective-permute-start(bf16[1024,128]{1,0:T(8,128)(2,1)S(1)} %collective-permute-done.1.refs_3_), channel_id=1, source_target_pairs={{0,1},{1,0},{2,3},{3,2},{4,5},{5,4},{6,7},{7,6},{8,9},{9,8},{10,11... | collective-permute-start | bytes 786440 | tf_op jit(solution)/shard_map/ppermute | solution.py:135
  105.5 6.3 %copy-start.6 = (bf16[1024,128]{1,0:T(8,128)(2,1)}, bf16[1024,128]{1,0:T(8,128)(2,1)S(1)}, u32[]{:S(2)}) copy-start(bf16[1024,128]{1,0:T(8,128)(2,1)S(1)} %collective-permute-done.3.refs_2_) | copy-start | bytes 786436
  105.5 6.2 %collective-permute-start.5 = (bf16[1024,128]{1,0:T(8,128)(2,1)S(1)}, bf16[1024,128]{1,0:T(8,128)(2,1)S(1)}, u32[]{:S(2)}, u32[]{:S(2)}) collective-permute-start(bf16[1024,128]{1,0:T(8,128)(2,1)S(1)} %collective-permute-done.3.refs_2_), channel_id=1, source_target_pairs={{0,1},{1,0},{2,3},{3,2},{4,5},{5,4},{6,7},{7,6},{8,9},{9,8},{10,11... | collective-permute-start | bytes 786440 | tf_op jit(solution)/shard_map/ppermute | solution.py:135
  111.7 0.7 copy-start.7
  111.7 0.8 copy-start.8
  111.7 0.8 copy-start.9
Sparse Core Ops, SparseCore 0:
  10.4 91.9 all-gather.1

commit v4 on v3

--- a/solution.py
+++ b/solution.py
@@ -10,6 +10,7 @@
 EPS = 1e-06
 LOSS_SCALE = 256.0
 CAP = 2
+HOPS = (0, 2, 3, 1)
 LANES = 128
 BF = jnp.bfloat16
 F32 = jnp.float32
@@ -82,7 +83,7 @@
     x, core = me // cores, me % cores
     copies = []
     for k, piece in enumerate(pieces):
-        member = (x + chips - k % chips) % chips * cores + (core ^ (k // chips))
+        member = (x + chips - HOPS[k % chips]) % chips * cores + (core ^ (k // chips))
         columns = pl.ds(pl.multiple_of(member * width, LANES), width)
         copies.append(pltpu.make_async_copy(piece, whole.at[:, columns], sems.at[k]))
     for copy in copies:
@@ -91,18 +92,27 @@
 
 
 def grad_kernel(members, cores, rows, me, stretch, shift, info, text, weights, *refs):
-    images, (out, img, wt, slopes, img_sems, wt_sems) = refs[:members], refs[members:]
+    images, (out, img, wt, norms, matches, slopes, img_sems, wt_sems) = refs[:members], refs[members:]
+    img_copies = load_columns(me[0], cores, images, img, img_sems)
     chunk = wt.shape[0] // wt_sems.shape[0]
     wt_copies = []
     for k in range(wt_sems.shape[0]):
         span = slice(k * chunk, (k + 1) * chunk)
         wt_copies.append(pltpu.make_async_copy(weights.at[span], wt.at[span], wt_sems.at[k]))
         wt_copies[k].start()
-    img_copies = load_columns(me[0], cores, images, img, img_sems)
     gain, offset = stretch[0], shift[0]
     pairs = text.shape[0]
     own_labels = info[me[0], 2:3, :]
-    same_micro = (iota((pairs, pairs), 0) >= rows) == (iota((pairs, pairs), 1) >= rows)
+    for g in range(members):
+        span = slice(g * pairs, (g + 1) * pairs)
+        matches[span, :] = (as_column(info[g, 2:3, :]) == own_labels).astype(F32)
+    for copy in img_copies:
+        copy.wait()
+    for g in range(members):
+        span = slice(g * pairs, (g + 1) * pairs)
+        wide = img[span, :].astype(F32)
+        inv = lax.rsqrt(jnp.sum(wide * wide, axis=1, keepdims=True) + EPS)
+        norms[span, :] = jnp.broadcast_to(inv, (pairs, pairs))
     raw = jnp.zeros((pairs, wt.shape[1]), F32)
     for k, copy in enumerate(wt_copies):
         copy.wait()
@@ -110,17 +120,13 @@
         raw = raw + dot(text[:, span], wt[span, :], 1, 0)
     inverse = lax.rsqrt(jnp.sum(raw * raw, axis=1, keepdims=True) + EPS)
     unit = raw * inverse
-    unit_bf = unit.astype(BF)
-    for copy in img_copies:
-        copy.wait()
+    similar = dot(img[...], unit.astype(BF), 1, 1)
+    same_micro = (iota((pairs, pairs), 0) >= rows) == (iota((pairs, pairs), 1) >= rows)
     for g in range(members):
         span = slice(g * pairs, (g + 1) * pairs)
-        block = img[span, :]
-        wide = block.astype(F32)
-        inv = lax.rsqrt(jnp.sum(wide * wide, axis=1, keepdims=True) + EPS)
-        logit = gain * inv * dot(block, unit_bf, 1, 1) + offset
-        match = (as_column(info[g, 2:3, :]) == own_labels).astype(F32)
-        slope = LOSS_SCALE * inv * (jax.nn.sigmoid(logit) - match)
+        inv = norms[span, :]
+        logit = gain * inv * similar[span, :] + offset
+        slope = LOSS_SCALE * inv * (jax.nn.sigmoid(logit) - matches[span, :])
         slopes[span, :] = jnp.where(same_micro, slope, 0.0).astype(BF)
     grad = gain * dot(slopes[...], img[...], 0, 0)
     grad = grad - unit * jnp.sum(unit * grad, axis=1, keepdims=True)
@@ -137,16 +143,9 @@
     def shift(v, by):
         return lax.ppermute(v, "x", [(i, (i + by) % nx) for i in range(nx)])
 
-    def turn(v):
-        moves = [(i * nc + c, (i + 1 - 2 * c) % nx * nc + c) for i in range(nx) for c in range(nc)]
-        return lax.ppermute(v, ("x", "core"), moves)
-
-    def whole_group(v, core):
-        up, down = shift(v, 1), shift(v, -1)
-        twin = swap(v)
-        up, down, twin = lax.optimization_barrier((up, down, twin))
-        far = turn(jnp.where(core == 0, up, down))
-        return [v, up, far, down, twin, swap(up), swap(far), swap(down)]
+    def whole_group(v):
+        near = [v] + [shift(v, hop) for hop in HOPS[1:]]
+        return near + [swap(p) for p in near]
 
     def local(text, cache, owner, entry, labels, wi, wt, stretch, offset):
         micro, rows, d_txt = text.shape
@@ -208,7 +207,7 @@
             compiler_params=SMALL,
         )(slot, fetched.reshape(owners * slots, width))
 
-        image_pieces = whole_group(mine, core)
+        image_pieces = whole_group(mine)
         out = pl.pallas_call(
             functools.partial(grad_kernel, members, nc, rows),
             out_shape=jax.ShapeDtypeStruct((pairs, d_txt), BF),
@@ -217,6 +216,8 @@
             scratch_shapes=[
                 pltpu.VMEM((members * pairs, emb), BF),
                 pltpu.VMEM((d_txt, emb), BF),
+                pltpu.VMEM((members * pairs, pairs), F32),
+                pltpu.VMEM((members * pairs, pairs), F32),
                 pltpu.VMEM((members * pairs, pairs), BF),
                 pltpu.SemaphoreType.DMA((members,)),
                 pltpu.SemaphoreType.DMA((4,)),

time: 128 us -> 122 us (0.953); the launches traced: 127 us -> 120 us
  waiting for transfers between devices: 26.4 us -> 17 us
  Pallas kernels: 11.3 us -> 12.9 us
    ppermute x2 -> x3, waiting for transfers between devices: 8.68 us -> 0.01 us  [shift(): return lax.ppermute(v, 'x', [(i, (i + by) % nx) for i in range(nx)])]
    ppermute x2 -> x3, starting transfers between devices: 5.28 us -> 8.75 us  [shift(): return lax.ppermute(v, 'x', [(i, (i + by) % nx) for i in range(nx)])]
    ppermute x1 -> x0, starting transfers between devices: 1.92 us -> none  [turn(): return lax.ppermute(v, ('x', 'core'), moves)]
    pallas_call x1, Pallas kernels: 7.93 us -> 9.54 us  [local(): pl.pallas_call(functools.partial(grad_kernel, members, nc, rows), out_sha...]
    ppermute x4, starting transfers between devices: 16 us -> 14.4 us  [swap(): return lax.ppermute(v, 'core', [(i, nc - 1 - i) for i in range(nc)])]
  transfers between devices with their start and end apart: 10 -> 10, of which waited for: 5 -> 2; matrix products, arithmetic and copies ran while one was open for 4% -> 5% of each run, Pallas kernels for 3% -> 3%
where the time goes in v4:
time: 122 us; the launch traced here: 120 us
  starting transfers between devices  45.2 us (37%)
  blocking collectives  23.1 us (19%)
  waiting for transfers between devices  17 us (14%)
  between operations  15 us (12%)
  Pallas kernels  12.9 us (11%)
  matrix products  3.55 us (3%)
  local copies, waits for them, and re-layouts  1.84 us (2%)
    all_to_all x1, blocking collectives, local(): lax.all_to_all(served, ('z', 'y'), split_axis=0, concat_axis=0, tiled=True)  23.1 us
    ppermute x4, starting transfers between devices, swap(): return lax.ppermute(v, 'core', [(i, nc - 1 - i) for i in range(nc)])  14.4 us
    all_to_all x1, waiting for transfers between devices, local(): lax.all_to_all(sent, ('z', 'y'), split_axis=0, concat_axis=0, tiled=True)  12.3 us
    all_to_all x1, starting transfers between devices, local(): lax.all_to_all(sent, ('z', 'y'), split_axis=0, concat_axis=0, tiled=True)  12 us
    all_to_all x1, starting transfers between devices, local(): lax.all_to_all(info, ('x', 'core'), split_axis=0, concat_axis=0, tiled=True)  10.1 us
    pallas_call x1, Pallas kernels, local(): pl.pallas_call(functools.partial(grad_kernel, members, nc, rows), out_sha...  9.54 us
    ppermute x3, starting transfers between devices, shift(): return lax.ppermute(v, 'x', [(i, (i + by) % nx) for i in range(nx)])  8.75 us
    all_to_all x1, waiting for transfers between devices, local(): lax.all_to_all(info, ('x', 'core'), split_axis=0, concat_axis=0, tiled=True)  3.89 us
  transfers between devices with their start and end apart: 10, of which 2 were waited for; matrix products, arithmetic and copies ran while one was open for 5% of the time, Pallas kernels for 3%

profile of v4, /device:TPU:1, one launch (start us, length us, event | category | flops | bytes accessed | tf_op | source)
XLA Modules:
  0.0 119.7 jit_solution(12915566687333223133)
XLA Ops:
  6.5 0.0 copy-start
  6.5 0.0 all-gather.2.cloned.1.call-start
  6.5 0.7 all-gather.2.cloned.1.call-update
  7.3 1.4 %shard_map.91 = s32[8,3,128]{2,1,0:T(4,128)} custom-call(s32[2,1,64]{2,1,0:T(1,128)} %bitcast.24, s32[2,64]{1,0:T(2,128)} %entry.1, s32[2,64]{1,0:T(2,128)} %labels.1), custom_call_target="tpu_custom_call" | custom-call | tf_op jit(solution)/shard_map/pallas_call | solution.py:162
  8.7 10.1 %all-to-all-start = ((s32[8,3,128]{2,1,0:T(4,128)}), s32[8,3,128]{2,1,0:T(4,128)S(1)}, u32[]{:S(2)}, u32[]{:S(2)}) async-start(s32[8,3,128]{2,1,0:T(4,128)} %shard_map.91), calls=%async_computation | async-start | bytes 32768 | tf_op jit(solution)/shard_map/all_to_all | solution.py:169
  18.8 0.7 constant_dynamic-slice_fusion
  19.5 0.1 pad.2.clone
  19.6 3.9 %all-to-all-done.info = s32[8,3,128]{2,1,0:T(4,128)S(1)} async-done(((s32[8,3,128]{2,1,0:T(4,128)}), s32[8,3,128]{2,1,0:T(4,128)S(1)}, u32[]{:S(2)}, u32[]{:S(2)}) %all-to-all-start) | async-done | bytes 12320 | tf_op jit(solution)/shard_map/all_to_all | solution.py:169
  23.4 0.0 copy-start.2
  23.4 0.7 shard_map.92
  24.1 0.1 copy.14
  24.2 0.1 broadcast_in_dim.6
  24.2 0.9 maximum_maximum_fusion
  25.2 12.0 %all-to-all-start.1 = ((bf16[64,24,128]{2,1,0:T(8,128)(2,1)}), bf16[64,24,128]{2,1,0:T(8,128)(2,1)S(1)}, u32[]{:S(2)}, u32[]{:S(2)}) async-start(bf16[64,24,128]{2,1,0:T(8,128)(2,1)} %maximum_maximum_fusion), calls=%async_computation.1 | async-start | bytes 786432 | tf_op jit(solution)/shard_map/all_to_all | solution.py:191
  37.2 0.0 copy-done
  37.2 2.6 %fusion.5.clone.6 = bf16[1536,256]{1,0:T(8,128)(2,1)S(1)} fusion(bf16[256,1408]{1,0:T(8,128)(2,1)S(1)} %copy-done, s32[1408]{0:T(1024)S(1)} %get-tuple-element.10, s32[1408]{0:T(1024)S(1)} %get-tuple-element.11, s32[1408]{0:T(1024)S(1)} %get-tuple-element.9, s32[1408]{0:T(1024)S(1)} %get-tuple-element.12, ...), kind=kOutput, calls=%fused_computation.5.clone.clone.clone.clone.clone.1 | convolution fusion | flops 1120665600 | bytes 1532672 | tf_op jit(solution)/shard_map/dot_general | solution.py:26
  39.8 0.0 copy-done.2
  39.8 12.3 %all-to-all-done.1 = bf16[64,24,128]{2,1,0:T(8,128)(2,1)S(1)} async-done(((bf16[64,24,128]{2,1,0:T(8,128)(2,1)}), bf16[64,24,128]{2,1,0:T(8,128)(2,1)S(1)}, u32[]{:S(2)}, u32[]{:S(2)}) %all-to-all-start.1) | async-done | bytes 393248 | tf_op jit(solution)/shard_map/all_to_all | solution.py:191
  52.2 0.1 fusion.15
  52.3 0.1 reshape.32
  52.4 0.4 fusion.11
  52.8 0.5 convolution_convert_fusion
  53.3 23.1 %all_to_all.15 = bf16[64,32,128]{2,1,0:T(8,128)(2,1)S(1)} all-to-all(bf16[64,32,128]{2,1,0:T(8,128)(2,1)S(1)} %bitcast.22), channel_id=1, replica_groups=mesh['z'=8,'y'=8,'x'=4,'core'=2] {'z','y'}, dimensions={0} | all-to-all | bytes 1048576 | tf_op jit(solution)/shard_map/all_to_all | solution.py:201
  76.4 1.3 %shard_map.93.refs_0_ = bf16[1024,128]{1,0:T(8,128)(2,1)S(1)} custom-call(s32[8,128]{1,0:T(8,128)S(1)} %get-tuple-element.7.slot, bf16[2048,128]{1,0:T(8,128)(2,1)S(1)} %bitcast.19), custom_call_target="tpu_custom_call" | custom-call | tf_op jit(solution)/shard_map/pallas_call | solution.py:202
  77.7 0.0 copy-start.1
  77.7 1.9 %collective-permute-start.2 = (bf16[1024,128]{1,0:T(8,128)(2,1)S(1)}, bf16[1024,128]{1,0:T(8,128)(2,1)S(1)}, u32[]{:S(2)}, u32[]{:S(2)}) collective-permute-start(bf16[1024,128]{1,0:T(8,128)(2,1)S(1)} %shard_map.93.refs_0_), channel_id=1, source_target_pairs={{0,2},{2,4},{4,6},{6,0},{1,3},{3,5},{5,7},{7,1},{8,10},{10,12},{12... | collective-permute-start | bytes 786440 | tf_op jit(solution)/shard_map/ppermute | solution.py:144
  79.7 4.6 %collective-permute-start.1 = (bf16[1024,128]{1,0:T(8,128)(2,1)S(1)}, bf16[1024,128]{1,0:T(8,128)(2,1)S(1)}, u32[]{:S(2)}, u32[]{:S(2)}) collective-permute-start(bf16[1024,128]{1,0:T(8,128)(2,1)S(1)} %shard_map.93.refs_0_), channel_id=1, source_target_pairs={{0,6},{2,0},{4,2},{6,4},{1,7},{3,1},{5,3},{7,5},{8,14},{10,8},{12,... | collective-permute-start | bytes 786440 | tf_op jit(solution)/shard_map/ppermute | solution.py:144
  84.3 2.3 %collective-permute-start = (bf16[1024,128]{1,0:T(8,128)(2,1)S(1)}, bf16[1024,128]{1,0:T(8,128)(2,1)S(1)}, u32[]{:S(2)}, u32[]{:S(2)}) collective-permute-start(bf16[1024,128]{1,0:T(8,128)(2,1)S(1)} %shard_map.93.refs_0_), channel_id=1, source_target_pairs={{0,4},{2,6},{4,0},{6,2},{1,5},{3,7},{5,1},{7,3},{8,12},{10,14},{12... | collective-permute-start | bytes 786440 | tf_op jit(solution)/shard_map/ppermute | solution.py:144
  86.5 6.7 %collective-permute-start.3 = (bf16[1024,128]{1,0:T(8,128)(2,1)S(1)}, bf16[1024,128]{1,0:T(8,128)(2,1)S(1)}, u32[]{:S(2)}, u32[]{:S(2)}) collective-permute-start(bf16[1024,128]{1,0:T(8,128)(2,1)S(1)} %shard_map.93.refs_0_), channel_id=1, source_target_pairs={{0,1},{1,0},{2,3},{3,2},{4,5},{5,4},{6,7},{7,6},{8,9},{9,8},{10,11... | collective-permute-start | bytes 786440 | tf_op jit(solution)/shard_map/ppermute | solution.py:141
  93.2 0.0 collective-permute-done.2.refs_3_
  93.3 0.0 copy-start.3
  93.3 3.0 %collective-permute-start.6 = (bf16[1024,128]{1,0:T(8,128)(2,1)S(1)}, bf16[1024,128]{1,0:T(8,128)(2,1)S(1)}, u32[]{:S(2)}, u32[]{:S(2)}) collective-permute-start(bf16[1024,128]{1,0:T(8,128)(2,1)S(1)} %collective-permute-done.2.refs_3_), channel_id=1, source_target_pairs={{0,1},{1,0},{2,3},{3,2},{4,5},{5,4},{6,7},{7,6},{8,9},{9,8},{10,11... | collective-permute-start | bytes 786440 | tf_op jit(solution)/shard_map/ppermute | solution.py:141
  96.3 0.0 collective-permute-done.1.refs_2_
  96.3 0.0 copy-start.4
  96.3 2.5 %collective-permute-start.5 = (bf16[1024,128]{1,0:T(8,128)(2,1)S(1)}, bf16[1024,128]{1,0:T(8,128)(2,1)S(1)}, u32[]{:S(2)}, u32[]{:S(2)}) collective-permute-start(bf16[1024,128]{1,0:T(8,128)(2,1)S(1)} %collective-permute-done.1.refs_2_), channel_id=1, source_target_pairs={{0,1},{1,0},{2,3},{3,2},{4,5},{5,4},{6,7},{7,6},{8,9},{9,8},{10,11... | collective-permute-start | bytes 786440 | tf_op jit(solution)/shard_map/ppermute | solution.py:141
  98.7 0.0 collective-permute-done.refs_1_
  98.8 0.0 copy-start.5
  98.8 2.2 %collective-permute-start.4 = (bf16[1024,128]{1,0:T(8,128)(2,1)S(1)}, bf16[1024,128]{1,0:T(8,128)(2,1)S(1)}, u32[]{:S(2)}, u32[]{:S(2)}) collective-permute-start(bf16[1024,128]{1,0:T(8,128)(2,1)S(1)} %collective-permute-done.refs_1_), channel_id=1, source_target_pairs={{0,1},{1,0},{2,3},{3,2},{4,5},{5,4},{6,7},{7,6},{8,9},{9,8},{10,11... | collective-permute-start | bytes 786440 | tf_op jit(solution)/shard_map/ppermute | solution.py:141
  102.3 0.0 collective-permute-done.3.refs_4_
  102.3 0.0 copy-start.6
  102.3 0.0 collective-permute-done.6.refs_7_
  102.3 0.0 copy-start.7
  102.3 0.0 collective-permute-done.5.refs_6_
  102.3 0.0 copy-start.8
  102.3 0.0 collective-permute-done.4.refs_5_
  102.4 0.0 copy-start.9
  102.4 0.0 all-gather.2.cloned.1.call-done.weights
  102.4 0.0 copy-done.1
  102.4 0.0 copy-done.3
  102.4 0.0 copy-done.4
  102.4 0.0 copy-done.5
  102.4 0.6 copy-done.6
  103.0 0.1 copy-done.7
  103.1 0.1 copy-done.8
  103.2 0.1 copy-done.9
  103.3 9.5 %shard_map.94 = bf16[128,2048]{1,0:T(8,128)(2,1)} custom-call(s32[1]{0:T(128)} %bitcast.me, f32[1]{0:T(128)S(6)} %copy.15.stretch, f32[1]{0:T(128)S(6)} %copy.16.shift, s32[8,3,128]{2,1,0:T(4,128)} %copy-done.2, bf16[128,2048]{1,0:T(8,128)(2,1)} %bitcast.23, bf16[2048,1024]{1,0:T(8,128)(2,1)} %all-gather.2.cloned.1.call-done.weights, ...), custom_call_target="tpu_custom_call" | custom-call | flops 1073741824 | bytes 4194304 | tf_op jit(solution)/shard_map/pallas_call | solution.py:211
  (3 shorter events, 0.0 us)
Async XLA Ops:
  6.5 30.7 %copy-start = (bf16[256,1408]{1,0:T(8,128)(2,1)S(1)}, bf16[256,1408]{1,0:T(8,128)(2,1)}, u32[]{:S(2)}) copy-start(bf16[256,1408]{1,0:T(8,128)(2,1)} %param.10) | copy-start | bytes 2162692
  6.5 95.9 %all-gather.2.cloned.1.call-start = ((), (), s32[]{:S(2)}) async-start(), calls=%async_computation.3 | async-start | bytes 4259840 | tf_op jit(solution)/shard_map/all_gather | solution.py:160
  8.7 14.8 %all-to-all-start = ((s32[8,3,128]{2,1,0:T(4,128)}), s32[8,3,128]{2,1,0:T(4,128)S(1)}, u32[]{:S(2)}, u32[]{:S(2)}) async-start(s32[8,3,128]{2,1,0:T(4,128)} %shard_map.91), calls=%async_computation | async-start | bytes 32768 | tf_op jit(solution)/shard_map/all_to_all | solution.py:169
  23.4 16.4 %copy-start.2 = (s32[8,3,128]{2,1,0:T(4,128)}, s32[8,3,128]{2,1,0:T(4,128)S(1)}, u32[]{:S(2)}) copy-start(s32[8,3,128]{2,1,0:T(4,128)S(1)} %all-to-all-done.info) | copy-start | bytes 36868
  25.2 27.0 %all-to-all-start.1 = ((bf16[64,24,128]{2,1,0:T(8,128)(2,1)}), bf16[64,24,128]{2,1,0:T(8,128)(2,1)S(1)}, u32[]{:S(2)}, u32[]{:S(2)}) async-start(bf16[64,24,128]{2,1,0:T(8,128)(2,1)} %maximum_maximum_fusion), calls=%async_computation.1 | async-start | bytes 786432 | tf_op jit(solution)/shard_map/all_to_all | solution.py:191
  77.7 24.7 %copy-start.1 = (bf16[1024,128]{1,0:T(8,128)(2,1)}, bf16[1024,128]{1,0:T(8,128)(2,1)S(1)}, u32[]{:S(2)}) copy-start(bf16[1024,128]{1,0:T(8,128)(2,1)S(1)} %shard_map.93.refs_0_) | copy-start | bytes 786436
  77.7 15.5 %collective-permute-start.2 = (bf16[1024,128]{1,0:T(8,128)(2,1)S(1)}, bf16[1024,128]{1,0:T(8,128)(2,1)S(1)}, u32[]{:S(2)}, u32[]{:S(2)}) collective-permute-start(bf16[1024,128]{1,0:T(8,128)(2,1)S(1)} %shard_map.93.refs_0_), channel_id=1, source_target_pairs={{0,2},{2,4},{4,6},{6,0},{1,3},{3,5},{5,7},{7,1},{8,10},{10,12},{12... | collective-permute-start | bytes 786440 | tf_op jit(solution)/shard_map/ppermute | solution.py:144
  79.7 16.6 %collective-permute-start.1 = (bf16[1024,128]{1,0:T(8,128)(2,1)S(1)}, bf16[1024,128]{1,0:T(8,128)(2,1)S(1)}, u32[]{:S(2)}, u32[]{:S(2)}) collective-permute-start(bf16[1024,128]{1,0:T(8,128)(2,1)S(1)} %shard_map.93.refs_0_), channel_id=1, source_target_pairs={{0,6},{2,0},{4,2},{6,4},{1,7},{3,1},{5,3},{7,5},{8,14},{10,8},{12,... | collective-permute-start | bytes 786440 | tf_op jit(solution)/shard_map/ppermute | solution.py:144
  84.3 14.5 %collective-permute-start = (bf16[1024,128]{1,0:T(8,128)(2,1)S(1)}, bf16[1024,128]{1,0:T(8,128)(2,1)S(1)}, u32[]{:S(2)}, u32[]{:S(2)}) collective-permute-start(bf16[1024,128]{1,0:T(8,128)(2,1)S(1)} %shard_map.93.refs_0_), channel_id=1, source_target_pairs={{0,4},{2,6},{4,0},{6,2},{1,5},{3,7},{5,1},{7,3},{8,12},{10,14},{12... | collective-permute-start | bytes 786440 | tf_op jit(solution)/shard_map/ppermute | solution.py:144
  86.5 15.8 %collective-permute-start.3 = (bf16[1024,128]{1,0:T(8,128)(2,1)S(1)}, bf16[1024,128]{1,0:T(8,128)(2,1)S(1)}, u32[]{:S(2)}, u32[]{:S(2)}) collective-permute-start(bf16[1024,128]{1,0:T(8,128)(2,1)S(1)} %shard_map.93.refs_0_), channel_id=1, source_target_pairs={{0,1},{1,0},{2,3},{3,2},{4,5},{5,4},{6,7},{7,6},{8,9},{9,8},{10,11... | collective-permute-start | bytes 786440 | tf_op jit(solution)/shard_map/ppermute | solution.py:141
  93.3 9.2 %copy-start.3 = (bf16[1024,128]{1,0:T(8,128)(2,1)}, bf16[1024,128]{1,0:T(8,128)(2,1)S(1)}, u32[]{:S(2)}) copy-start(bf16[1024,128]{1,0:T(8,128)(2,1)S(1)} %collective-permute-done.2.refs_3_) | copy-start | bytes 786436
  93.3 9.0 %collective-permute-start.6 = (bf16[1024,128]{1,0:T(8,128)(2,1)S(1)}, bf16[1024,128]{1,0:T(8,128)(2,1)S(1)}, u32[]{:S(2)}, u32[]{:S(2)}) collective-permute-start(bf16[1024,128]{1,0:T(8,128)(2,1)S(1)} %collective-permute-done.2.refs_3_), channel_id=1, source_target_pairs={{0,1},{1,0},{2,3},{3,2},{4,5},{5,4},{6,7},{7,6},{8,9},{9,8},{10,11... | collective-permute-start | bytes 786440 | tf_op jit(solution)/shard_map/ppermute | solution.py:141
  96.3 6.2 %copy-start.4 = (bf16[1024,128]{1,0:T(8,128)(2,1)}, bf16[1024,128]{1,0:T(8,128)(2,1)S(1)}, u32[]{:S(2)}) copy-start(bf16[1024,128]{1,0:T(8,128)(2,1)S(1)} %collective-permute-done.1.refs_2_) | copy-start | bytes 786436
  96.3 6.1 %collective-permute-start.5 = (bf16[1024,128]{1,0:T(8,128)(2,1)S(1)}, bf16[1024,128]{1,0:T(8,128)(2,1)S(1)}, u32[]{:S(2)}, u32[]{:S(2)}) collective-permute-start(bf16[1024,128]{1,0:T(8,128)(2,1)S(1)} %collective-permute-done.1.refs_2_), channel_id=1, source_target_pairs={{0,1},{1,0},{2,3},{3,2},{4,5},{5,4},{6,7},{7,6},{8,9},{9,8},{10,11... | collective-permute-start | bytes 786440 | tf_op jit(solution)/shard_map/ppermute | solution.py:141
  98.8 3.7 %copy-start.5 = (bf16[1024,128]{1,0:T(8,128)(2,1)}, bf16[1024,128]{1,0:T(8,128)(2,1)S(1)}, u32[]{:S(2)}) copy-start(bf16[1024,128]{1,0:T(8,128)(2,1)S(1)} %collective-permute-done.refs_1_) | copy-start | bytes 786436
  98.8 3.6 %collective-permute-start.4 = (bf16[1024,128]{1,0:T(8,128)(2,1)S(1)}, bf16[1024,128]{1,0:T(8,128)(2,1)S(1)}, u32[]{:S(2)}, u32[]{:S(2)}) collective-permute-start(bf16[1024,128]{1,0:T(8,128)(2,1)S(1)} %collective-permute-done.refs_1_), channel_id=1, source_target_pairs={{0,1},{1,0},{2,3},{3,2},{4,5},{5,4},{6,7},{7,6},{8,9},{9,8},{10,11... | collective-permute-start | bytes 786440 | tf_op jit(solution)/shard_map/ppermute | solution.py:141
  102.3 0.7 copy-start.6
  102.3 0.8 copy-start.7
  102.3 0.8 copy-start.8
  102.4 0.9 copy-start.9
Sparse Core Ops, SparseCore 0:
  10.4 91.3 all-gather.1

commit v5 on v4

--- a/solution.py
+++ b/solution.py
@@ -10,7 +10,7 @@
 EPS = 1e-06
 LOSS_SCALE = 256.0
 CAP = 2
-HOPS = (0, 2, 3, 1)
+HOPS = (0, 1, 3, 2)
 LANES = 128
 BF = jnp.bfloat16
 F32 = jnp.float32
@@ -91,38 +91,49 @@
     return copies
 
 
-def grad_kernel(members, cores, rows, me, stretch, shift, info, text, weights, *refs):
-    images, (out, img, wt, norms, matches, slopes, img_sems, wt_sems) = refs[:members], refs[members:]
-    img_copies = load_columns(me[0], cores, images, img, img_sems)
-    chunk = wt.shape[0] // wt_sems.shape[0]
-    wt_copies = []
-    for k in range(wt_sems.shape[0]):
-        span = slice(k * chunk, (k + 1) * chunk)
-        wt_copies.append(pltpu.make_async_copy(weights.at[span], wt.at[span], wt_sems.at[k]))
-        wt_copies[k].start()
-    gain, offset = stretch[0], shift[0]
-    pairs = text.shape[0]
+def image_kernel(members, cores, me, info, *refs):
+    images, (whole, norms, matches, img, sems, out_sem) = refs[:members], refs[members:]
+    copies = load_columns(me[0], cores, images, img, sems)
+    pairs = matches.shape[1]
     own_labels = info[me[0], 2:3, :]
     for g in range(members):
         span = slice(g * pairs, (g + 1) * pairs)
         matches[span, :] = (as_column(info[g, 2:3, :]) == own_labels).astype(F32)
-    for copy in img_copies:
+    for copy in copies:
         copy.wait()
+    write = pltpu.make_async_copy(img, whole, out_sem)
+    write.start()
     for g in range(members):
         span = slice(g * pairs, (g + 1) * pairs)
         wide = img[span, :].astype(F32)
         inv = lax.rsqrt(jnp.sum(wide * wide, axis=1, keepdims=True) + EPS)
         norms[span, :] = jnp.broadcast_to(inv, (pairs, pairs))
+    write.wait()
+
+
+def grad_kernel(rows, stretch, shift, text_in, weights, img_in, norms_in, matches_in, out,
+                text, wt, img, norms, matches, slopes, wt_sems, sems):
+    ins, bufs = (text_in, img_in, norms_in, matches_in), (text, img, norms, matches)
+    copies = [pltpu.make_async_copy(a, b, sems.at[k]) for k, (a, b) in enumerate(zip(ins, bufs))]
+    chunk = wt.shape[0] // wt_sems.shape[0]
+    spans = [slice(k * chunk, (k + 1) * chunk) for k in range(wt_sems.shape[0])]
+    wt_copies = [pltpu.make_async_copy(weights.at[p], wt.at[p], wt_sems.at[k]) for k, p in enumerate(spans)]
+    for copy in copies[:1] + wt_copies + copies[1:]:
+        copy.start()
+    gain, offset = stretch[0], shift[0]
+    pairs = text.shape[0]
+    same_micro = (iota((pairs, pairs), 0) >= rows) == (iota((pairs, pairs), 1) >= rows)
+    copies[0].wait()
     raw = jnp.zeros((pairs, wt.shape[1]), F32)
-    for k, copy in enumerate(wt_copies):
+    for copy, span in zip(wt_copies, spans):
         copy.wait()
-        span = slice(k * chunk, (k + 1) * chunk)
         raw = raw + dot(text[:, span], wt[span, :], 1, 0)
     inverse = lax.rsqrt(jnp.sum(raw * raw, axis=1, keepdims=True) + EPS)
     unit = raw * inverse
+    for copy in copies[1:]:
+        copy.wait()
     similar = dot(img[...], unit.astype(BF), 1, 1)
-    same_micro = (iota((pairs, pairs), 0) >= rows) == (iota((pairs, pairs), 1) >= rows)
-    for g in range(members):
+    for g in range(img.shape[0] // pairs):
         span = slice(g * pairs, (g + 1) * pairs)
         inv = norms[span, :]
         logit = gain * inv * similar[span, :] + offset
@@ -208,25 +219,43 @@
         )(slot, fetched.reshape(owners * slots, width))
 
         image_pieces = whole_group(mine)
+        images = members * pairs
+        img, norms, matches = pl.pallas_call(
+            functools.partial(image_kernel, members, nc),
+            out_shape=(
+                jax.ShapeDtypeStruct((images, emb), BF),
+                jax.ShapeDtypeStruct((images, pairs), F32),
+                jax.ShapeDtypeStruct((images, pairs), F32),
+            ),
+            in_specs=[SMEM, VMEM] + [ANY] * members,
+            out_specs=(ANY, VMEM, VMEM),
+            scratch_shapes=[
+                pltpu.VMEM((images, emb), BF),
+                pltpu.SemaphoreType.DMA((members,)),
+                pltpu.SemaphoreType.DMA,
+            ],
+            compiler_params=SMALL,
+        )(me.reshape(1), info, *image_pieces)
         out = pl.pallas_call(
-            functools.partial(grad_kernel, members, nc, rows),
+            functools.partial(grad_kernel, rows),
             out_shape=jax.ShapeDtypeStruct((pairs, d_txt), BF),
-            in_specs=[SMEM, SMEM, SMEM, VMEM, VMEM] + [ANY] * (members + 1),
+            in_specs=[SMEM, SMEM] + [ANY] * 5,
             out_specs=VMEM,
             scratch_shapes=[
-                pltpu.VMEM((members * pairs, emb), BF),
+                pltpu.VMEM((pairs, d_txt), BF),
                 pltpu.VMEM((d_txt, emb), BF),
-                pltpu.VMEM((members * pairs, pairs), F32),
-                pltpu.VMEM((members * pairs, pairs), F32),
-                pltpu.VMEM((members * pairs, pairs), BF),
-                pltpu.SemaphoreType.DMA((members,)),
+                pltpu.VMEM((images, emb), BF),
+                pltpu.VMEM((images, pairs), F32),
+                pltpu.VMEM((images, pairs), F32),
+                pltpu.VMEM((images, pairs), BF),
+                pltpu.SemaphoreType.DMA((4,)),
                 pltpu.SemaphoreType.DMA((4,)),
             ],
             compiler_params=LARGE,
             cost_estimate=pl.CostEstimate(
                 flops=4 * pairs * d_txt * emb, bytes_accessed=2 * d_txt * emb, transcendentals=0
             ),
-        )(me.reshape(1), stretch, offset, info, text.reshape(pairs, d_txt), wt_all, *image_pieces)
+        )(stretch, offset, text.reshape(pairs, d_txt), wt_all, img, norms, matches)
         return out.reshape(micro, rows, d_txt)
 
     return local

time: 122 us -> 123 us (level)
  local copies, waits for them, and re-layouts: 1.84 us -> 3.89 us
    unnamed x20 -> x8, local copies, waits for them, and re-layouts: 0.88 us -> 2.95 us
    pallas_call x1 -> x2, Pallas kernels: 9.54 us -> 9.6 us  [the longest x1 8.03 us: local(): pl.pallas_call(functools.partial(grad_kernel, rows), out_shape=jax.ShapeD...]
  transfers between devices with their start and end apart: 10 -> 10, of which waited for: 2 -> 2; matrix products, arithmetic and copies ran while one was open for 5% -> 5% of each run, Pallas kernels for 3% -> 4%
where the time goes in v5:
time: 123 us; the launch traced here: 122 us
  starting transfers between devices  45.2 us (37%)
  blocking collectives  23.1 us (19%)
  waiting for transfers between devices  17.1 us (14%)
  between operations  14.9 us (12%)
  Pallas kernels  13 us (11%)
  local copies, waits for them, and re-layouts  3.89 us (3%)
  matrix products  3.55 us (3%)
    all_to_all x1, blocking collectives, local(): lax.all_to_all(served, ('z', 'y'), split_axis=0, concat_axis=0, tiled=True)  23.1 us
    ppermute x4, starting transfers between devices, swap(): return lax.ppermute(v, 'core', [(i, nc - 1 - i) for i in range(nc)])  14.4 us
    all_to_all x1, waiting for transfers between devices, local(): lax.all_to_all(sent, ('z', 'y'), split_axis=0, concat_axis=0, tiled=True)  12.4 us
    all_to_all x1, starting transfers between devices, local(): lax.all_to_all(sent, ('z', 'y'), split_axis=0, concat_axis=0, tiled=True)  12 us
    all_to_all x1, starting transfers between devices, local(): lax.all_to_all(info, ('x', 'core'), split_axis=0, concat_axis=0, tiled=True)  10.1 us
    ppermute x3, starting transfers between devices, shift(): return lax.ppermute(v, 'x', [(i, (i + by) % nx) for i in range(nx)])  8.67 us
    pallas_call x1, Pallas kernels, local(): pl.pallas_call(functools.partial(grad_kernel, rows), out_shape=jax.ShapeD...  8.03 us
    all_to_all x1, waiting for transfers between devices, local(): lax.all_to_all(info, ('x', 'core'), split_axis=0, concat_axis=0, tiled=True)  3.9 us
  transfers between devices with their start and end apart: 10, of which 2 were waited for; matrix products, arithmetic and copies ran while one was open for 5% of the time, Pallas kernels for 4%

profile of v5, /device:TPU:1, one launch (start us, length us, event | category | flops | bytes accessed | tf_op | source)
XLA Modules:
  0.0 121.7 jit_solution(2408772268822884613)
XLA Ops:
  6.5 0.0 copy-start
  6.5 0.0 all-gather.2.cloned.1.call-start
  6.5 0.7 all-gather.2.cloned.1.call-update
  7.3 1.4 %shard_map.91 = s32[8,3,128]{2,1,0:T(4,128)} custom-call(s32[2,1,64]{2,1,0:T(1,128)} %bitcast.24, s32[2,64]{1,0:T(2,128)} %entry.1, s32[2,64]{1,0:T(2,128)} %labels.1), custom_call_target="tpu_custom_call" | custom-call | tf_op jit(solution)/shard_map/pallas_call | solution.py:173
  8.7 10.1 %all-to-all-start = ((s32[8,3,128]{2,1,0:T(4,128)}), s32[8,3,128]{2,1,0:T(4,128)S(1)}, u32[]{:S(2)}, u32[]{:S(2)}) async-start(s32[8,3,128]{2,1,0:T(4,128)} %shard_map.91), calls=%async_computation | async-start | bytes 32768 | tf_op jit(solution)/shard_map/all_to_all | solution.py:180
  18.8 0.7 constant_dynamic-slice_fusion
  19.5 0.1 pad.2.clone
  19.5 3.9 %all-to-all-done.info = s32[8,3,128]{2,1,0:T(4,128)S(1)} async-done(((s32[8,3,128]{2,1,0:T(4,128)}), s32[8,3,128]{2,1,0:T(4,128)S(1)}, u32[]{:S(2)}, u32[]{:S(2)}) %all-to-all-start) | async-done | bytes 12320 | tf_op jit(solution)/shard_map/all_to_all | solution.py:180
  23.4 0.7 shard_map.92
  24.1 0.1 copy.14
  24.2 0.1 broadcast_in_dim.6
  24.2 0.9 maximum_maximum_fusion
  25.2 12.0 %all-to-all-start.1 = ((bf16[64,24,128]{2,1,0:T(8,128)(2,1)}), bf16[64,24,128]{2,1,0:T(8,128)(2,1)S(1)}, u32[]{:S(2)}, u32[]{:S(2)}) async-start(bf16[64,24,128]{2,1,0:T(8,128)(2,1)} %maximum_maximum_fusion), calls=%async_computation.1 | async-start | bytes 786432 | tf_op jit(solution)/shard_map/all_to_all | solution.py:202
  37.2 0.0 copy-done
  37.2 2.6 %fusion.5.clone.6 = bf16[1536,256]{1,0:T(8,128)(2,1)S(1)} fusion(bf16[256,1408]{1,0:T(8,128)(2,1)S(1)} %copy-done, s32[1408]{0:T(1024)S(1)} %get-tuple-element.16, s32[1408]{0:T(1024)S(1)} %get-tuple-element.17, s32[1408]{0:T(1024)S(1)} %get-tuple-element.15, s32[1408]{0:T(1024)S(1)} %get-tuple-element.18, ...), kind=kOutput, calls=%fused_computation.5.clone.clone.clone.clone.clone.1 | convolution fusion | flops 1120665600 | bytes 1532672 | tf_op jit(solution)/shard_map/dot_general | solution.py:26
  39.8 12.4 %all-to-all-done.1 = bf16[64,24,128]{2,1,0:T(8,128)(2,1)S(1)} async-done(((bf16[64,24,128]{2,1,0:T(8,128)(2,1)}), bf16[64,24,128]{2,1,0:T(8,128)(2,1)S(1)}, u32[]{:S(2)}, u32[]{:S(2)}) %all-to-all-start.1) | async-done | bytes 393248 | tf_op jit(solution)/shard_map/all_to_all | solution.py:202
  52.3 0.1 fusion.15
  52.4 0.1 reshape.32
  52.5 0.4 fusion.11
  52.9 0.5 convolution_convert_fusion
  53.4 23.1 %all_to_all.15 = bf16[64,32,128]{2,1,0:T(8,128)(2,1)S(1)} all-to-all(bf16[64,32,128]{2,1,0:T(8,128)(2,1)S(1)} %bitcast.23), channel_id=1, replica_groups=mesh['z'=8,'y'=8,'x'=4,'core'=2] {'z','y'}, dimensions={0} | all-to-all | bytes 1048576 | tf_op jit(solution)/shard_map/all_to_all | solution.py:212
  76.5 1.3 %shard_map.93.refs_0_ = bf16[1024,128]{1,0:T(8,128)(2,1)S(1)} custom-call(s32[8,128]{1,0:T(8,128)S(1)} %get-tuple-element.10.slot, bf16[2048,128]{1,0:T(8,128)(2,1)S(1)} %bitcast.19), custom_call_target="tpu_custom_call" | custom-call | tf_op jit(solution)/shard_map/pallas_call | solution.py:213
  77.8 1.9 %collective-permute-start = (bf16[1024,128]{1,0:T(8,128)(2,1)S(1)}, bf16[1024,128]{1,0:T(8,128)(2,1)S(1)}, u32[]{:S(2)}, u32[]{:S(2)}) collective-permute-start(bf16[1024,128]{1,0:T(8,128)(2,1)S(1)} %shard_map.93.refs_0_), channel_id=1, source_target_pairs={{0,2},{2,4},{4,6},{6,0},{1,3},{3,5},{5,7},{7,1},{8,10},{10,12},{12... | collective-permute-start | bytes 786440 | tf_op jit(solution)/shard_map/ppermute | solution.py:155
  79.7 4.6 %collective-permute-start.1 = (bf16[1024,128]{1,0:T(8,128)(2,1)S(1)}, bf16[1024,128]{1,0:T(8,128)(2,1)S(1)}, u32[]{:S(2)}, u32[]{:S(2)}) collective-permute-start(bf16[1024,128]{1,0:T(8,128)(2,1)S(1)} %shard_map.93.refs_0_), channel_id=1, source_target_pairs={{0,6},{2,0},{4,2},{6,4},{1,7},{3,1},{5,3},{7,5},{8,14},{10,8},{12,... | collective-permute-start | bytes 786440 | tf_op jit(solution)/shard_map/ppermute | solution.py:155
  84.3 2.2 %collective-permute-start.2 = (bf16[1024,128]{1,0:T(8,128)(2,1)S(1)}, bf16[1024,128]{1,0:T(8,128)(2,1)S(1)}, u32[]{:S(2)}, u32[]{:S(2)}) collective-permute-start(bf16[1024,128]{1,0:T(8,128)(2,1)S(1)} %shard_map.93.refs_0_), channel_id=1, source_target_pairs={{0,4},{2,6},{4,0},{6,2},{1,5},{3,7},{5,1},{7,3},{8,12},{10,14},{12... | collective-permute-start | bytes 786440 | tf_op jit(solution)/shard_map/ppermute | solution.py:155
  86.5 6.7 %collective-permute-start.3 = (bf16[1024,128]{1,0:T(8,128)(2,1)S(1)}, bf16[1024,128]{1,0:T(8,128)(2,1)S(1)}, u32[]{:S(2)}, u32[]{:S(2)}) collective-permute-start(bf16[1024,128]{1,0:T(8,128)(2,1)S(1)} %shard_map.93.refs_0_), channel_id=1, source_target_pairs={{0,1},{1,0},{2,3},{3,2},{4,5},{5,4},{6,7},{7,6},{8,9},{9,8},{10,11... | collective-permute-start | bytes 786440 | tf_op jit(solution)/shard_map/ppermute | solution.py:152
  93.2 0.0 collective-permute-done.refs_1_
  93.2 3.0 %collective-permute-start.4 = (bf16[1024,128]{1,0:T(8,128)(2,1)S(1)}, bf16[1024,128]{1,0:T(8,128)(2,1)S(1)}, u32[]{:S(2)}, u32[]{:S(2)}) collective-permute-start(bf16[1024,128]{1,0:T(8,128)(2,1)S(1)} %collective-permute-done.refs_1_), channel_id=1, source_target_pairs={{0,1},{1,0},{2,3},{3,2},{4,5},{5,4},{6,7},{7,6},{8,9},{9,8},{10,11... | collective-permute-start | bytes 786440 | tf_op jit(solution)/shard_map/ppermute | solution.py:152
  96.2 0.0 collective-permute-done.1.refs_2_
  96.2 2.5 %collective-permute-start.5 = (bf16[1024,128]{1,0:T(8,128)(2,1)S(1)}, bf16[1024,128]{1,0:T(8,128)(2,1)S(1)}, u32[]{:S(2)}, u32[]{:S(2)}) collective-permute-start(bf16[1024,128]{1,0:T(8,128)(2,1)S(1)} %collective-permute-done.1.refs_2_), channel_id=1, source_target_pairs={{0,1},{1,0},{2,3},{3,2},{4,5},{5,4},{6,7},{7,6},{8,9},{9,8},{10,11... | collective-permute-start | bytes 786440 | tf_op jit(solution)/shard_map/ppermute | solution.py:152
  98.8 0.0 collective-permute-done.2.refs_3_
  98.8 2.2 %collective-permute-start.6 = (bf16[1024,128]{1,0:T(8,128)(2,1)S(1)}, bf16[1024,128]{1,0:T(8,128)(2,1)S(1)}, u32[]{:S(2)}, u32[]{:S(2)}) collective-permute-start(bf16[1024,128]{1,0:T(8,128)(2,1)S(1)} %collective-permute-done.2.refs_3_), channel_id=1, source_target_pairs={{0,1},{1,0},{2,3},{3,2},{4,5},{5,4},{6,7},{7,6},{8,9},{9,8},{10,11... | collective-permute-start | bytes 786440 | tf_op jit(solution)/shard_map/ppermute | solution.py:152
  102.3 0.0 collective-permute-done.3.refs_4_
  102.3 0.0 collective-permute-done.4.refs_5_
  102.3 0.0 collective-permute-done.5.refs_6_
  102.3 0.0 collective-permute-done.6.refs_7_
  102.3 1.6 %shard_map.94 = (bf16[1024,1024]{1,0:T(8,128)(2,1)S(1)}, f32[1024,128]{1,0:T(8,128)S(1)}, f32[1024,128]{1,0:T(8,128)S(1)}) custom-call(s32[1]{0:T(128)} %bitcast.1.me, s32[8,3,128]{2,1,0:T(4,128)S(1)} %all-to-all-done.info, bf16[1024,128]{1,0:T(8,128)(2,1)S(1)} %shard_map.93.refs_0_, bf16[1024,128]{1,0:T(8,128)(2,1)S(1)} %collective-permute-done.refs_1_, ...), custom_call_target="tpu_custom_call" | custom-call | tf_op jit(solution)/shard_map/pallas_call | solution.py:223
  103.9 0.0 copy-start.1
  103.9 1.3 %copy-done.1 = bf16[1024,1024]{1,0:T(8,128)(2,1)} copy-done((bf16[1024,1024]{1,0:T(8,128)(2,1)}, bf16[1024,1024]{1,0:T(8,128)(2,1)S(1)}, u32[]{:S(2)}) %copy-start.1) | copy-done | bytes 2097176
  105.2 0.0 copy-start.2
  105.2 0.8 copy-done.2
  106.0 0.0 copy-start.3
  106.0 0.8 copy-done.3
  106.8 0.0 all-gather.2.cloned.1.call-done.weights
  106.8 8.0 %shard_map.95 = bf16[128,2048]{1,0:T(8,128)(2,1)} custom-call(f32[1]{0:T(128)S(6)} %copy.15.stretch, f32[1]{0:T(128)S(6)} %copy.16.shift, bf16[128,2048]{1,0:T(8,128)(2,1)} %bitcast.22, bf16[2048,1024]{1,0:T(8,128)(2,1)} %all-gather.2.cloned.1.call-done.weights, bf16[1024,1024]{1,0:T(8,128)(2,1)} %copy-done.1, f32[1024,128]{1,0:T(8,128)} %copy-done.2, ...), custom_call_target="tpu_custom_call" | custom-call | flops 1073741824 | bytes 4194304 | tf_op jit(solution)/shard_map/pallas_call | solution.py:239
  (3 shorter events, 0.0 us)
Async XLA Ops:
  6.5 30.6 %copy-start = (bf16[256,1408]{1,0:T(8,128)(2,1)S(1)}, bf16[256,1408]{1,0:T(8,128)(2,1)}, u32[]{:S(2)}) copy-start(bf16[256,1408]{1,0:T(8,128)(2,1)} %param.10) | copy-start | bytes 2162692
  6.5 100.3 %all-gather.2.cloned.1.call-start = ((), (), s32[]{:S(2)}) async-start(), calls=%async_computation.3 | async-start | bytes 4259840 | tf_op jit(solution)/shard_map/all_gather | solution.py:171
  8.7 14.8 %all-to-all-start = ((s32[8,3,128]{2,1,0:T(4,128)}), s32[8,3,128]{2,1,0:T(4,128)S(1)}, u32[]{:S(2)}, u32[]{:S(2)}) async-start(s32[8,3,128]{2,1,0:T(4,128)} %shard_map.91), calls=%async_computation | async-start | bytes 32768 | tf_op jit(solution)/shard_map/all_to_all | solution.py:180
  25.2 27.1 %all-to-all-start.1 = ((bf16[64,24,128]{2,1,0:T(8,128)(2,1)}), bf16[64,24,128]{2,1,0:T(8,128)(2,1)S(1)}, u32[]{:S(2)}, u32[]{:S(2)}) async-start(bf16[64,24,128]{2,1,0:T(8,128)(2,1)} %maximum_maximum_fusion), calls=%async_computation.1 | async-start | bytes 786432 | tf_op jit(solution)/shard_map/all_to_all | solution.py:202
  77.8 15.4 %collective-permute-start = (bf16[1024,128]{1,0:T(8,128)(2,1)S(1)}, bf16[1024,128]{1,0:T(8,128)(2,1)S(1)}, u32[]{:S(2)}, u32[]{:S(2)}) collective-permute-start(bf16[1024,128]{1,0:T(8,128)(2,1)S(1)} %shard_map.93.refs_0_), channel_id=1, source_target_pairs={{0,2},{2,4},{4,6},{6,0},{1,3},{3,5},{5,7},{7,1},{8,10},{10,12},{12... | collective-permute-start | bytes 786440 | tf_op jit(solution)/shard_map/ppermute | solution.py:155
  79.7 16.5 %collective-permute-start.1 = (bf16[1024,128]{1,0:T(8,128)(2,1)S(1)}, bf16[1024,128]{1,0:T(8,128)(2,1)S(1)}, u32[]{:S(2)}, u32[]{:S(2)}) collective-permute-start(bf16[1024,128]{1,0:T(8,128)(2,1)S(1)} %shard_map.93.refs_0_), channel_id=1, source_target_pairs={{0,6},{2,0},{4,2},{6,4},{1,7},{3,1},{5,3},{7,5},{8,14},{10,8},{12,... | collective-permute-start | bytes 786440 | tf_op jit(solution)/shard_map/ppermute | solution.py:155
  84.3 14.5 %collective-permute-start.2 = (bf16[1024,128]{1,0:T(8,128)(2,1)S(1)}, bf16[1024,128]{1,0:T(8,128)(2,1)S(1)}, u32[]{:S(2)}, u32[]{:S(2)}) collective-permute-start(bf16[1024,128]{1,0:T(8,128)(2,1)S(1)} %shard_map.93.refs_0_), channel_id=1, source_target_pairs={{0,4},{2,6},{4,0},{6,2},{1,5},{3,7},{5,1},{7,3},{8,12},{10,14},{12... | collective-permute-start | bytes 786440 | tf_op jit(solution)/shard_map/ppermute | solution.py:155
  86.5 15.8 %collective-permute-start.3 = (bf16[1024,128]{1,0:T(8,128)(2,1)S(1)}, bf16[1024,128]{1,0:T(8,128)(2,1)S(1)}, u32[]{:S(2)}, u32[]{:S(2)}) collective-permute-start(bf16[1024,128]{1,0:T(8,128)(2,1)S(1)} %shard_map.93.refs_0_), channel_id=1, source_target_pairs={{0,1},{1,0},{2,3},{3,2},{4,5},{5,4},{6,7},{7,6},{8,9},{9,8},{10,11... | collective-permute-start | bytes 786440 | tf_op jit(solution)/shard_map/ppermute | solution.py:152
  93.2 9.0 %collective-permute-start.4 = (bf16[1024,128]{1,0:T(8,128)(2,1)S(1)}, bf16[1024,128]{1,0:T(8,128)(2,1)S(1)}, u32[]{:S(2)}, u32[]{:S(2)}) collective-permute-start(bf16[1024,128]{1,0:T(8,128)(2,1)S(1)} %collective-permute-done.refs_1_), channel_id=1, source_target_pairs={{0,1},{1,0},{2,3},{3,2},{4,5},{5,4},{6,7},{7,6},{8,9},{9,8},{10,11... | collective-permute-start | bytes 786440 | tf_op jit(solution)/shard_map/ppermute | solution.py:152
  96.2 6.0 %collective-permute-start.5 = (bf16[1024,128]{1,0:T(8,128)(2,1)S(1)}, bf16[1024,128]{1,0:T(8,128)(2,1)S(1)}, u32[]{:S(2)}, u32[]{:S(2)}) collective-permute-start(bf16[1024,128]{1,0:T(8,128)(2,1)S(1)} %collective-permute-done.1.refs_2_), channel_id=1, source_target_pairs={{0,1},{1,0},{2,3},{3,2},{4,5},{5,4},{6,7},{7,6},{8,9},{9,8},{10,11... | collective-permute-start | bytes 786440 | tf_op jit(solution)/shard_map/ppermute | solution.py:152
  98.8 3.5 %collective-permute-start.6 = (bf16[1024,128]{1,0:T(8,128)(2,1)S(1)}, bf16[1024,128]{1,0:T(8,128)(2,1)S(1)}, u32[]{:S(2)}, u32[]{:S(2)}) collective-permute-start(bf16[1024,128]{1,0:T(8,128)(2,1)S(1)} %collective-permute-done.2.refs_3_), channel_id=1, source_target_pairs={{0,1},{1,0},{2,3},{3,2},{4,5},{5,4},{6,7},{7,6},{8,9},{9,8},{10,11... | collective-permute-start | bytes 786440 | tf_op jit(solution)/shard_map/ppermute | solution.py:152
  103.9 1.4 %copy-start.1 = (bf16[1024,1024]{1,0:T(8,128)(2,1)}, bf16[1024,1024]{1,0:T(8,128)(2,1)S(1)}, u32[]{:S(2)}) copy-start(bf16[1024,1024]{1,0:T(8,128)(2,1)S(1)} %get-tuple-element.12.img_in) | copy-start | bytes 6291460
  105.2 0.8 copy-start.2
  106.0 0.8 copy-start.3
Sparse Core Ops, SparseCore 0:
  10.4 91.9 all-gather.1

commit v6 on v5

--- a/solution.py
+++ b/solution.py
@@ -132,11 +132,11 @@
     unit = raw * inverse
     for copy in copies[1:]:
         copy.wait()
-    similar = dot(img[...], unit.astype(BF), 1, 1)
+    unit_bf = unit.astype(BF)
     for g in range(img.shape[0] // pairs):
         span = slice(g * pairs, (g + 1) * pairs)
         inv = norms[span, :]
-        logit = gain * inv * similar[span, :] + offset
+        logit = gain * inv * dot(img[span, :], unit_bf, 1, 1) + offset
         slope = LOSS_SCALE * inv * (jax.nn.sigmoid(logit) - matches[span, :])
         slopes[span, :] = jnp.where(same_micro, slope, 0.0).astype(BF)
     grad = gain * dot(slopes[...], img[...], 0, 0)
@@ -234,7 +234,7 @@
                 pltpu.SemaphoreType.DMA((members,)),
                 pltpu.SemaphoreType.DMA,
             ],
-            compiler_params=SMALL,
+            compiler_params=LARGE,
         )(me.reshape(1), info, *image_pieces)
         out = pl.pallas_call(
             functools.partial(grad_kernel, rows),

time: 123 us -> 123 us (level)
  Pallas kernels: 13 us -> 15.1 us
  local copies, waits for them, and re-layouts: 3.89 us -> 1.94 us
    pallas_call x1, Pallas kernels: 1.57 us -> 4.63 us  [local(): pl.pallas_call(functools.partial(image_kernel, members, nc), out_shape=(j...]
    unnamed x8 -> x20, local copies, waits for them, and re-layouts: 2.95 us -> 0.99 us
  transfers between devices with their start and end apart: 10 -> 10, of which waited for: 2 -> 2; matrix products, arithmetic and copies ran while one was open for 5% -> 5% of each run, Pallas kernels for 4% -> 7%
where the time goes in v6:
time: 123 us; the launch traced here: 122 us
  starting transfers between devices  45.2 us (37%)
  blocking collectives  23.1 us (19%)
  waiting for transfers between devices  17 us (14%)
  Pallas kernels  15.1 us (12%)
  between operations  15 us (12%)
  matrix products  3.56 us (3%)
  local copies, waits for them, and re-layouts  1.94 us (2%)
    all_to_all x1, blocking collectives, local(): lax.all_to_all(served, ('z', 'y'), split_axis=0, concat_axis=0, tiled=True)  23.1 us
    ppermute x4, starting transfers between devices, swap(): return lax.ppermute(v, 'core', [(i, nc - 1 - i) for i in range(nc)])  14.4 us
    all_to_all x1, waiting for transfers between devices, local(): lax.all_to_all(sent, ('z', 'y'), split_axis=0, concat_axis=0, tiled=True)  12.3 us
    all_to_all x1, starting transfers between devices, local(): lax.all_to_all(sent, ('z', 'y'), split_axis=0, concat_axis=0, tiled=True)  12 us
    all_to_all x1, starting transfers between devices, local(): lax.all_to_all(info, ('x', 'core'), split_axis=0, concat_axis=0, tiled=True)  10.1 us
    ppermute x3, starting transfers between devices, shift(): return lax.ppermute(v, 'x', [(i, (i + by) % nx) for i in range(nx)])  8.74 us
    pallas_call x1, Pallas kernels, local(): pl.pallas_call(functools.partial(grad_kernel, rows), out_shape=jax.ShapeD...  7.01 us
    pallas_call x1, Pallas kernels, local(): pl.pallas_call(functools.partial(image_kernel, members, nc), out_shape=(j...  4.63 us
  transfers between devices with their start and end apart: 10, of which 2 were waited for; matrix products, arithmetic and copies ran while one was open for 5% of the time, Pallas kernels for 7%

profile of v6, /device:TPU:1, one launch (start us, length us, event | category | flops | bytes accessed | tf_op | source)
XLA Modules:
  0.0 121.9 jit_solution(6522843784395736683)
XLA Ops:
  6.5 0.0 copy-start
  6.5 0.0 all-gather.2.cloned.1.call-start
  6.5 0.7 all-gather.2.cloned.1.call-update
  7.3 1.4 %shard_map.91 = s32[8,3,128]{2,1,0:T(4,128)} custom-call(s32[2,1,64]{2,1,0:T(1,128)} %bitcast.24, s32[2,64]{1,0:T(2,128)} %entry.1, s32[2,64]{1,0:T(2,128)} %labels.1), custom_call_target="tpu_custom_call" | custom-call | tf_op jit(solution)/shard_map/pallas_call | solution.py:173
  8.7 10.1 %all-to-all-start = ((s32[8,3,128]{2,1,0:T(4,128)}), s32[8,3,128]{2,1,0:T(4,128)S(1)}, u32[]{:S(2)}, u32[]{:S(2)}) async-start(s32[8,3,128]{2,1,0:T(4,128)} %shard_map.91), calls=%async_computation | async-start | bytes 32768 | tf_op jit(solution)/shard_map/all_to_all | solution.py:180
  18.8 0.7 constant_dynamic-slice_fusion
  19.5 0.1 pad.2.clone
  19.5 3.9 %all-to-all-done.info = s32[8,3,128]{2,1,0:T(4,128)S(1)} async-done(((s32[8,3,128]{2,1,0:T(4,128)}), s32[8,3,128]{2,1,0:T(4,128)S(1)}, u32[]{:S(2)}, u32[]{:S(2)}) %all-to-all-start) | async-done | bytes 12320 | tf_op jit(solution)/shard_map/all_to_all | solution.py:180
  23.4 0.0 copy-start.2
  23.4 0.7 shard_map.92
  24.1 0.1 copy.14
  24.2 0.1 broadcast_in_dim.6
  24.2 0.9 maximum_maximum_fusion
  25.2 12.0 %all-to-all-start.1 = ((bf16[64,24,128]{2,1,0:T(8,128)(2,1)}), bf16[64,24,128]{2,1,0:T(8,128)(2,1)S(1)}, u32[]{:S(2)}, u32[]{:S(2)}) async-start(bf16[64,24,128]{2,1,0:T(8,128)(2,1)} %maximum_maximum_fusion), calls=%async_computation.1 | async-start | bytes 786432 | tf_op jit(solution)/shard_map/all_to_all | solution.py:202
  37.2 0.0 copy-done
  37.2 2.6 %fusion.5.clone.6 = bf16[1536,256]{1,0:T(8,128)(2,1)S(1)} fusion(bf16[256,1408]{1,0:T(8,128)(2,1)S(1)} %copy-done, s32[1408]{0:T(1024)S(1)} %get-tuple-element.16, s32[1408]{0:T(1024)S(1)} %get-tuple-element.17, s32[1408]{0:T(1024)S(1)} %get-tuple-element.15, s32[1408]{0:T(1024)S(1)} %get-tuple-element.18, ...), kind=kOutput, calls=%fused_computation.5.clone.clone.clone.clone.clone.1 | convolution fusion | flops 1120665600 | bytes 1532672 | tf_op jit(solution)/shard_map/dot_general | solution.py:26
  39.8 0.0 copy-done.2
  39.8 12.3 %all-to-all-done.1 = bf16[64,24,128]{2,1,0:T(8,128)(2,1)S(1)} async-done(((bf16[64,24,128]{2,1,0:T(8,128)(2,1)}), bf16[64,24,128]{2,1,0:T(8,128)(2,1)S(1)}, u32[]{:S(2)}, u32[]{:S(2)}) %all-to-all-start.1) | async-done | bytes 393248 | tf_op jit(solution)/shard_map/all_to_all | solution.py:202
  52.2 0.1 fusion.15
  52.3 0.1 reshape.32
  52.4 0.4 fusion.11
  52.8 0.5 convolution_convert_fusion
  53.3 23.1 %all_to_all.15 = bf16[64,32,128]{2,1,0:T(8,128)(2,1)S(1)} all-to-all(bf16[64,32,128]{2,1,0:T(8,128)(2,1)S(1)} %bitcast.23), channel_id=1, replica_groups=mesh['z'=8,'y'=8,'x'=4,'core'=2] {'z','y'}, dimensions={0} | all-to-all | bytes 1048576 | tf_op jit(solution)/shard_map/all_to_all | solution.py:212
  76.4 1.3 %shard_map.93.refs_0_ = bf16[1024,128]{1,0:T(8,128)(2,1)S(1)} custom-call(s32[8,128]{1,0:T(8,128)S(1)} %get-tuple-element.10.slot, bf16[2048,128]{1,0:T(8,128)(2,1)S(1)} %bitcast.19), custom_call_target="tpu_custom_call" | custom-call | tf_op jit(solution)/shard_map/pallas_call | solution.py:213
  77.7 0.0 copy-start.1
  77.8 1.9 %collective-permute-start = (bf16[1024,128]{1,0:T(8,128)(2,1)S(1)}, bf16[1024,128]{1,0:T(8,128)(2,1)S(1)}, u32[]{:S(2)}, u32[]{:S(2)}) collective-permute-start(bf16[1024,128]{1,0:T(8,128)(2,1)S(1)} %shard_map.93.refs_0_), channel_id=1, source_target_pairs={{0,2},{2,4},{4,6},{6,0},{1,3},{3,5},{5,7},{7,1},{8,10},{10,12},{12... | collective-permute-start | bytes 786440 | tf_op jit(solution)/shard_map/ppermute | solution.py:155
  79.7 4.6 %collective-permute-start.1 = (bf16[1024,128]{1,0:T(8,128)(2,1)S(1)}, bf16[1024,128]{1,0:T(8,128)(2,1)S(1)}, u32[]{:S(2)}, u32[]{:S(2)}) collective-permute-start(bf16[1024,128]{1,0:T(8,128)(2,1)S(1)} %shard_map.93.refs_0_), channel_id=1, source_target_pairs={{0,6},{2,0},{4,2},{6,4},{1,7},{3,1},{5,3},{7,5},{8,14},{10,8},{12,... | collective-permute-start | bytes 786440 | tf_op jit(solution)/shard_map/ppermute | solution.py:155
  84.3 2.3 %collective-permute-start.2 = (bf16[1024,128]{1,0:T(8,128)(2,1)S(1)}, bf16[1024,128]{1,0:T(8,128)(2,1)S(1)}, u32[]{:S(2)}, u32[]{:S(2)}) collective-permute-start(bf16[1024,128]{1,0:T(8,128)(2,1)S(1)} %shard_map.93.refs_0_), channel_id=1, source_target_pairs={{0,4},{2,6},{4,0},{6,2},{1,5},{3,7},{5,1},{7,3},{8,12},{10,14},{12... | collective-permute-start | bytes 786440 | tf_op jit(solution)/shard_map/ppermute | solution.py:155
  86.5 6.7 %collective-permute-start.3 = (bf16[1024,128]{1,0:T(8,128)(2,1)S(1)}, bf16[1024,128]{1,0:T(8,128)(2,1)S(1)}, u32[]{:S(2)}, u32[]{:S(2)}) collective-permute-start(bf16[1024,128]{1,0:T(8,128)(2,1)S(1)} %shard_map.93.refs_0_), channel_id=1, source_target_pairs={{0,1},{1,0},{2,3},{3,2},{4,5},{5,4},{6,7},{7,6},{8,9},{9,8},{10,11... | collective-permute-start | bytes 786440 | tf_op jit(solution)/shard_map/ppermute | solution.py:152
  93.2 0.0 collective-permute-done.refs_1_
  93.3 0.0 copy-start.3
  93.3 3.0 %collective-permute-start.4 = (bf16[1024,128]{1,0:T(8,128)(2,1)S(1)}, bf16[1024,128]{1,0:T(8,128)(2,1)S(1)}, u32[]{:S(2)}, u32[]{:S(2)}) collective-permute-start(bf16[1024,128]{1,0:T(8,128)(2,1)S(1)} %collective-permute-done.refs_1_), channel_id=1, source_target_pairs={{0,1},{1,0},{2,3},{3,2},{4,5},{5,4},{6,7},{7,6},{8,9},{9,8},{10,11... | collective-permute-start | bytes 786440 | tf_op jit(solution)/shard_map/ppermute | solution.py:152
  96.3 0.0 collective-permute-done.1.refs_2_
  96.3 0.0 copy-start.4
  96.3 2.5 %collective-permute-start.5 = (bf16[1024,128]{1,0:T(8,128)(2,1)S(1)}, bf16[1024,128]{1,0:T(8,128)(2,1)S(1)}, u32[]{:S(2)}, u32[]{:S(2)}) collective-permute-start(bf16[1024,128]{1,0:T(8,128)(2,1)S(1)} %collective-permute-done.1.refs_2_), channel_id=1, source_target_pairs={{0,1},{1,0},{2,3},{3,2},{4,5},{5,4},{6,7},{7,6},{8,9},{9,8},{10,11... | collective-permute-start | bytes 786440 | tf_op jit(solution)/shard_map/ppermute | solution.py:152
  98.7 0.0 collective-permute-done.2.refs_3_
  98.8 0.0 copy-start.5
  98.8 2.2 %collective-permute-start.6 = (bf16[1024,128]{1,0:T(8,128)(2,1)S(1)}, bf16[1024,128]{1,0:T(8,128)(2,1)S(1)}, u32[]{:S(2)}, u32[]{:S(2)}) collective-permute-start(bf16[1024,128]{1,0:T(8,128)(2,1)S(1)} %collective-permute-done.2.refs_3_), channel_id=1, source_target_pairs={{0,1},{1,0},{2,3},{3,2},{4,5},{5,4},{6,7},{7,6},{8,9},{9,8},{10,11... | collective-permute-start | bytes 786440 | tf_op jit(solution)/shard_map/ppermute | solution.py:152
  102.3 0.0 collective-permute-done.3.refs_4_
  102.3 0.0 copy-start.6
  102.3 0.0 collective-permute-done.4.refs_5_
  102.3 0.0 copy-start.7
  102.3 0.0 collective-permute-done.5.refs_6_
  102.3 0.0 copy-start.8
  102.3 0.0 collective-permute-done.6.refs_7_
  102.4 0.0 copy-start.9
  102.4 0.0 copy-done.1
  102.4 0.0 copy-done.3
  102.4 0.0 copy-done.4
  102.4 0.0 copy-done.5
  102.4 0.6 copy-done.6
  103.0 0.1 copy-done.7
  103.1 0.1 copy-done.8
  103.2 0.1 copy-done.9
  103.4 4.6 %shard_map.94 = (bf16[1024,1024]{1,0:T(8,128)(2,1)}, f32[1024,128]{1,0:T(8,128)}, f32[1024,128]{1,0:T(8,128)}) custom-call(s32[1]{0:T(128)} %bitcast.1.me, s32[8,3,128]{2,1,0:T(4,128)} %copy-done.2, bf16[1024,128]{1,0:T(8,128)(2,1)} %copy-done.1, bf16[1024,128]{1,0:T(8,128)(2,1)} %copy-done.3, bf16[1024,128]{1,0:T(8,128)(2,1)} %copy-done.4, ...), custom_call_target="tpu_custom_call" | custom-call | tf_op jit(solution)/shard_map/pallas_call | solution.py:223
  108.0 0.0 all-gather.2.cloned.1.call-done.weights
  108.0 7.0 %shard_map.95 = bf16[128,2048]{1,0:T(8,128)(2,1)} custom-call(f32[1]{0:T(128)S(6)} %copy.15.stretch, f32[1]{0:T(128)S(6)} %copy.16.shift, bf16[128,2048]{1,0:T(8,128)(2,1)} %bitcast.22, bf16[2048,1024]{1,0:T(8,128)(2,1)} %all-gather.2.cloned.1.call-done.weights, bf16[1024,1024]{1,0:T(8,128)(2,1)} %get-tuple-element.12.img_in, ...), custom_call_target="tpu_custom_call" | custom-call | flops 1073741824 | bytes 4194304 | tf_op jit(solution)/shard_map/pallas_call | solution.py:239
  (3 shorter events, 0.0 us)
Async XLA Ops:
  6.5 30.7 %copy-start = (bf16[256,1408]{1,0:T(8,128)(2,1)S(1)}, bf16[256,1408]{1,0:T(8,128)(2,1)}, u32[]{:S(2)}) copy-start(bf16[256,1408]{1,0:T(8,128)(2,1)} %param.10) | copy-start | bytes 2162692
  6.5 101.5 %all-gather.2.cloned.1.call-start = ((), (), s32[]{:S(2)}) async-start(), calls=%async_computation.3 | async-start | bytes 4259840 | tf_op jit(solution)/shard_map/all_gather | solution.py:171
  8.7 14.8 %all-to-all-start = ((s32[8,3,128]{2,1,0:T(4,128)}), s32[8,3,128]{2,1,0:T(4,128)S(1)}, u32[]{:S(2)}, u32[]{:S(2)}) async-start(s32[8,3,128]{2,1,0:T(4,128)} %shard_map.91), calls=%async_computation | async-start | bytes 32768 | tf_op jit(solution)/shard_map/all_to_all | solution.py:180
  23.4 16.4 %copy-start.2 = (s32[8,3,128]{2,1,0:T(4,128)}, s32[8,3,128]{2,1,0:T(4,128)S(1)}, u32[]{:S(2)}) copy-start(s32[8,3,128]{2,1,0:T(4,128)S(1)} %all-to-all-done.info) | copy-start | bytes 36868
  25.2 27.0 %all-to-all-start.1 = ((bf16[64,24,128]{2,1,0:T(8,128)(2,1)}), bf16[64,24,128]{2,1,0:T(8,128)(2,1)S(1)}, u32[]{:S(2)}, u32[]{:S(2)}) async-start(bf16[64,24,128]{2,1,0:T(8,128)(2,1)} %maximum_maximum_fusion), calls=%async_computation.1 | async-start | bytes 786432 | tf_op jit(solution)/shard_map/all_to_all | solution.py:202
  77.7 24.6 %copy-start.1 = (bf16[1024,128]{1,0:T(8,128)(2,1)}, bf16[1024,128]{1,0:T(8,128)(2,1)S(1)}, u32[]{:S(2)}) copy-start(bf16[1024,128]{1,0:T(8,128)(2,1)S(1)} %shard_map.93.refs_0_) | copy-start | bytes 786436
  77.8 15.5 %collective-permute-start = (bf16[1024,128]{1,0:T(8,128)(2,1)S(1)}, bf16[1024,128]{1,0:T(8,128)(2,1)S(1)}, u32[]{:S(2)}, u32[]{:S(2)}) collective-permute-start(bf16[1024,128]{1,0:T(8,128)(2,1)S(1)} %shard_map.93.refs_0_), channel_id=1, source_target_pairs={{0,2},{2,4},{4,6},{6,0},{1,3},{3,5},{5,7},{7,1},{8,10},{10,12},{12... | collective-permute-start | bytes 786440 | tf_op jit(solution)/shard_map/ppermute | solution.py:155
  79.7 16.6 %collective-permute-start.1 = (bf16[1024,128]{1,0:T(8,128)(2,1)S(1)}, bf16[1024,128]{1,0:T(8,128)(2,1)S(1)}, u32[]{:S(2)}, u32[]{:S(2)}) collective-permute-start(bf16[1024,128]{1,0:T(8,128)(2,1)S(1)} %shard_map.93.refs_0_), channel_id=1, source_target_pairs={{0,6},{2,0},{4,2},{6,4},{1,7},{3,1},{5,3},{7,5},{8,14},{10,8},{12,... | collective-permute-start | bytes 786440 | tf_op jit(solution)/shard_map/ppermute | solution.py:155
  84.3 14.5 %collective-permute-start.2 = (bf16[1024,128]{1,0:T(8,128)(2,1)S(1)}, bf16[1024,128]{1,0:T(8,128)(2,1)S(1)}, u32[]{:S(2)}, u32[]{:S(2)}) collective-permute-start(bf16[1024,128]{1,0:T(8,128)(2,1)S(1)} %shard_map.93.refs_0_), channel_id=1, source_target_pairs={{0,4},{2,6},{4,0},{6,2},{1,5},{3,7},{5,1},{7,3},{8,12},{10,14},{12... | collective-permute-start | bytes 786440 | tf_op jit(solution)/shard_map/ppermute | solution.py:155
  86.5 15.8 %collective-permute-start.3 = (bf16[1024,128]{1,0:T(8,128)(2,1)S(1)}, bf16[1024,128]{1,0:T(8,128)(2,1)S(1)}, u32[]{:S(2)}, u32[]{:S(2)}) collective-permute-start(bf16[1024,128]{1,0:T(8,128)(2,1)S(1)} %shard_map.93.refs_0_), channel_id=1, source_target_pairs={{0,1},{1,0},{2,3},{3,2},{4,5},{5,4},{6,7},{7,6},{8,9},{9,8},{10,11... | collective-permute-start | bytes 786440 | tf_op jit(solution)/shard_map/ppermute | solution.py:152
  93.3 9.1 %copy-start.3 = (bf16[1024,128]{1,0:T(8,128)(2,1)}, bf16[1024,128]{1,0:T(8,128)(2,1)S(1)}, u32[]{:S(2)}) copy-start(bf16[1024,128]{1,0:T(8,128)(2,1)S(1)} %collective-permute-done.refs_1_) | copy-start | bytes 786436
  93.3 9.0 %collective-permute-start.4 = (bf16[1024,128]{1,0:T(8,128)(2,1)S(1)}, bf16[1024,128]{1,0:T(8,128)(2,1)S(1)}, u32[]{:S(2)}, u32[]{:S(2)}) collective-permute-start(bf16[1024,128]{1,0:T(8,128)(2,1)S(1)} %collective-permute-done.refs_1_), channel_id=1, source_target_pairs={{0,1},{1,0},{2,3},{3,2},{4,5},{5,4},{6,7},{7,6},{8,9},{9,8},{10,11... | collective-permute-start | bytes 786440 | tf_op jit(solution)/shard_map/ppermute | solution.py:152
  96.3 6.1 %copy-start.4 = (bf16[1024,128]{1,0:T(8,128)(2,1)}, bf16[1024,128]{1,0:T(8,128)(2,1)S(1)}, u32[]{:S(2)}) copy-start(bf16[1024,128]{1,0:T(8,128)(2,1)S(1)} %collective-permute-done.1.refs_2_) | copy-start | bytes 786436
  96.3 6.1 %collective-permute-start.5 = (bf16[1024,128]{1,0:T(8,128)(2,1)S(1)}, bf16[1024,128]{1,0:T(8,128)(2,1)S(1)}, u32[]{:S(2)}, u32[]{:S(2)}) collective-permute-start(bf16[1024,128]{1,0:T(8,128)(2,1)S(1)} %collective-permute-done.1.refs_2_), channel_id=1, source_target_pairs={{0,1},{1,0},{2,3},{3,2},{4,5},{5,4},{6,7},{7,6},{8,9},{9,8},{10,11... | collective-permute-start | bytes 786440 | tf_op jit(solution)/shard_map/ppermute | solution.py:152
  98.8 3.6 %copy-start.5 = (bf16[1024,128]{1,0:T(8,128)(2,1)}, bf16[1024,128]{1,0:T(8,128)(2,1)S(1)}, u32[]{:S(2)}) copy-start(bf16[1024,128]{1,0:T(8,128)(2,1)S(1)} %collective-permute-done.2.refs_3_) | copy-start | bytes 786436
  98.8 3.6 %collective-permute-start.6 = (bf16[1024,128]{1,0:T(8,128)(2,1)S(1)}, bf16[1024,128]{1,0:T(8,128)(2,1)S(1)}, u32[]{:S(2)}, u32[]{:S(2)}) collective-permute-start(bf16[1024,128]{1,0:T(8,128)(2,1)S(1)} %collective-permute-done.2.refs_3_), channel_id=1, source_target_pairs={{0,1},{1,0},{2,3},{3,2},{4,5},{5,4},{6,7},{7,6},{8,9},{9,8},{10,11... | collective-permute-start | bytes 786440 | tf_op jit(solution)/shard_map/ppermute | solution.py:152
  102.3 0.8 copy-start.6
  102.3 0.8 copy-start.7
  102.3 0.9 copy-start.8
  102.4 1.0 copy-start.9
Sparse Core Ops, SparseCore 0:
  10.4 91.3 all-gather.1

commit v7 on v4

--- a/solution.py
+++ b/solution.py
@@ -10,7 +10,7 @@
 EPS = 1e-06
 LOSS_SCALE = 256.0
 CAP = 2
-HOPS = (0, 2, 3, 1)
+HOPS = (0, 1, 3, 2)
 LANES = 128
 BF = jnp.bfloat16
 F32 = jnp.float32
@@ -91,42 +91,31 @@
     return copies
 
 
-def grad_kernel(members, cores, rows, me, stretch, shift, info, text, weights, *refs):
-    images, (out, img, wt, norms, matches, slopes, img_sems, wt_sems) = refs[:members], refs[members:]
-    img_copies = load_columns(me[0], cores, images, img, img_sems)
-    chunk = wt.shape[0] // wt_sems.shape[0]
-    wt_copies = []
-    for k in range(wt_sems.shape[0]):
-        span = slice(k * chunk, (k + 1) * chunk)
-        wt_copies.append(pltpu.make_async_copy(weights.at[span], wt.at[span], wt_sems.at[k]))
-        wt_copies[k].start()
+def image_kernel(members, cores, me, *refs):
+    images, (img, raw, sems) = refs[:members], refs[members:]
+    for copy in load_columns(me[0], cores, images, raw, sems):
+        copy.wait()
+    for g in range(members):
+        span = slice(g * LANES, (g + 1) * LANES)
+        wide = raw[span, :].astype(F32)
+        inv = lax.rsqrt(jnp.sum(wide * wide, axis=1, keepdims=True) + EPS)
+        img[span, :] = (wide * inv).astype(BF)
+
+
+def grad_kernel(rows, me, stretch, shift, info, text, wt, img, out, slopes):
     gain, offset = stretch[0], shift[0]
     pairs = text.shape[0]
+    same_micro = (iota((pairs, pairs), 0) >= rows) == (iota((pairs, pairs), 1) >= rows)
     own_labels = info[me[0], 2:3, :]
-    for g in range(members):
-        span = slice(g * pairs, (g + 1) * pairs)
-        matches[span, :] = (as_column(info[g, 2:3, :]) == own_labels).astype(F32)
-    for copy in img_copies:
-        copy.wait()
-    for g in range(members):
-        span = slice(g * pairs, (g + 1) * pairs)
-        wide = img[span, :].astype(F32)
-        inv = lax.rsqrt(jnp.sum(wide * wide, axis=1, keepdims=True) + EPS)
-        norms[span, :] = jnp.broadcast_to(inv, (pairs, pairs))
-    raw = jnp.zeros((pairs, wt.shape[1]), F32)
-    for k, copy in enumerate(wt_copies):
-        copy.wait()
-        span = slice(k * chunk, (k + 1) * chunk)
-        raw = raw + dot(text[:, span], wt[span, :], 1, 0)
+    raw = dot(text[...], wt[...], 1, 0)
     inverse = lax.rsqrt(jnp.sum(raw * raw, axis=1, keepdims=True) + EPS)
     unit = raw * inverse
-    similar = dot(img[...], unit.astype(BF), 1, 1)
-    same_micro = (iota((pairs, pairs), 0) >= rows) == (iota((pairs, pairs), 1) >= rows)
-    for g in range(members):
+    unit_bf = unit.astype(BF)
+    for g in range(img.shape[0] // pairs):
         span = slice(g * pairs, (g + 1) * pairs)
-        inv = norms[span, :]
-        logit = gain * inv * similar[span, :] + offset
-        slope = LOSS_SCALE * inv * (jax.nn.sigmoid(logit) - matches[span, :])
+        match = (as_column(info[g, 2:3, :]) == own_labels).astype(F32)
+        logit = gain * dot(img[span, :], unit_bf, 1, 1) + offset
+        slope = LOSS_SCALE * (jax.nn.sigmoid(logit) - match)
         slopes[span, :] = jnp.where(same_micro, slope, 0.0).astype(BF)
     grad = gain * dot(slopes[...], img[...], 0, 0)
     grad = grad - unit * jnp.sum(unit * grad, axis=1, keepdims=True)
@@ -208,25 +197,26 @@
         )(slot, fetched.reshape(owners * slots, width))
 
         image_pieces = whole_group(mine)
+        images = members * pairs
+        img = pl.pallas_call(
+            functools.partial(image_kernel, members, nc),
+            out_shape=jax.ShapeDtypeStruct((images, emb), BF),
+            in_specs=[SMEM] + [ANY] * members,
+            out_specs=VMEM,
+            scratch_shapes=[pltpu.VMEM((images, emb), BF), pltpu.SemaphoreType.DMA((members,))],
+            compiler_params=SMALL,
+        )(me.reshape(1), *image_pieces)
         out = pl.pallas_call(
-            functools.partial(grad_kernel, members, nc, rows),
+            functools.partial(grad_kernel, rows),
             out_shape=jax.ShapeDtypeStruct((pairs, d_txt), BF),
-            in_specs=[SMEM, SMEM, SMEM, VMEM, VMEM] + [ANY] * (members + 1),
-            out_specs=VMEM,
-            scratch_shapes=[
-                pltpu.VMEM((members * pairs, emb), BF),
-                pltpu.VMEM((d_txt, emb), BF),
-                pltpu.VMEM((members * pairs, pairs), F32),
-                pltpu.VMEM((members * pairs, pairs), F32),
-                pltpu.VMEM((members * pairs, pairs), BF),
-                pltpu.SemaphoreType.DMA((members,)),
-                pltpu.SemaphoreType.DMA((4,)),
-            ],
-            compiler_params=LARGE,
+            in_specs=[SMEM, SMEM, SMEM] + [VMEM] * 4,
+            out_specs=VMEM,
+            scratch_shapes=[pltpu.VMEM((images, pairs), BF)],
+            compiler_params=SMALL,
             cost_estimate=pl.CostEstimate(
                 flops=4 * pairs * d_txt * emb, bytes_accessed=2 * d_txt * emb, transcendentals=0
             ),
-        )(me.reshape(1), stretch, offset, info, text.reshape(pairs, d_txt), wt_all, *image_pieces)
+        )(me.reshape(1), stretch, offset, info, text.reshape(pairs, d_txt), wt_all, img)
         return out.reshape(micro, rows, d_txt)
 
     return local

time: 122 us -> 119 us (0.975)
  Pallas kernels: 12.9 us -> 8.98 us
  local copies, waits for them, and re-layouts: 1.84 us -> 3.14 us
    pallas_call x1 -> x2, Pallas kernels: 9.54 us -> 5.57 us  [the longest x1 4.21 us: local(): pl.pallas_call(functools.partial(grad_kernel, rows), out_shape=jax.ShapeD...]
    unnamed x20 -> x6, local copies, waits for them, and re-layouts: 0.88 us -> 2.19 us
  transfers between devices with their start and end apart: 10 -> 10, of which waited for: 2 -> 2; matrix products, arithmetic and copies ran while one was open for 5% -> 5% of each run, Pallas kernels for 3% -> 4%
where the time goes in v7:
time: 119 us; the launch traced here: 117 us
  starting transfers between devices  45.2 us (38%)
  blocking collectives  23.1 us (19%)
  waiting for transfers between devices  17.1 us (14%)
  between operations  14.9 us (13%)
  Pallas kernels  8.98 us (8%)
  matrix products  3.55 us (3%)
  local copies, waits for them, and re-layouts  3.14 us (3%)
    all_to_all x1, blocking collectives, local(): lax.all_to_all(served, ('z', 'y'), split_axis=0, concat_axis=0, tiled=True)  23.1 us
    ppermute x4, starting transfers between devices, swap(): return lax.ppermute(v, 'core', [(i, nc - 1 - i) for i in range(nc)])  14.4 us
    all_to_all x1, waiting for transfers between devices, local(): lax.all_to_all(sent, ('z', 'y'), split_axis=0, concat_axis=0, tiled=True)  12.4 us
    all_to_all x1, starting transfers between devices, local(): lax.all_to_all(sent, ('z', 'y'), split_axis=0, concat_axis=0, tiled=True)  12 us
    all_to_all x1, starting transfers between devices, local(): lax.all_to_all(info, ('x', 'core'), split_axis=0, concat_axis=0, tiled=True)  10.1 us
    ppermute x3, starting transfers between devices, shift(): return lax.ppermute(v, 'x', [(i, (i + by) % nx) for i in range(nx)])  8.69 us
    pallas_call x1, Pallas kernels, local(): pl.pallas_call(functools.partial(grad_kernel, rows), out_shape=jax.ShapeD...  4.21 us
    all_to_all x1, waiting for transfers between devices, local(): lax.all_to_all(info, ('x', 'core'), split_axis=0, concat_axis=0, tiled=True)  3.9 us
  transfers between devices with their start and end apart: 10, of which 2 were waited for; matrix products, arithmetic and copies ran while one was open for 5% of the time, Pallas kernels for 4%

profile of v7, /device:TPU:1, one launch (start us, length us, event | category | flops | bytes accessed | tf_op | source)
XLA Modules:
  0.0 116.9 jit_solution(7304292275926390827)
XLA Ops:
  6.5 0.0 copy-start
  6.5 0.0 all-gather.2.cloned.1.call-start
  6.5 0.7 all-gather.2.cloned.1.call-update
  7.3 1.4 %shard_map.91 = s32[8,3,128]{2,1,0:T(4,128)} custom-call(s32[2,1,64]{2,1,0:T(1,128)} %bitcast.24, s32[2,64]{1,0:T(2,128)} %entry.1, s32[2,64]{1,0:T(2,128)} %labels.1), custom_call_target="tpu_custom_call" | custom-call | tf_op jit(solution)/shard_map/pallas_call | solution.py:151
  8.7 10.1 %all-to-all-start = ((s32[8,3,128]{2,1,0:T(4,128)}), s32[8,3,128]{2,1,0:T(4,128)S(1)}, u32[]{:S(2)}, u32[]{:S(2)}) async-start(s32[8,3,128]{2,1,0:T(4,128)} %shard_map.91), calls=%async_computation | async-start | bytes 32768 | tf_op jit(solution)/shard_map/all_to_all | solution.py:158
  18.8 0.7 constant_dynamic-slice_fusion
  19.5 0.1 pad.2.clone
  19.5 3.9 %all-to-all-done.info = s32[8,3,128]{2,1,0:T(4,128)S(1)} async-done(((s32[8,3,128]{2,1,0:T(4,128)}), s32[8,3,128]{2,1,0:T(4,128)S(1)}, u32[]{:S(2)}, u32[]{:S(2)}) %all-to-all-start) | async-done | bytes 12320 | tf_op jit(solution)/shard_map/all_to_all | solution.py:158
  23.4 0.7 shard_map.92
  24.1 0.1 copy.14
  24.2 0.1 broadcast_in_dim.6
  24.2 0.9 maximum_maximum_fusion
  25.2 12.0 %all-to-all-start.1 = ((bf16[64,24,128]{2,1,0:T(8,128)(2,1)}), bf16[64,24,128]{2,1,0:T(8,128)(2,1)S(1)}, u32[]{:S(2)}, u32[]{:S(2)}) async-start(bf16[64,24,128]{2,1,0:T(8,128)(2,1)} %maximum_maximum_fusion), calls=%async_computation.1 | async-start | bytes 786432 | tf_op jit(solution)/shard_map/all_to_all | solution.py:180
  37.2 0.0 copy-done
  37.2 2.6 %fusion.5.clone.6 = bf16[1536,256]{1,0:T(8,128)(2,1)S(1)} fusion(bf16[256,1408]{1,0:T(8,128)(2,1)S(1)} %copy-done, s32[1408]{0:T(1024)S(1)} %get-tuple-element.10, s32[1408]{0:T(1024)S(1)} %get-tuple-element.11, s32[1408]{0:T(1024)S(1)} %get-tuple-element.9, s32[1408]{0:T(1024)S(1)} %get-tuple-element.12, ...), kind=kOutput, calls=%fused_computation.5.clone.clone.clone.clone.clone.1 | convolution fusion | flops 1120665600 | bytes 1532672 | tf_op jit(solution)/shard_map/dot_general | solution.py:26
  39.8 0.0 copy-start.2
  39.8 12.4 %all-to-all-done.1 = bf16[64,24,128]{2,1,0:T(8,128)(2,1)S(1)} async-done(((bf16[64,24,128]{2,1,0:T(8,128)(2,1)}), bf16[64,24,128]{2,1,0:T(8,128)(2,1)S(1)}, u32[]{:S(2)}, u32[]{:S(2)}) %all-to-all-start.1) | async-done | bytes 393248 | tf_op jit(solution)/shard_map/all_to_all | solution.py:180
  52.3 0.1 fusion.15
  52.4 0.1 reshape.33
  52.5 0.4 fusion.11
  52.9 0.5 convolution_convert_fusion
  53.4 23.1 %all_to_all.15 = bf16[64,32,128]{2,1,0:T(8,128)(2,1)S(1)} all-to-all(bf16[64,32,128]{2,1,0:T(8,128)(2,1)S(1)} %bitcast.23), channel_id=1, replica_groups=mesh['z'=8,'y'=8,'x'=4,'core'=2] {'z','y'}, dimensions={0} | all-to-all | bytes 1048576 | tf_op jit(solution)/shard_map/all_to_all | solution.py:190
  76.5 1.3 %shard_map.93.refs_0_ = bf16[1024,128]{1,0:T(8,128)(2,1)S(1)} custom-call(s32[8,128]{1,0:T(8,128)S(1)} %get-tuple-element.7.slot, bf16[2048,128]{1,0:T(8,128)(2,1)S(1)} %bitcast.19), custom_call_target="tpu_custom_call" | custom-call | tf_op jit(solution)/shard_map/pallas_call | solution.py:191
  77.8 1.9 %collective-permute-start = (bf16[1024,128]{1,0:T(8,128)(2,1)S(1)}, bf16[1024,128]{1,0:T(8,128)(2,1)S(1)}, u32[]{:S(2)}, u32[]{:S(2)}) collective-permute-start(bf16[1024,128]{1,0:T(8,128)(2,1)S(1)} %shard_map.93.refs_0_), channel_id=1, source_target_pairs={{0,2},{2,4},{4,6},{6,0},{1,3},{3,5},{5,7},{7,1},{8,10},{10,12},{12... | collective-permute-start | bytes 786440 | tf_op jit(solution)/shard_map/ppermute | solution.py:133
  79.7 4.6 %collective-permute-start.1 = (bf16[1024,128]{1,0:T(8,128)(2,1)S(1)}, bf16[1024,128]{1,0:T(8,128)(2,1)S(1)}, u32[]{:S(2)}, u32[]{:S(2)}) collective-permute-start(bf16[1024,128]{1,0:T(8,128)(2,1)S(1)} %shard_map.93.refs_0_), channel_id=1, source_target_pairs={{0,6},{2,0},{4,2},{6,4},{1,7},{3,1},{5,3},{7,5},{8,14},{10,8},{12,... | collective-permute-start | bytes 786440 | tf_op jit(solution)/shard_map/ppermute | solution.py:133
  84.3 2.2 %collective-permute-start.2 = (bf16[1024,128]{1,0:T(8,128)(2,1)S(1)}, bf16[1024,128]{1,0:T(8,128)(2,1)S(1)}, u32[]{:S(2)}, u32[]{:S(2)}) collective-permute-start(bf16[1024,128]{1,0:T(8,128)(2,1)S(1)} %shard_map.93.refs_0_), channel_id=1, source_target_pairs={{0,4},{2,6},{4,0},{6,2},{1,5},{3,7},{5,1},{7,3},{8,12},{10,14},{12... | collective-permute-start | bytes 786440 | tf_op jit(solution)/shard_map/ppermute | solution.py:133
  86.5 6.7 %collective-permute-start.3 = (bf16[1024,128]{1,0:T(8,128)(2,1)S(1)}, bf16[1024,128]{1,0:T(8,128)(2,1)S(1)}, u32[]{:S(2)}, u32[]{:S(2)}) collective-permute-start(bf16[1024,128]{1,0:T(8,128)(2,1)S(1)} %shard_map.93.refs_0_), channel_id=1, source_target_pairs={{0,1},{1,0},{2,3},{3,2},{4,5},{5,4},{6,7},{7,6},{8,9},{9,8},{10,11... | collective-permute-start | bytes 786440 | tf_op jit(solution)/shard_map/ppermute | solution.py:130
  93.2 0.0 collective-permute-done.refs_1_
  93.2 3.0 %collective-permute-start.4 = (bf16[1024,128]{1,0:T(8,128)(2,1)S(1)}, bf16[1024,128]{1,0:T(8,128)(2,1)S(1)}, u32[]{:S(2)}, u32[]{:S(2)}) collective-permute-start(bf16[1024,128]{1,0:T(8,128)(2,1)S(1)} %collective-permute-done.refs_1_), channel_id=1, source_target_pairs={{0,1},{1,0},{2,3},{3,2},{4,5},{5,4},{6,7},{7,6},{8,9},{9,8},{10,11... | collective-permute-start | bytes 786440 | tf_op jit(solution)/shard_map/ppermute | solution.py:130
  96.2 0.0 collective-permute-done.1.refs_2_
  96.2 2.5 %collective-permute-start.5 = (bf16[1024,128]{1,0:T(8,128)(2,1)S(1)}, bf16[1024,128]{1,0:T(8,128)(2,1)S(1)}, u32[]{:S(2)}, u32[]{:S(2)}) collective-permute-start(bf16[1024,128]{1,0:T(8,128)(2,1)S(1)} %collective-permute-done.1.refs_2_), channel_id=1, source_target_pairs={{0,1},{1,0},{2,3},{3,2},{4,5},{5,4},{6,7},{7,6},{8,9},{9,8},{10,11... | collective-permute-start | bytes 786440 | tf_op jit(solution)/shard_map/ppermute | solution.py:130
  98.7 0.0 collective-permute-done.2.refs_3_
  98.7 2.2 %collective-permute-start.6 = (bf16[1024,128]{1,0:T(8,128)(2,1)S(1)}, bf16[1024,128]{1,0:T(8,128)(2,1)S(1)}, u32[]{:S(2)}, u32[]{:S(2)}) collective-permute-start(bf16[1024,128]{1,0:T(8,128)(2,1)S(1)} %collective-permute-done.2.refs_3_), channel_id=1, source_target_pairs={{0,1},{1,0},{2,3},{3,2},{4,5},{5,4},{6,7},{7,6},{8,9},{9,8},{10,11... | collective-permute-start | bytes 786440 | tf_op jit(solution)/shard_map/ppermute | solution.py:130
  102.2 0.0 collective-permute-done.3.refs_4_
  102.3 0.0 collective-permute-done.4.refs_5_
  102.3 0.0 collective-permute-done.5.refs_6_
  102.3 0.0 collective-permute-done.6.refs_7_
  102.3 1.4 %shard_map.94.img = bf16[1024,1024]{1,0:T(8,128)(2,1)S(1)} custom-call(s32[1]{0:T(128)} %bitcast.me, bf16[1024,128]{1,0:T(8,128)(2,1)S(1)} %shard_map.93.refs_0_, bf16[1024,128]{1,0:T(8,128)(2,1)S(1)} %collective-permute-done.refs_1_, bf16[1024,128]{1,0:T(8,128)(2,1)S(1)} %collective-permute-done.1.refs_2_, ...), custom_call_target="tpu_custom_call" | custom-call | tf_op jit(solution)/shard_map/pallas_call | solution.py:201
  103.7 0.0 all-gather.2.cloned.1.call-done.wt
  103.7 0.0 copy-done.2
  103.7 0.0 copy-start.1
  103.7 2.2 %copy-done.1 = bf16[2048,1024]{1,0:T(8,128)(2,1)S(1)} copy-done((bf16[2048,1024]{1,0:T(8,128)(2,1)S(1)}, bf16[2048,1024]{1,0:T(8,128)(2,1)}, u32[]{:S(2)}) %copy-start.1) | copy-done | bytes 4194328
  105.9 4.2 %shard_map.95 = bf16[128,2048]{1,0:T(8,128)(2,1)} custom-call(s32[1]{0:T(128)} %bitcast.me, f32[1]{0:T(128)S(6)} %copy.15.stretch, f32[1]{0:T(128)S(6)} %copy.16.shift, s32[8,3,128]{2,1,0:T(4,128)S(1)} %all-to-all-done.info, bf16[128,2048]{1,0:T(8,128)(2,1)S(1)} %bitcast.20, bf16[2048,1024]{1,0:T(8,128)(2,1)S(1)} %copy-done.1, ...), custom_call_target="tpu_custom_call" | custom-call | flops 1073741824 | bytes 4194304 | tf_op jit(solution)/shard_map/pallas_call | solution.py:209
  (3 shorter events, 0.0 us)
Async XLA Ops:
  6.5 30.6 %copy-start = (bf16[256,1408]{1,0:T(8,128)(2,1)S(1)}, bf16[256,1408]{1,0:T(8,128)(2,1)}, u32[]{:S(2)}) copy-start(bf16[256,1408]{1,0:T(8,128)(2,1)} %param.10) | copy-start | bytes 2162692
  6.5 97.1 %all-gather.2.cloned.1.call-start = ((), (), s32[]{:S(2)}) async-start(), calls=%async_computation.3 | async-start | bytes 4259840 | tf_op jit(solution)/shard_map/all_gather | solution.py:149
  8.7 14.8 %all-to-all-start = ((s32[8,3,128]{2,1,0:T(4,128)}), s32[8,3,128]{2,1,0:T(4,128)S(1)}, u32[]{:S(2)}, u32[]{:S(2)}) async-start(s32[8,3,128]{2,1,0:T(4,128)} %shard_map.91), calls=%async_computation | async-start | bytes 32768 | tf_op jit(solution)/shard_map/all_to_all | solution.py:158
  25.2 27.1 %all-to-all-start.1 = ((bf16[64,24,128]{2,1,0:T(8,128)(2,1)}), bf16[64,24,128]{2,1,0:T(8,128)(2,1)S(1)}, u32[]{:S(2)}, u32[]{:S(2)}) async-start(bf16[64,24,128]{2,1,0:T(8,128)(2,1)} %maximum_maximum_fusion), calls=%async_computation.1 | async-start | bytes 786432 | tf_op jit(solution)/shard_map/all_to_all | solution.py:180
  39.8 63.9 %copy-start.2 = (bf16[2,64,2048]{2,1,0:T(8,128)(2,1)S(1)}, bf16[2,64,2048]{2,1,0:T(8,128)(2,1)}, u32[]{:S(2)}) copy-start(bf16[2,64,2048]{2,1,0:T(8,128)(2,1)} %param.9) | copy-start | bytes 1572868
  77.8 15.4 %collective-permute-start = (bf16[1024,128]{1,0:T(8,128)(2,1)S(1)}, bf16[1024,128]{1,0:T(8,128)(2,1)S(1)}, u32[]{:S(2)}, u32[]{:S(2)}) collective-permute-start(bf16[1024,128]{1,0:T(8,128)(2,1)S(1)} %shard_map.93.refs_0_), channel_id=1, source_target_pairs={{0,2},{2,4},{4,6},{6,0},{1,3},{3,5},{5,7},{7,1},{8,10},{10,12},{12... | collective-permute-start | bytes 786440 | tf_op jit(solution)/shard_map/ppermute | solution.py:133
  79.7 16.5 %collective-permute-start.1 = (bf16[1024,128]{1,0:T(8,128)(2,1)S(1)}, bf16[1024,128]{1,0:T(8,128)(2,1)S(1)}, u32[]{:S(2)}, u32[]{:S(2)}) collective-permute-start(bf16[1024,128]{1,0:T(8,128)(2,1)S(1)} %shard_map.93.refs_0_), channel_id=1, source_target_pairs={{0,6},{2,0},{4,2},{6,4},{1,7},{3,1},{5,3},{7,5},{8,14},{10,8},{12,... | collective-permute-start | bytes 786440 | tf_op jit(solution)/shard_map/ppermute | solution.py:133
  84.3 14.4 %collective-permute-start.2 = (bf16[1024,128]{1,0:T(8,128)(2,1)S(1)}, bf16[1024,128]{1,0:T(8,128)(2,1)S(1)}, u32[]{:S(2)}, u32[]{:S(2)}) collective-permute-start(bf16[1024,128]{1,0:T(8,128)(2,1)S(1)} %shard_map.93.refs_0_), channel_id=1, source_target_pairs={{0,4},{2,6},{4,0},{6,2},{1,5},{3,7},{5,1},{7,3},{8,12},{10,14},{12... | collective-permute-start | bytes 786440 | tf_op jit(solution)/shard_map/ppermute | solution.py:133
  86.5 15.7 %collective-permute-start.3 = (bf16[1024,128]{1,0:T(8,128)(2,1)S(1)}, bf16[1024,128]{1,0:T(8,128)(2,1)S(1)}, u32[]{:S(2)}, u32[]{:S(2)}) collective-permute-start(bf16[1024,128]{1,0:T(8,128)(2,1)S(1)} %shard_map.93.refs_0_), channel_id=1, source_target_pairs={{0,1},{1,0},{2,3},{3,2},{4,5},{5,4},{6,7},{7,6},{8,9},{9,8},{10,11... | collective-permute-start | bytes 786440 | tf_op jit(solution)/shard_map/ppermute | solution.py:130
  93.2 9.0 %collective-permute-start.4 = (bf16[1024,128]{1,0:T(8,128)(2,1)S(1)}, bf16[1024,128]{1,0:T(8,128)(2,1)S(1)}, u32[]{:S(2)}, u32[]{:S(2)}) collective-permute-start(bf16[1024,128]{1,0:T(8,128)(2,1)S(1)} %collective-permute-done.refs_1_), channel_id=1, source_target_pairs={{0,1},{1,0},{2,3},{3,2},{4,5},{5,4},{6,7},{7,6},{8,9},{9,8},{10,11... | collective-permute-start | bytes 786440 | tf_op jit(solution)/shard_map/ppermute | solution.py:130
  96.2 6.0 %collective-permute-start.5 = (bf16[1024,128]{1,0:T(8,128)(2,1)S(1)}, bf16[1024,128]{1,0:T(8,128)(2,1)S(1)}, u32[]{:S(2)}, u32[]{:S(2)}) collective-permute-start(bf16[1024,128]{1,0:T(8,128)(2,1)S(1)} %collective-permute-done.1.refs_2_), channel_id=1, source_target_pairs={{0,1},{1,0},{2,3},{3,2},{4,5},{5,4},{6,7},{7,6},{8,9},{9,8},{10,11... | collective-permute-start | bytes 786440 | tf_op jit(solution)/shard_map/ppermute | solution.py:130
  98.7 3.5 %collective-permute-start.6 = (bf16[1024,128]{1,0:T(8,128)(2,1)S(1)}, bf16[1024,128]{1,0:T(8,128)(2,1)S(1)}, u32[]{:S(2)}, u32[]{:S(2)}) collective-permute-start(bf16[1024,128]{1,0:T(8,128)(2,1)S(1)} %collective-permute-done.2.refs_3_), channel_id=1, source_target_pairs={{0,1},{1,0},{2,3},{3,2},{4,5},{5,4},{6,7},{7,6},{8,9},{9,8},{10,11... | collective-permute-start | bytes 786440 | tf_op jit(solution)/shard_map/ppermute | solution.py:130
  103.7 2.2 %copy-start.1 = (bf16[2048,1024]{1,0:T(8,128)(2,1)S(1)}, bf16[2048,1024]{1,0:T(8,128)(2,1)}, u32[]{:S(2)}) copy-start(bf16[2048,1024]{1,0:T(8,128)(2,1)} %all-gather.2.cloned.1.call-done.wt) | copy-start | bytes 12582916
Sparse Core Ops, SparseCore 0:
  10.4 91.8 all-gather.1

commit v8 on v7

--- a/solution.py
+++ b/solution.py
@@ -19,6 +19,7 @@
 SMEM = pl.BlockSpec(memory_space=pltpu.SMEM)
 ANY = pl.BlockSpec(memory_space=pl.ANY)
 SMALL = pltpu.CompilerParams(vmem_limit_bytes=16 * 1024 * 1024)
+LAST = pltpu.CompilerParams(vmem_limit_bytes=48 * 1024 * 1024)
 LARGE = pltpu.CompilerParams(vmem_limit_bytes=58 * 1024 * 1024)
 
 
@@ -102,12 +103,20 @@
         img[span, :] = (wide * inv).astype(BF)
 
 
-def grad_kernel(rows, me, stretch, shift, info, text, wt, img, out, slopes):
+def grad_kernel(rows, me, stretch, shift, info, text, img, weights, out, wt, slopes, sems):
+    chunk = wt.shape[0] // sems.shape[0]
+    spans = [slice(k * chunk, (k + 1) * chunk) for k in range(sems.shape[0])]
+    copies = [pltpu.make_async_copy(weights.at[p], wt.at[p], sems.at[k]) for k, p in enumerate(spans)]
+    for copy in copies:
+        copy.start()
     gain, offset = stretch[0], shift[0]
     pairs = text.shape[0]
     same_micro = (iota((pairs, pairs), 0) >= rows) == (iota((pairs, pairs), 1) >= rows)
     own_labels = info[me[0], 2:3, :]
-    raw = dot(text[...], wt[...], 1, 0)
+    raw = jnp.zeros((pairs, wt.shape[1]), F32)
+    for copy, span in zip(copies, spans):
+        copy.wait()
+        raw = raw + dot(text[:, span], wt[span, :], 1, 0)
     inverse = lax.rsqrt(jnp.sum(raw * raw, axis=1, keepdims=True) + EPS)
     unit = raw * inverse
     unit_bf = unit.astype(BF)
@@ -209,14 +218,18 @@
         out = pl.pallas_call(
             functools.partial(grad_kernel, rows),
             out_shape=jax.ShapeDtypeStruct((pairs, d_txt), BF),
-            in_specs=[SMEM, SMEM, SMEM] + [VMEM] * 4,
-            out_specs=VMEM,
-            scratch_shapes=[pltpu.VMEM((images, pairs), BF)],
-            compiler_params=SMALL,
+            in_specs=[SMEM, SMEM, SMEM] + [VMEM] * 3 + [ANY],
+            out_specs=VMEM,
+            scratch_shapes=[
+                pltpu.VMEM((d_txt, emb), BF),
+                pltpu.VMEM((images, pairs), BF),
+                pltpu.SemaphoreType.DMA((4,)),
+            ],
+            compiler_params=LAST,
             cost_estimate=pl.CostEstimate(
                 flops=4 * pairs * d_txt * emb, bytes_accessed=2 * d_txt * emb, transcendentals=0
             ),
-        )(me.reshape(1), stretch, offset, info, text.reshape(pairs, d_txt), wt_all, img)
+        )(me.reshape(1), stretch, offset, info, text.reshape(pairs, d_txt), img, wt_all)
         return out.reshape(micro, rows, d_txt)
 
     return local

time: 119 us -> 119 us (level)
  local copies, waits for them, and re-layouts: 3.14 us -> 0.96 us
  Pallas kernels: 8.98 us -> 10.8 us
    unnamed x6 -> x4, local copies, waits for them, and re-layouts: 2.19 us -> 0.01 us
    pallas_call x1, Pallas kernels: 4.21 us -> 6.01 us  [local(): pl.pallas_call(functools.partial(grad_kernel, rows), out_shape=jax.ShapeD...]
where the time goes in v8:
time: 119 us; the launch traced here: 117 us
  starting transfers between devices  45.2 us (38%)
  blocking collectives  23.1 us (19%)
  waiting for transfers between devices  17.1 us (14%)
  between operations  14.9 us (13%)
  Pallas kernels  10.8 us (9%)
  matrix products  3.55 us (3%)
    all_to_all x1, blocking collectives, local(): lax.all_to_all(served, ('z', 'y'), split_axis=0, concat_axis=0, tiled=True)  23.1 us
    ppermute x4, starting transfers between devices, swap(): return lax.ppermute(v, 'core', [(i, nc - 1 - i) for i in range(nc)])  14.4 us
    all_to_all x1, waiting for transfers between devices, local(): lax.all_to_all(sent, ('z', 'y'), split_axis=0, concat_axis=0, tiled=True)  12.4 us
    all_to_all x1, starting transfers between devices, local(): lax.all_to_all(sent, ('z', 'y'), split_axis=0, concat_axis=0, tiled=True)  12 us
    all_to_all x1, starting transfers between devices, local(): lax.all_to_all(info, ('x', 'core'), split_axis=0, concat_axis=0, tiled=True)  10.1 us
    ppermute x3, starting transfers between devices, shift(): return lax.ppermute(v, 'x', [(i, (i + by) % nx) for i in range(nx)])  8.69 us
    pallas_call x1, Pallas kernels, local(): pl.pallas_call(functools.partial(grad_kernel, rows), out_shape=jax.ShapeD...  6.01 us
    all_to_all x1, waiting for transfers between devices, local(): lax.all_to_all(info, ('x', 'core'), split_axis=0, concat_axis=0, tiled=True)  3.9 us
  transfers between devices with their start and end apart: 10, of which 2 were waited for; matrix products, arithmetic and copies ran while one was open for 5% of the time, Pallas kernels for 4%

profile of v8, /device:TPU:1, one launch (start us, length us, event | category | flops | bytes accessed | tf_op | source)
XLA Modules:
  0.0 116.6 jit_solution(5685170936237820975)
XLA Ops:
  6.5 0.0 copy-start
  6.5 0.0 all-gather.2.cloned.1.call-start
  6.5 0.7 all-gather.2.cloned.1.call-update
  7.3 1.4 %shard_map.91 = s32[8,3,128]{2,1,0:T(4,128)} custom-call(s32[2,1,64]{2,1,0:T(1,128)} %bitcast.24, s32[2,64]{1,0:T(2,128)} %entry.1, s32[2,64]{1,0:T(2,128)} %labels.1), custom_call_target="tpu_custom_call" | custom-call | tf_op jit(solution)/shard_map/pallas_call | solution.py:160
  8.7 10.1 %all-to-all-start = ((s32[8,3,128]{2,1,0:T(4,128)}), s32[8,3,128]{2,1,0:T(4,128)S(1)}, u32[]{:S(2)}, u32[]{:S(2)}) async-start(s32[8,3,128]{2,1,0:T(4,128)} %shard_map.91), calls=%async_computation | async-start | bytes 32768 | tf_op jit(solution)/shard_map/all_to_all | solution.py:167
  18.8 0.7 constant_dynamic-slice_fusion
  19.5 0.1 pad.2.clone
  19.5 3.9 %all-to-all-done.info = s32[8,3,128]{2,1,0:T(4,128)S(1)} async-done(((s32[8,3,128]{2,1,0:T(4,128)}), s32[8,3,128]{2,1,0:T(4,128)S(1)}, u32[]{:S(2)}, u32[]{:S(2)}) %all-to-all-start) | async-done | bytes 12320 | tf_op jit(solution)/shard_map/all_to_all | solution.py:167
  23.4 0.7 shard_map.92
  24.1 0.1 copy.14
  24.2 0.1 broadcast_in_dim.6
  24.2 0.9 maximum_maximum_fusion
  25.2 12.0 %all-to-all-start.1 = ((bf16[64,24,128]{2,1,0:T(8,128)(2,1)}), bf16[64,24,128]{2,1,0:T(8,128)(2,1)S(1)}, u32[]{:S(2)}, u32[]{:S(2)}) async-start(bf16[64,24,128]{2,1,0:T(8,128)(2,1)} %maximum_maximum_fusion), calls=%async_computation.1 | async-start | bytes 786432 | tf_op jit(solution)/shard_map/all_to_all | solution.py:189
  37.2 0.0 copy-done
  37.2 2.6 %fusion.5.clone.6 = bf16[1536,256]{1,0:T(8,128)(2,1)S(1)} fusion(bf16[256,1408]{1,0:T(8,128)(2,1)S(1)} %copy-done, s32[1408]{0:T(1024)S(1)} %get-tuple-element.10, s32[1408]{0:T(1024)S(1)} %get-tuple-element.11, s32[1408]{0:T(1024)S(1)} %get-tuple-element.9, s32[1408]{0:T(1024)S(1)} %get-tuple-element.12, ...), kind=kOutput, calls=%fused_computation.5.clone.clone.clone.clone.clone.1 | convolution fusion | flops 1120665600 | bytes 1532672 | tf_op jit(solution)/shard_map/dot_general | solution.py:27
  39.8 0.0 copy-start.1
  39.8 12.4 %all-to-all-done.1 = bf16[64,24,128]{2,1,0:T(8,128)(2,1)S(1)} async-done(((bf16[64,24,128]{2,1,0:T(8,128)(2,1)}), bf16[64,24,128]{2,1,0:T(8,128)(2,1)S(1)}, u32[]{:S(2)}, u32[]{:S(2)}) %all-to-all-start.1) | async-done | bytes 393248 | tf_op jit(solution)/shard_map/all_to_all | solution.py:189
  52.3 0.1 fusion.15
  52.4 0.1 reshape.33
  52.5 0.4 fusion.11
  52.9 0.5 convolution_convert_fusion
  53.4 23.1 %all_to_all.15 = bf16[64,32,128]{2,1,0:T(8,128)(2,1)S(1)} all-to-all(bf16[64,32,128]{2,1,0:T(8,128)(2,1)S(1)} %bitcast.23), channel_id=1, replica_groups=mesh['z'=8,'y'=8,'x'=4,'core'=2] {'z','y'}, dimensions={0} | all-to-all | bytes 1048576 | tf_op jit(solution)/shard_map/all_to_all | solution.py:199
  76.5 1.3 %shard_map.93.refs_0_ = bf16[1024,128]{1,0:T(8,128)(2,1)S(1)} custom-call(s32[8,128]{1,0:T(8,128)S(1)} %get-tuple-element.7.slot, bf16[2048,128]{1,0:T(8,128)(2,1)S(1)} %bitcast.19), custom_call_target="tpu_custom_call" | custom-call | tf_op jit(solution)/shard_map/pallas_call | solution.py:200
  77.8 1.9 %collective-permute-start = (bf16[1024,128]{1,0:T(8,128)(2,1)S(1)}, bf16[1024,128]{1,0:T(8,128)(2,1)S(1)}, u32[]{:S(2)}, u32[]{:S(2)}) collective-permute-start(bf16[1024,128]{1,0:T(8,128)(2,1)S(1)} %shard_map.93.refs_0_), channel_id=1, source_target_pairs={{0,2},{2,4},{4,6},{6,0},{1,3},{3,5},{5,7},{7,1},{8,10},{10,12},{12... | collective-permute-start | bytes 786440 | tf_op jit(solution)/shard_map/ppermute | solution.py:142
  79.7 4.6 %collective-permute-start.1 = (bf16[1024,128]{1,0:T(8,128)(2,1)S(1)}, bf16[1024,128]{1,0:T(8,128)(2,1)S(1)}, u32[]{:S(2)}, u32[]{:S(2)}) collective-permute-start(bf16[1024,128]{1,0:T(8,128)(2,1)S(1)} %shard_map.93.refs_0_), channel_id=1, source_target_pairs={{0,6},{2,0},{4,2},{6,4},{1,7},{3,1},{5,3},{7,5},{8,14},{10,8},{12,... | collective-permute-start | bytes 786440 | tf_op jit(solution)/shard_map/ppermute | solution.py:142
  84.3 2.2 %collective-permute-start.2 = (bf16[1024,128]{1,0:T(8,128)(2,1)S(1)}, bf16[1024,128]{1,0:T(8,128)(2,1)S(1)}, u32[]{:S(2)}, u32[]{:S(2)}) collective-permute-start(bf16[1024,128]{1,0:T(8,128)(2,1)S(1)} %shard_map.93.refs_0_), channel_id=1, source_target_pairs={{0,4},{2,6},{4,0},{6,2},{1,5},{3,7},{5,1},{7,3},{8,12},{10,14},{12... | collective-permute-start | bytes 786440 | tf_op jit(solution)/shard_map/ppermute | solution.py:142
  86.5 6.7 %collective-permute-start.3 = (bf16[1024,128]{1,0:T(8,128)(2,1)S(1)}, bf16[1024,128]{1,0:T(8,128)(2,1)S(1)}, u32[]{:S(2)}, u32[]{:S(2)}) collective-permute-start(bf16[1024,128]{1,0:T(8,128)(2,1)S(1)} %shard_map.93.refs_0_), channel_id=1, source_target_pairs={{0,1},{1,0},{2,3},{3,2},{4,5},{5,4},{6,7},{7,6},{8,9},{9,8},{10,11... | collective-permute-start | bytes 786440 | tf_op jit(solution)/shard_map/ppermute | solution.py:139
  93.2 0.0 collective-permute-done.refs_1_
  93.2 3.0 %collective-permute-start.4 = (bf16[1024,128]{1,0:T(8,128)(2,1)S(1)}, bf16[1024,128]{1,0:T(8,128)(2,1)S(1)}, u32[]{:S(2)}, u32[]{:S(2)}) collective-permute-start(bf16[1024,128]{1,0:T(8,128)(2,1)S(1)} %collective-permute-done.refs_1_), channel_id=1, source_target_pairs={{0,1},{1,0},{2,3},{3,2},{4,5},{5,4},{6,7},{7,6},{8,9},{9,8},{10,11... | collective-permute-start | bytes 786440 | tf_op jit(solution)/shard_map/ppermute | solution.py:139
  96.2 0.0 collective-permute-done.1.refs_2_
  96.2 2.5 %collective-permute-start.5 = (bf16[1024,128]{1,0:T(8,128)(2,1)S(1)}, bf16[1024,128]{1,0:T(8,128)(2,1)S(1)}, u32[]{:S(2)}, u32[]{:S(2)}) collective-permute-start(bf16[1024,128]{1,0:T(8,128)(2,1)S(1)} %collective-permute-done.1.refs_2_), channel_id=1, source_target_pairs={{0,1},{1,0},{2,3},{3,2},{4,5},{5,4},{6,7},{7,6},{8,9},{9,8},{10,11... | collective-permute-start | bytes 786440 | tf_op jit(solution)/shard_map/ppermute | solution.py:139
  98.7 0.0 collective-permute-done.2.refs_3_
  98.7 2.2 %collective-permute-start.6 = (bf16[1024,128]{1,0:T(8,128)(2,1)S(1)}, bf16[1024,128]{1,0:T(8,128)(2,1)S(1)}, u32[]{:S(2)}, u32[]{:S(2)}) collective-permute-start(bf16[1024,128]{1,0:T(8,128)(2,1)S(1)} %collective-permute-done.2.refs_3_), channel_id=1, source_target_pairs={{0,1},{1,0},{2,3},{3,2},{4,5},{5,4},{6,7},{7,6},{8,9},{9,8},{10,11... | collective-permute-start | bytes 786440 | tf_op jit(solution)/shard_map/ppermute | solution.py:139
  102.2 0.0 collective-permute-done.3.refs_4_
  102.3 0.0 collective-permute-done.4.refs_5_
  102.3 0.0 collective-permute-done.5.refs_6_
  102.3 0.0 collective-permute-done.6.refs_7_
  102.3 1.4 %shard_map.94.img = bf16[1024,1024]{1,0:T(8,128)(2,1)S(1)} custom-call(s32[1]{0:T(128)} %bitcast.me, bf16[1024,128]{1,0:T(8,128)(2,1)S(1)} %shard_map.93.refs_0_, bf16[1024,128]{1,0:T(8,128)(2,1)S(1)} %collective-permute-done.refs_1_, bf16[1024,128]{1,0:T(8,128)(2,1)S(1)} %collective-permute-done.1.refs_2_, ...), custom_call_target="tpu_custom_call" | custom-call | tf_op jit(solution)/shard_map/pallas_call | solution.py:210
  103.7 0.0 all-gather.2.cloned.1.call-done.weights
  103.7 0.0 copy-done.1
  103.7 6.0 %shard_map.95 = bf16[128,2048]{1,0:T(8,128)(2,1)} custom-call(s32[1]{0:T(128)} %bitcast.me, f32[1]{0:T(128)S(6)} %copy.15.stretch, f32[1]{0:T(128)S(6)} %copy.16.shift, s32[8,3,128]{2,1,0:T(4,128)S(1)} %all-to-all-done.info, bf16[128,2048]{1,0:T(8,128)(2,1)S(1)} %bitcast.20, bf16[1024,1024]{1,0:T(8,128)(2,1)S(1)} %shard_map.94.img, ...), custom_call_target="tpu_custom_call" | custom-call | flops 1073741824 | bytes 4194304 | tf_op jit(solution)/shard_map/pallas_call | solution.py:218
  (3 shorter events, 0.0 us)
Async XLA Ops:
  6.5 30.6 %copy-start = (bf16[256,1408]{1,0:T(8,128)(2,1)S(1)}, bf16[256,1408]{1,0:T(8,128)(2,1)}, u32[]{:S(2)}) copy-start(bf16[256,1408]{1,0:T(8,128)(2,1)} %param.10) | copy-start | bytes 2162692
  6.5 97.1 %all-gather.2.cloned.1.call-start = ((), (), s32[]{:S(2)}) async-start(), calls=%async_computation.3 | async-start | bytes 4259840 | tf_op jit(solution)/shard_map/all_gather | solution.py:158
  8.7 14.8 %all-to-all-start = ((s32[8,3,128]{2,1,0:T(4,128)}), s32[8,3,128]{2,1,0:T(4,128)S(1)}, u32[]{:S(2)}, u32[]{:S(2)}) async-start(s32[8,3,128]{2,1,0:T(4,128)} %shard_map.91), calls=%async_computation | async-start | bytes 32768 | tf_op jit(solution)/shard_map/all_to_all | solution.py:167
  25.2 27.1 %all-to-all-start.1 = ((bf16[64,24,128]{2,1,0:T(8,128)(2,1)}), bf16[64,24,128]{2,1,0:T(8,128)(2,1)S(1)}, u32[]{:S(2)}, u32[]{:S(2)}) async-start(bf16[64,24,128]{2,1,0:T(8,128)(2,1)} %maximum_maximum_fusion), calls=%async_computation.1 | async-start | bytes 786432 | tf_op jit(solution)/shard_map/all_to_all | solution.py:189
  39.8 63.9 %copy-start.1 = (bf16[2,64,2048]{2,1,0:T(8,128)(2,1)S(1)}, bf16[2,64,2048]{2,1,0:T(8,128)(2,1)}, u32[]{:S(2)}) copy-start(bf16[2,64,2048]{2,1,0:T(8,128)(2,1)} %param.9) | copy-start | bytes 1572868
  77.8 15.4 %collective-permute-start = (bf16[1024,128]{1,0:T(8,128)(2,1)S(1)}, bf16[1024,128]{1,0:T(8,128)(2,1)S(1)}, u32[]{:S(2)}, u32[]{:S(2)}) collective-permute-start(bf16[1024,128]{1,0:T(8,128)(2,1)S(1)} %shard_map.93.refs_0_), channel_id=1, source_target_pairs={{0,2},{2,4},{4,6},{6,0},{1,3},{3,5},{5,7},{7,1},{8,10},{10,12},{12... | collective-permute-start | bytes 786440 | tf_op jit(solution)/shard_map/ppermute | solution.py:142
  79.7 16.5 %collective-permute-start.1 = (bf16[1024,128]{1,0:T(8,128)(2,1)S(1)}, bf16[1024,128]{1,0:T(8,128)(2,1)S(1)}, u32[]{:S(2)}, u32[]{:S(2)}) collective-permute-start(bf16[1024,128]{1,0:T(8,128)(2,1)S(1)} %shard_map.93.refs_0_), channel_id=1, source_target_pairs={{0,6},{2,0},{4,2},{6,4},{1,7},{3,1},{5,3},{7,5},{8,14},{10,8},{12,... | collective-permute-start | bytes 786440 | tf_op jit(solution)/shard_map/ppermute | solution.py:142
  84.3 14.4 %collective-permute-start.2 = (bf16[1024,128]{1,0:T(8,128)(2,1)S(1)}, bf16[1024,128]{1,0:T(8,128)(2,1)S(1)}, u32[]{:S(2)}, u32[]{:S(2)}) collective-permute-start(bf16[1024,128]{1,0:T(8,128)(2,1)S(1)} %shard_map.93.refs_0_), channel_id=1, source_target_pairs={{0,4},{2,6},{4,0},{6,2},{1,5},{3,7},{5,1},{7,3},{8,12},{10,14},{12... | collective-permute-start | bytes 786440 | tf_op jit(solution)/shard_map/ppermute | solution.py:142
  86.5 15.7 %collective-permute-start.3 = (bf16[1024,128]{1,0:T(8,128)(2,1)S(1)}, bf16[1024,128]{1,0:T(8,128)(2,1)S(1)}, u32[]{:S(2)}, u32[]{:S(2)}) collective-permute-start(bf16[1024,128]{1,0:T(8,128)(2,1)S(1)} %shard_map.93.refs_0_), channel_id=1, source_target_pairs={{0,1},{1,0},{2,3},{3,2},{4,5},{5,4},{6,7},{7,6},{8,9},{9,8},{10,11... | collective-permute-start | bytes 786440 | tf_op jit(solution)/shard_map/ppermute | solution.py:139
  93.2 9.0 %collective-permute-start.4 = (bf16[1024,128]{1,0:T(8,128)(2,1)S(1)}, bf16[1024,128]{1,0:T(8,128)(2,1)S(1)}, u32[]{:S(2)}, u32[]{:S(2)}) collective-permute-start(bf16[1024,128]{1,0:T(8,128)(2,1)S(1)} %collective-permute-done.refs_1_), channel_id=1, source_target_pairs={{0,1},{1,0},{2,3},{3,2},{4,5},{5,4},{6,7},{7,6},{8,9},{9,8},{10,11... | collective-permute-start | bytes 786440 | tf_op jit(solution)/shard_map/ppermute | solution.py:139
  96.2 6.0 %collective-permute-start.5 = (bf16[1024,128]{1,0:T(8,128)(2,1)S(1)}, bf16[1024,128]{1,0:T(8,128)(2,1)S(1)}, u32[]{:S(2)}, u32[]{:S(2)}) collective-permute-start(bf16[1024,128]{1,0:T(8,128)(2,1)S(1)} %collective-permute-done.1.refs_2_), channel_id=1, source_target_pairs={{0,1},{1,0},{2,3},{3,2},{4,5},{5,4},{6,7},{7,6},{8,9},{9,8},{10,11... | collective-permute-start | bytes 786440 | tf_op jit(solution)/shard_map/ppermute | solution.py:139
  98.7 3.5 %collective-permute-start.6 = (bf16[1024,128]{1,0:T(8,128)(2,1)S(1)}, bf16[1024,128]{1,0:T(8,128)(2,1)S(1)}, u32[]{:S(2)}, u32[]{:S(2)}) collective-permute-start(bf16[1024,128]{1,0:T(8,128)(2,1)S(1)} %collective-permute-done.2.refs_3_), channel_id=1, source_target_pairs={{0,1},{1,0},{2,3},{3,2},{4,5},{5,4},{6,7},{7,6},{8,9},{9,8},{10,11... | collective-permute-start | bytes 786440 | tf_op jit(solution)/shard_map/ppermute | solution.py:139
Sparse Core Ops, SparseCore 0:
  10.4 91.8 all-gather.1

commit v9 on v8

--- a/solution.py
+++ b/solution.py
@@ -112,7 +112,7 @@
     gain, offset = stretch[0], shift[0]
     pairs = text.shape[0]
     same_micro = (iota((pairs, pairs), 0) >= rows) == (iota((pairs, pairs), 1) >= rows)
-    own_labels = info[me[0], 2:3, :]
+    own_labels = as_column(info[me[0], 2:3, :])
     raw = jnp.zeros((pairs, wt.shape[1]), F32)
     for copy, span in zip(copies, spans):
         copy.wait()
@@ -120,13 +120,13 @@
     inverse = lax.rsqrt(jnp.sum(raw * raw, axis=1, keepdims=True) + EPS)
     unit = raw * inverse
     unit_bf = unit.astype(BF)
+    similar = dot(unit_bf, img[...], 1, 1)
     for g in range(img.shape[0] // pairs):
         span = slice(g * pairs, (g + 1) * pairs)
-        match = (as_column(info[g, 2:3, :]) == own_labels).astype(F32)
-        logit = gain * dot(img[span, :], unit_bf, 1, 1) + offset
-        slope = LOSS_SCALE * (jax.nn.sigmoid(logit) - match)
-        slopes[span, :] = jnp.where(same_micro, slope, 0.0).astype(BF)
-    grad = gain * dot(slopes[...], img[...], 0, 0)
+        match = (own_labels == info[g, 2:3, :]).astype(F32)
+        slope = LOSS_SCALE * (jax.nn.sigmoid(gain * similar[:, span] + offset) - match)
+        slopes[:, span] = jnp.where(same_micro, slope, 0.0).astype(BF)
+    grad = gain * dot(slopes[...], img[...], 1, 0)
     grad = grad - unit * jnp.sum(unit * grad, axis=1, keepdims=True)
     grad = (inverse * grad).astype(BF)
     out[...] = dot(grad, wt[...], 1, 1).astype(BF)
@@ -222,7 +222,7 @@
             out_specs=VMEM,
             scratch_shapes=[
                 pltpu.VMEM((d_txt, emb), BF),
-                pltpu.VMEM((images, pairs), BF),
+                pltpu.VMEM((pairs, images), BF),
                 pltpu.SemaphoreType.DMA((4,)),
             ],
             compiler_params=LAST,

time: 119 us -> 119 us (level)
  no operation moved by 1% of the time
where the time goes in v9:
time: 119 us; the launch traced here: 117 us
  starting transfers between devices  45.2 us (38%)
  blocking collectives  23.1 us (19%)
  waiting for transfers between devices  17.1 us (14%)
  between operations  14.9 us (13%)
  Pallas kernels  10.8 us (9%)
  matrix products  3.55 us (3%)
    all_to_all x1, blocking collectives, local(): lax.all_to_all(served, ('z', 'y'), split_axis=0, concat_axis=0, tiled=True)  23.1 us
    ppermute x4, starting transfers between devices, swap(): return lax.ppermute(v, 'core', [(i, nc - 1 - i) for i in range(nc)])  14.4 us
    all_to_all x1, waiting for transfers between devices, local(): lax.all_to_all(sent, ('z', 'y'), split_axis=0, concat_axis=0, tiled=True)  12.4 us
    all_to_all x1, starting transfers between devices, local(): lax.all_to_all(sent, ('z', 'y'), split_axis=0, concat_axis=0, tiled=True)  12 us
    all_to_all x1, starting transfers between devices, local(): lax.all_to_all(info, ('x', 'core'), split_axis=0, concat_axis=0, tiled=True)  10.1 us
    ppermute x3, starting transfers between devices, shift(): return lax.ppermute(v, 'x', [(i, (i + by) % nx) for i in range(nx)])  8.69 us
    pallas_call x1, Pallas kernels, local(): pl.pallas_call(functools.partial(grad_kernel, rows), out_shape=jax.ShapeD...  6.02 us
    all_to_all x1, waiting for transfers between devices, local(): lax.all_to_all(info, ('x', 'core'), split_axis=0, concat_axis=0, tiled=True)  3.9 us
  transfers between devices with their start and end apart: 10, of which 2 were waited for; matrix products, arithmetic and copies ran while one was open for 5% of the time, Pallas kernels for 4%

profile of v9, /device:TPU:1, one launch (start us, length us, event | category | flops | bytes accessed | tf_op | source)
XLA Modules:
  0.0 116.6 jit_solution(14893112523042405690)
XLA Ops:
  6.5 0.0 copy-start
  6.5 0.0 all-gather.2.cloned.1.call-start
  6.5 0.7 all-gather.2.cloned.1.call-update
  7.3 1.4 %shard_map.91 = s32[8,3,128]{2,1,0:T(4,128)} custom-call(s32[2,1,64]{2,1,0:T(1,128)} %bitcast.24, s32[2,64]{1,0:T(2,128)} %entry.1, s32[2,64]{1,0:T(2,128)} %labels.1), custom_call_target="tpu_custom_call" | custom-call | tf_op jit(solution)/shard_map/pallas_call | solution.py:160
  8.7 10.1 %all-to-all-start = ((s32[8,3,128]{2,1,0:T(4,128)}), s32[8,3,128]{2,1,0:T(4,128)S(1)}, u32[]{:S(2)}, u32[]{:S(2)}) async-start(s32[8,3,128]{2,1,0:T(4,128)} %shard_map.91), calls=%async_computation | async-start | bytes 32768 | tf_op jit(solution)/shard_map/all_to_all | solution.py:167
  18.8 0.7 constant_dynamic-slice_fusion
  19.5 0.1 pad.2.clone
  19.5 3.9 %all-to-all-done.info = s32[8,3,128]{2,1,0:T(4,128)S(1)} async-done(((s32[8,3,128]{2,1,0:T(4,128)}), s32[8,3,128]{2,1,0:T(4,128)S(1)}, u32[]{:S(2)}, u32[]{:S(2)}) %all-to-all-start) | async-done | bytes 12320 | tf_op jit(solution)/shard_map/all_to_all | solution.py:167
  23.4 0.7 shard_map.92
  24.1 0.1 copy.14
  24.2 0.1 broadcast_in_dim.6
  24.2 0.9 maximum_maximum_fusion
  25.2 12.0 %all-to-all-start.1 = ((bf16[64,24,128]{2,1,0:T(8,128)(2,1)}), bf16[64,24,128]{2,1,0:T(8,128)(2,1)S(1)}, u32[]{:S(2)}, u32[]{:S(2)}) async-start(bf16[64,24,128]{2,1,0:T(8,128)(2,1)} %maximum_maximum_fusion), calls=%async_computation.1 | async-start | bytes 786432 | tf_op jit(solution)/shard_map/all_to_all | solution.py:189
  37.2 0.0 copy-done
  37.2 2.6 %fusion.5.clone.6 = bf16[1536,256]{1,0:T(8,128)(2,1)S(1)} fusion(bf16[256,1408]{1,0:T(8,128)(2,1)S(1)} %copy-done, s32[1408]{0:T(1024)S(1)} %get-tuple-element.10, s32[1408]{0:T(1024)S(1)} %get-tuple-element.11, s32[1408]{0:T(1024)S(1)} %get-tuple-element.9, s32[1408]{0:T(1024)S(1)} %get-tuple-element.12, ...), kind=kOutput, calls=%fused_computation.5.clone.clone.clone.clone.clone.1 | convolution fusion | flops 1120665600 | bytes 1532672 | tf_op jit(solution)/shard_map/dot_general | solution.py:27
  39.8 0.0 copy-start.1
  39.8 12.4 %all-to-all-done.1 = bf16[64,24,128]{2,1,0:T(8,128)(2,1)S(1)} async-done(((bf16[64,24,128]{2,1,0:T(8,128)(2,1)}), bf16[64,24,128]{2,1,0:T(8,128)(2,1)S(1)}, u32[]{:S(2)}, u32[]{:S(2)}) %all-to-all-start.1) | async-done | bytes 393248 | tf_op jit(solution)/shard_map/all_to_all | solution.py:189
  52.3 0.1 fusion.15
  52.4 0.1 reshape.33
  52.5 0.4 fusion.11
  52.9 0.5 convolution_convert_fusion
  53.4 23.1 %all_to_all.15 = bf16[64,32,128]{2,1,0:T(8,128)(2,1)S(1)} all-to-all(bf16[64,32,128]{2,1,0:T(8,128)(2,1)S(1)} %bitcast.23), channel_id=1, replica_groups=mesh['z'=8,'y'=8,'x'=4,'core'=2] {'z','y'}, dimensions={0} | all-to-all | bytes 1048576 | tf_op jit(solution)/shard_map/all_to_all | solution.py:199
  76.5 1.3 %shard_map.93.refs_0_ = bf16[1024,128]{1,0:T(8,128)(2,1)S(1)} custom-call(s32[8,128]{1,0:T(8,128)S(1)} %get-tuple-element.7.slot, bf16[2048,128]{1,0:T(8,128)(2,1)S(1)} %bitcast.19), custom_call_target="tpu_custom_call" | custom-call | tf_op jit(solution)/shard_map/pallas_call | solution.py:200
  77.8 1.9 %collective-permute-start = (bf16[1024,128]{1,0:T(8,128)(2,1)S(1)}, bf16[1024,128]{1,0:T(8,128)(2,1)S(1)}, u32[]{:S(2)}, u32[]{:S(2)}) collective-permute-start(bf16[1024,128]{1,0:T(8,128)(2,1)S(1)} %shard_map.93.refs_0_), channel_id=1, source_target_pairs={{0,2},{2,4},{4,6},{6,0},{1,3},{3,5},{5,7},{7,1},{8,10},{10,12},{12... | collective-permute-start | bytes 786440 | tf_op jit(solution)/shard_map/ppermute | solution.py:142
  79.7 4.6 %collective-permute-start.1 = (bf16[1024,128]{1,0:T(8,128)(2,1)S(1)}, bf16[1024,128]{1,0:T(8,128)(2,1)S(1)}, u32[]{:S(2)}, u32[]{:S(2)}) collective-permute-start(bf16[1024,128]{1,0:T(8,128)(2,1)S(1)} %shard_map.93.refs_0_), channel_id=1, source_target_pairs={{0,6},{2,0},{4,2},{6,4},{1,7},{3,1},{5,3},{7,5},{8,14},{10,8},{12,... | collective-permute-start | bytes 786440 | tf_op jit(solution)/shard_map/ppermute | solution.py:142
  84.3 2.2 %collective-permute-start.2 = (bf16[1024,128]{1,0:T(8,128)(2,1)S(1)}, bf16[1024,128]{1,0:T(8,128)(2,1)S(1)}, u32[]{:S(2)}, u32[]{:S(2)}) collective-permute-start(bf16[1024,128]{1,0:T(8,128)(2,1)S(1)} %shard_map.93.refs_0_), channel_id=1, source_target_pairs={{0,4},{2,6},{4,0},{6,2},{1,5},{3,7},{5,1},{7,3},{8,12},{10,14},{12... | collective-permute-start | bytes 786440 | tf_op jit(solution)/shard_map/ppermute | solution.py:142
  86.5 6.7 %collective-permute-start.3 = (bf16[1024,128]{1,0:T(8,128)(2,1)S(1)}, bf16[1024,128]{1,0:T(8,128)(2,1)S(1)}, u32[]{:S(2)}, u32[]{:S(2)}) collective-permute-start(bf16[1024,128]{1,0:T(8,128)(2,1)S(1)} %shard_map.93.refs_0_), channel_id=1, source_target_pairs={{0,1},{1,0},{2,3},{3,2},{4,5},{5,4},{6,7},{7,6},{8,9},{9,8},{10,11... | collective-permute-start | bytes 786440 | tf_op jit(solution)/shard_map/ppermute | solution.py:139
  93.2 0.0 collective-permute-done.refs_1_
  93.2 3.0 %collective-permute-start.4 = (bf16[1024,128]{1,0:T(8,128)(2,1)S(1)}, bf16[1024,128]{1,0:T(8,128)(2,1)S(1)}, u32[]{:S(2)}, u32[]{:S(2)}) collective-permute-start(bf16[1024,128]{1,0:T(8,128)(2,1)S(1)} %collective-permute-done.refs_1_), channel_id=1, source_target_pairs={{0,1},{1,0},{2,3},{3,2},{4,5},{5,4},{6,7},{7,6},{8,9},{9,8},{10,11... | collective-permute-start | bytes 786440 | tf_op jit(solution)/shard_map/ppermute | solution.py:139
  96.2 0.0 collective-permute-done.1.refs_2_
  96.2 2.5 %collective-permute-start.5 = (bf16[1024,128]{1,0:T(8,128)(2,1)S(1)}, bf16[1024,128]{1,0:T(8,128)(2,1)S(1)}, u32[]{:S(2)}, u32[]{:S(2)}) collective-permute-start(bf16[1024,128]{1,0:T(8,128)(2,1)S(1)} %collective-permute-done.1.refs_2_), channel_id=1, source_target_pairs={{0,1},{1,0},{2,3},{3,2},{4,5},{5,4},{6,7},{7,6},{8,9},{9,8},{10,11... | collective-permute-start | bytes 786440 | tf_op jit(solution)/shard_map/ppermute | solution.py:139
  98.7 0.0 collective-permute-done.2.refs_3_
  98.7 2.2 %collective-permute-start.6 = (bf16[1024,128]{1,0:T(8,128)(2,1)S(1)}, bf16[1024,128]{1,0:T(8,128)(2,1)S(1)}, u32[]{:S(2)}, u32[]{:S(2)}) collective-permute-start(bf16[1024,128]{1,0:T(8,128)(2,1)S(1)} %collective-permute-done.2.refs_3_), channel_id=1, source_target_pairs={{0,1},{1,0},{2,3},{3,2},{4,5},{5,4},{6,7},{7,6},{8,9},{9,8},{10,11... | collective-permute-start | bytes 786440 | tf_op jit(solution)/shard_map/ppermute | solution.py:139
  102.2 0.0 collective-permute-done.3.refs_4_
  102.3 0.0 collective-permute-done.4.refs_5_
  102.3 0.0 collective-permute-done.5.refs_6_
  102.3 0.0 collective-permute-done.6.refs_7_
  102.3 1.4 %shard_map.94.img = bf16[1024,1024]{1,0:T(8,128)(2,1)S(1)} custom-call(s32[1]{0:T(128)} %bitcast.me, bf16[1024,128]{1,0:T(8,128)(2,1)S(1)} %shard_map.93.refs_0_, bf16[1024,128]{1,0:T(8,128)(2,1)S(1)} %collective-permute-done.refs_1_, bf16[1024,128]{1,0:T(8,128)(2,1)S(1)} %collective-permute-done.1.refs_2_, ...), custom_call_target="tpu_custom_call" | custom-call | tf_op jit(solution)/shard_map/pallas_call | solution.py:210
  103.7 0.0 all-gather.2.cloned.1.call-done.weights
  103.7 0.0 copy-done.1
  103.7 6.0 %shard_map.95 = bf16[128,2048]{1,0:T(8,128)(2,1)} custom-call(s32[1]{0:T(128)} %bitcast.me, f32[1]{0:T(128)S(6)} %copy.15.stretch, f32[1]{0:T(128)S(6)} %copy.16.shift, s32[8,3,128]{2,1,0:T(4,128)S(1)} %all-to-all-done.info, bf16[128,2048]{1,0:T(8,128)(2,1)S(1)} %bitcast.20, bf16[1024,1024]{1,0:T(8,128)(2,1)S(1)} %shard_map.94.img, ...), custom_call_target="tpu_custom_call" | custom-call | flops 1073741824 | bytes 4194304 | tf_op jit(solution)/shard_map/pallas_call | solution.py:218
  (3 shorter events, 0.0 us)
Async XLA Ops:
  6.5 30.6 %copy-start = (bf16[256,1408]{1,0:T(8,128)(2,1)S(1)}, bf16[256,1408]{1,0:T(8,128)(2,1)}, u32[]{:S(2)}) copy-start(bf16[256,1408]{1,0:T(8,128)(2,1)} %param.10) | copy-start | bytes 2162692
  6.5 97.1 %all-gather.2.cloned.1.call-start = ((), (), s32[]{:S(2)}) async-start(), calls=%async_computation.3 | async-start | bytes 4259840 | tf_op jit(solution)/shard_map/all_gather | solution.py:158
  8.7 14.8 %all-to-all-start = ((s32[8,3,128]{2,1,0:T(4,128)}), s32[8,3,128]{2,1,0:T(4,128)S(1)}, u32[]{:S(2)}, u32[]{:S(2)}) async-start(s32[8,3,128]{2,1,0:T(4,128)} %shard_map.91), calls=%async_computation | async-start | bytes 32768 | tf_op jit(solution)/shard_map/all_to_all | solution.py:167
  25.2 27.1 %all-to-all-start.1 = ((bf16[64,24,128]{2,1,0:T(8,128)(2,1)}), bf16[64,24,128]{2,1,0:T(8,128)(2,1)S(1)}, u32[]{:S(2)}, u32[]{:S(2)}) async-start(bf16[64,24,128]{2,1,0:T(8,128)(2,1)} %maximum_maximum_fusion), calls=%async_computation.1 | async-start | bytes 786432 | tf_op jit(solution)/shard_map/all_to_all | solution.py:189
  39.8 63.9 %copy-start.1 = (bf16[2,64,2048]{2,1,0:T(8,128)(2,1)S(1)}, bf16[2,64,2048]{2,1,0:T(8,128)(2,1)}, u32[]{:S(2)}) copy-start(bf16[2,64,2048]{2,1,0:T(8,128)(2,1)} %param.9) | copy-start | bytes 1572868
  77.8 15.4 %collective-permute-start = (bf16[1024,128]{1,0:T(8,128)(2,1)S(1)}, bf16[1024,128]{1,0:T(8,128)(2,1)S(1)}, u32[]{:S(2)}, u32[]{:S(2)}) collective-permute-start(bf16[1024,128]{1,0:T(8,128)(2,1)S(1)} %shard_map.93.refs_0_), channel_id=1, source_target_pairs={{0,2},{2,4},{4,6},{6,0},{1,3},{3,5},{5,7},{7,1},{8,10},{10,12},{12... | collective-permute-start | bytes 786440 | tf_op jit(solution)/shard_map/ppermute | solution.py:142
  79.7 16.5 %collective-permute-start.1 = (bf16[1024,128]{1,0:T(8,128)(2,1)S(1)}, bf16[1024,128]{1,0:T(8,128)(2,1)S(1)}, u32[]{:S(2)}, u32[]{:S(2)}) collective-permute-start(bf16[1024,128]{1,0:T(8,128)(2,1)S(1)} %shard_map.93.refs_0_), channel_id=1, source_target_pairs={{0,6},{2,0},{4,2},{6,4},{1,7},{3,1},{5,3},{7,5},{8,14},{10,8},{12,... | collective-permute-start | bytes 786440 | tf_op jit(solution)/shard_map/ppermute | solution.py:142
  84.3 14.4 %collective-permute-start.2 = (bf16[1024,128]{1,0:T(8,128)(2,1)S(1)}, bf16[1024,128]{1,0:T(8,128)(2,1)S(1)}, u32[]{:S(2)}, u32[]{:S(2)}) collective-permute-start(bf16[1024,128]{1,0:T(8,128)(2,1)S(1)} %shard_map.93.refs_0_), channel_id=1, source_target_pairs={{0,4},{2,6},{4,0},{6,2},{1,5},{3,7},{5,1},{7,3},{8,12},{10,14},{12... | collective-permute-start | bytes 786440 | tf_op jit(solution)/shard_map/ppermute | solution.py:142
  86.5 15.7 %collective-permute-start.3 = (bf16[1024,128]{1,0:T(8,128)(2,1)S(1)}, bf16[1024,128]{1,0:T(8,128)(2,1)S(1)}, u32[]{:S(2)}, u32[]{:S(2)}) collective-permute-start(bf16[1024,128]{1,0:T(8,128)(2,1)S(1)} %shard_map.93.refs_0_), channel_id=1, source_target_pairs={{0,1},{1,0},{2,3},{3,2},{4,5},{5,4},{6,7},{7,6},{8,9},{9,8},{10,11... | collective-permute-start | bytes 786440 | tf_op jit(solution)/shard_map/ppermute | solution.py:139
  93.2 9.0 %collective-permute-start.4 = (bf16[1024,128]{1,0:T(8,128)(2,1)S(1)}, bf16[1024,128]{1,0:T(8,128)(2,1)S(1)}, u32[]{:S(2)}, u32[]{:S(2)}) collective-permute-start(bf16[1024,128]{1,0:T(8,128)(2,1)S(1)} %collective-permute-done.refs_1_), channel_id=1, source_target_pairs={{0,1},{1,0},{2,3},{3,2},{4,5},{5,4},{6,7},{7,6},{8,9},{9,8},{10,11... | collective-permute-start | bytes 786440 | tf_op jit(solution)/shard_map/ppermute | solution.py:139
  96.2 6.0 %collective-permute-start.5 = (bf16[1024,128]{1,0:T(8,128)(2,1)S(1)}, bf16[1024,128]{1,0:T(8,128)(2,1)S(1)}, u32[]{:S(2)}, u32[]{:S(2)}) collective-permute-start(bf16[1024,128]{1,0:T(8,128)(2,1)S(1)} %collective-permute-done.1.refs_2_), channel_id=1, source_target_pairs={{0,1},{1,0},{2,3},{3,2},{4,5},{5,4},{6,7},{7,6},{8,9},{9,8},{10,11... | collective-permute-start | bytes 786440 | tf_op jit(solution)/shard_map/ppermute | solution.py:139
  98.7 3.5 %collective-permute-start.6 = (bf16[1024,128]{1,0:T(8,128)(2,1)S(1)}, bf16[1024,128]{1,0:T(8,128)(2,1)S(1)}, u32[]{:S(2)}, u32[]{:S(2)}) collective-permute-start(bf16[1024,128]{1,0:T(8,128)(2,1)S(1)} %collective-permute-done.2.refs_3_), channel_id=1, source_target_pairs={{0,1},{1,0},{2,3},{3,2},{4,5},{5,4},{6,7},{7,6},{8,9},{9,8},{10,11... | collective-permute-start | bytes 786440 | tf_op jit(solution)/shard_map/ppermute | solution.py:139
Sparse Core Ops, SparseCore 0:
  10.4 91.8 all-gather.1
